TPU v7x, 128 devices: a whole 4x4x4 slice. The times are simulated.
128 devices in a mesh: ctx: 64 (over y_lo, z, x, core), ch: 2 (over y_hi).
Axes of the slice: x: 4, y: 4 (y_hi: 2, y_lo: 2; y = y_hi * 2 + y_lo), z: 4, core: 2. Of those that a mesh axis runs over, the one named last changes fastest.
Arguments:
- features: bfloat16 [3, 8192, 4096], P(None, 'ctx', 'ch'), may hold values from -6 to 6
- short_weight: float32 [3, 3, 4096], P(None, None, 'ch'), may hold values from -3 to 3
- skip: float32 [4096], P('ch'), may hold values from 0.5 to 1.5
- long_filter: float32 [8192, 256], P('ctx'), may hold values from -2 to 2
- cotangent: bfloat16 [8192, 4096], P('ctx', 'ch'), may hold values from -6 to 6
Outputs:
- mixed: bfloat16 [8192, 4096], P('ctx', 'ch')
- feature_gradient: float32 [3, 8192, 4096], P(None, 'ctx', 'ch')
- grad_short: float32 [3, 3, 4096], P(None, None, 'ch')
- grad_skip: float32 [4096], P('ch')
- grad_filter: float32 [8192, 256], P('ctx', 'ch')
All inputs are finite; a program needn't handle non-finite values.
Results may differ from a plain program's by a relative error of at most 0.00105.
Values may be sent and summed in bfloat16 or wider, within the bound.
No kernel may reach another device: no remote copies, remote signals or barrier semaphores. Data moves between devices by JAX's collectives and lax.ppermute only.
A program may use at most 128 MiB of HBM per device.

v0:
```python
import math

import jax
import jax.numpy as jnp
from jax import lax
from jax.sharding import PartitionSpec as P

full_turn = 2.0 * math.pi
exact = lax.Precision.HIGHEST


def from_behind(block, axis, distance):
    devices = range(lax.axis_size(axis))
    route = [(i - distance, i) for i in devices if i - distance in devices]
    return lax.ppermute(block, axis, route)


def twiddle_turn(row_ids, col_ids, period):
    angle = full_turn * (row_ids[:, None] * col_ids[None, :] % period).astype(jnp.float32) / period
    return (jnp.cos(angle), jnp.sin(angle))


def regroup(values):
    return lax.all_to_all(values, "ctx", split_axis=1, concat_axis=0, tiled=True)


def to_spectrum(signal, pieces, device_rank):
    extent = signal.shape[0]
    breadth = signal.shape[1]
    portion = extent // pieces
    period = 2 * pieces * extent
    columns = regroup(signal.reshape(1, extent, breadth))
    cos_blk, sine_block = twiddle_turn(jnp.arange(pieces), jnp.arange(2 * pieces), 2 * pieces)
    real_part = jnp.einsum("pk,prc->rkc", cos_blk, columns, precision=exact)
    imag_part = -jnp.einsum("pk,prc->rkc", sine_block, columns, precision=exact)
    cos_tw, sin_tw = twiddle_turn(
        device_rank * portion + jnp.arange(portion), jnp.arange(2 * pieces), period
    )
    cos_tw = cos_tw[:, :, None]
    sin_tw = sin_tw[:, :, None]
    twisted = jnp.stack(
        [real_part * cos_tw + imag_part * sin_tw, imag_part * cos_tw - real_part * sin_tw], axis=2
    )
    rows_all = regroup(twisted)
    cosine_line, sin_row = twiddle_turn(jnp.arange(extent), jnp.arange(extent), extent)
    real_in = rows_all[:, :, 0].reshape(extent, 2 * breadth)
    imag_in = rows_all[:, :, 1].reshape(extent, 2 * breadth)
    real_out = jnp.dot(cosine_line, real_in, precision=exact) + jnp.dot(
        sin_row, imag_in, precision=exact
    )
    imag_out = jnp.dot(cosine_line, imag_in, precision=exact) - jnp.dot(
        sin_row, real_in, precision=exact
    )
    return jnp.stack(
        [real_out.reshape(extent, 2, breadth), imag_out.reshape(extent, 2, breadth)], axis=2
    )


def from_spectrum(spectrum, pieces, device_rank):
    extent = spectrum.shape[0]
    breadth = spectrum.shape[3]
    period = 2 * pieces * extent
    cosine_line, sin_row = twiddle_turn(jnp.arange(extent), jnp.arange(extent), extent)
    real_in = spectrum[:, :, 0]
    imag_in = spectrum[:, :, 1]
    real_mid = jnp.einsum("nk,kjc->jnc", cosine_line, real_in, precision=exact) - jnp.einsum(
        "nk,kjc->jnc", sin_row, imag_in, precision=exact
    )
    imag_mid = jnp.einsum("nk,kjc->jnc", cosine_line, imag_in, precision=exact) + jnp.einsum(
        "nk,kjc->jnc", sin_row, real_in, precision=exact
    )
    cos_tw, sin_tw = twiddle_turn(2 * device_rank + jnp.arange(2), jnp.arange(extent), period)
    cos_tw = cos_tw[:, :, None]
    sin_tw = sin_tw[:, :, None]
    twisted = jnp.stack(
        [real_mid * cos_tw - imag_mid * sin_tw, imag_mid * cos_tw + real_mid * sin_tw], axis=2
    )
    gathered = regroup(twisted)
    cos_blk, sine_block = twiddle_turn(jnp.arange(pieces), jnp.arange(2 * pieces), 2 * pieces)
    values = (
        jnp.einsum("nk,krc->rnc", cos_blk, gathered[:, :, 0], precision=exact)
        - jnp.einsum("nk,krc->rnc", sine_block, gathered[:, :, 1], precision=exact)
    ) / period
    return regroup(values).reshape(extent, breadth)


def complex_product(left, right, conjugate):
    sign = -1.0 if conjugate else 1.0
    real_part = left[:, :, 0] * right[:, :, 0] - sign * left[:, :, 1] * right[:, :, 1]
    imag_part = left[:, :, 1] * right[:, :, 0] + sign * left[:, :, 0] * right[:, :, 1]
    return jnp.stack([real_part, imag_part], axis=2)


def filter_product(signal_spec, filter_spec, conjugate):
    extent = signal_spec.shape[0]
    breadth = signal_spec.shape[3]
    groups = filter_spec.shape[3]
    spread = signal_spec.reshape(extent, 2, 2, breadth // groups, groups)
    result = complex_product(spread, filter_spec[:, :, :, None, :], conjugate)
    return result.reshape(extent, 2, 2, breadth)


def filter_sum(values):
    return lax.psum_scatter(values, "ch", scatter_dimension=1, tiled=True)


def shards(features, short_weight, skip, long_filter, cotangent):
    pieces = lax.axis_size("ctx")
    halves = lax.axis_size("ch")
    device_rank = lax.axis_index("ctx")
    extent = features.shape[1]
    breadth = features.shape[2]
    groups = long_filter.shape[1]
    before = from_behind(features[:, extent - 2 :, :], "ctx", 1)
    padded_in = jnp.concatenate([before, features], axis=1).astype(jnp.float32)
    shaped = (
        short_weight[:, 0, None, :] * padded_in[:, 2:, :]
        + short_weight[:, 1, None, :] * padded_in[:, 1 : extent + 1, :]
        + short_weight[:, 2, None, :] * padded_in[:, :extent, :]
    )
    query_f = shaped[0]
    key_f = shaped[1]
    value_f = shaped[2]
    mixer = key_f * value_f
    mixer_spec = to_spectrum(mixer, pieces, device_rank)
    filter_spec = to_spectrum(long_filter, pieces, device_rank)
    convolved = (
        from_spectrum(filter_product(mixer_spec, filter_spec, False), pieces, device_rank)
        + skip * mixer
    )
    mixed = (query_f * convolved).astype(jnp.bfloat16)
    upstream = cotangent.astype(jnp.float32)
    grad_query = upstream * convolved
    grad_conv = upstream * query_f
    mixer_again = to_spectrum(mixer, pieces, device_rank)
    filter_again = to_spectrum(long_filter, pieces, device_rank)
    conv_spec = to_spectrum(grad_conv, pieces, device_rank)
    grad_mixer = (
        from_spectrum(filter_product(conv_spec, filter_again, True), pieces, device_rank)
        + skip * grad_conv
    )
    cross_spec = complex_product(conv_spec, mixer_again, True)
    temporal = from_spectrum(cross_spec, pieces, device_rank)
    raw_filter = filter_sum(jnp.sum(temporal.reshape(extent, breadth // groups, groups), axis=1))
    grad_shaped = jnp.stack([grad_query, grad_mixer * value_f, grad_mixer * key_f])
    after = from_behind(grad_shaped[:, :2, :].astype(jnp.bfloat16), "ctx", -1).astype(jnp.float32)
    extended = jnp.concatenate([grad_shaped, after], axis=1)
    feature_gradient = (
        short_weight[:, 0, None, :] * extended[:, :extent, :]
        + short_weight[:, 1, None, :] * extended[:, 1 : extent + 1, :]
        + short_weight[:, 2, None, :] * extended[:, 2:, :]
    )
    tap_terms = jnp.stack(
        [
            jnp.sum(grad_shaped * padded_in[:, 2 - offset : 2 - offset + extent, :], axis=1)
            for offset in range(3)
        ],
        axis=1,
    )
    skip_term = jnp.sum(grad_conv * mixer, axis=0)
    total_taps, total_skip = lax.psum((tap_terms, skip_term), "ctx")
    seq_scale = 1.0 / math.sqrt(extent * pieces)
    grad_short = total_taps * seq_scale
    grad_skip = total_skip * seq_scale
    grad_filter = raw_filter / math.sqrt(extent * pieces * (breadth * halves // groups))
    return (mixed, feature_gradient, grad_short, grad_skip, grad_filter)


def solution(mesh):
    return jax.shard_map(
        shards,
        mesh=mesh,
        in_specs=(
            P(None, "ctx", "ch"),
            P(None, None, "ch"),
            P("ch"),
            P("ctx", None),
            P("ctx", "ch"),
        ),
        out_specs=(
            P("ctx", "ch"),
            P(None, "ctx", "ch"),
            P(None, None, "ch"),
            P("ch"),
            P("ctx", "ch"),
        ),
        check_vma=False,
    )
```

profile of v0, /device:TPU:1, one launch (start us, length us, event | category | flops | bytes accessed | tf_op | source)
XLA Modules:
  0.0 1248.3 jit_solution(10426525942353204607)
XLA Ops:
  15.1 9.2 all-to-all-start.2
  32.8 8.5 all-to-all-start.6
  47.1 11.5 all-to-all-done.6
  74.2 6.4 convolution_negate_fusion
  86.2 9.2 all-to-all-start.3
  108.1 6.7 add_bitcast_fusion.2
  117.1 7.3 copy.95
  124.4 9.5 all-to-all-start.7
  138.3 7.3 copy.75
  145.7 40.4 %all-to-all-done.7 = f32[2,128,2,2048]{3,0,2,1:T(2,128)} async-done(((f32[2,128,2,2048]{3,0,2,1:T(2,128)}), f32[2,128,2,2048]{3,0,2,1:T(2,128)}, u32[]{:S(2)}, u32[]{:S(2)}) %all-to-all-start.7) | async-done | bytes 4194336 | tf_op jit(solution)/shard_map/all_to_all | solution.py:24
  186.0 8.7 all-to-all-start.1
  224.3 13.9 %slice_reduce_fusion.1 = (f32[128,2,2048]{2,1,0:T(2,128)S(1)}, f32[128,2,2048]{2,1,0:T(2,128)S(1)}) fusion(f32[128,2,2,2048]{3,2,1,0:T(2,128)S(1)} %bitcast.311), kind=kLoop, calls=%fused_computation.55 | loop fusion | bytes 8388608 | tf_op jit(solution)/shard_map/slice | solution.py:46
  266.6 13.9 %slice_reduce_fusion.3 = (f32[128,2,2048]{2,1,0:T(2,128)S(1)}, f32[128,2,2048]{2,1,0:T(2,128)S(1)}) fusion(f32[128,2,2,2048]{3,2,1,0:T(2,128)S(1)} %bitcast.312), kind=kLoop, calls=%fused_computation.60 | loop fusion | bytes 8388608 | tf_op jit(solution)/shard_map/slice | solution.py:46
  337.0 7.3 copy.115
  344.4 9.1 all-to-all-start.10
  357.9 7.3 copy.88
  365.2 40.2 %all-to-all-done.10 = f32[2,128,2,2048]{3,0,2,1:T(2,128)} async-done(((f32[2,128,2,2048]{3,0,2,1:T(2,128)}), f32[2,128,2,2048]{3,0,2,1:T(2,128)}, u32[]{:S(2)}, u32[]{:S(2)}) %all-to-all-start.10) | async-done | bytes 4194336 | tf_op jit(solution)/shard_map/all_to_all | solution.py:24
  405.4 9.0 all-to-all-start.4
  418.9 7.3 copy.103
  426.2 40.1 %all-to-all-done.4 = f32[2,128,2,2048]{3,0,2,1:T(2,128)} async-done(((f32[2,128,2,2048]{3,0,2,1:T(2,128)}), f32[2,128,2,2048]{3,0,2,1:T(2,128)}, u32[]{:S(2)}, u32[]{:S(2)}) %all-to-all-start.4) | async-done | bytes 4194336 | tf_op jit(solution)/shard_map/all_to_all | solution.py:24
  466.3 9.4 all-to-all-start.8
  475.7 6.7 copy.90
  496.3 31.5 %all-to-all-done.8 = f32[2,128,2,2048]{3,0,2,1:T(2,128)} async-done(((f32[2,128,2,2048]{3,0,2,1:T(2,128)}), f32[2,128,2,2048]{3,0,2,1:T(2,128)}, u32[]{:S(2)}, u32[]{:S(2)}) %all-to-all-start.8) | async-done | bytes 4194336 | tf_op jit(solution)/shard_map/all_to_all | solution.py:24
  527.8 9.1 all-to-all-start.5
  536.9 6.7 copy.105
  543.7 6.1 all_to_all.186
  557.6 9.5 all-to-all-start.9
  567.2 6.7 copy.117
  573.9 6.1 all_to_all.193
  601.7 9.1 all-to-all-start.11
  610.9 149.2 %psum.15 = f32[2048]{0:T(1024)S(1)} all-reduce(f32[2048]{0:T(1024)S(1)} %get-tuple-element.50), channel_id=1, replica_groups=mesh['ctx'=64,'ch'=2] {'ctx'}, use_global_device_ids=true, to_apply=%region_5.6 | all-reduce | flops 2048 | bytes 16384 | tf_op jit(solution)/shard_map/psum | solution.py:161
  770.4 466.8 %all-reduce.2.cloned.1.call-done = f32[3,3,2048]{2,0,1:T(4,128)} async-done(((f32[3,3,2048]{2,0,1:T(4,128)}), f32[3,3,2048]{2,0,1:T(4,128)}) %all-reduce.2.cloned.1.call-update) | async-done | bytes 73744 | tf_op jit(solution)/shard_map/psum | solution.py:161
  (163 shorter events, 241.7 us)
Async XLA Ops:
  8.9 16.5 %collective-permute-start = (bf16[3,2,2048]{2,1,0:T(2,128)(2,1)S(1)}, bf16[3,2,2048]{2,1,0:T(2,128)(2,1)}, u32[]{:S(2)}, u32[]{:S(2)}) collective-permute-start(bf16[3,2,2048]{2,1,0:T(2,128)(2,1)S(1)} %slice.111), channel_id=1, source_target_pairs={{0,2},{2,4},{4,6},{6,8},{8,10},{10,12},{12,14},{14,16},{16,18},{18... | collective-permute-start | bytes 73736 | tf_op jit(solution)/shard_map/ppermute | solution.py:15
  15.1 17.7 %all-to-all-start.2 = ((f32[1,128,256]{2,0,1:T(1,128)}), f32[1,128,256]{2,0,1:T(1,128)S(1)}, u32[]{:S(2)}, u32[]{:S(2)}) async-start(f32[1,128,256]{2,0,1:T(1,128)} %reshape.161), calls=%async_computation.2 | async-start | bytes 262144 | tf_op jit(solution)/shard_map/all_to_all | solution.py:24
  25.4 1.9 copy-start.19
  27.4 2.6 copy-start.18
  32.8 25.9 %all-to-all-start.6 = ((f32[1,128,2048]{2,0,1:T(1,128)}), f32[1,128,2048]{2,0,1:T(1,128)}, u32[]{:S(2)}, u32[]{:S(2)}) async-start(f32[1,128,2048]{2,0,1:T(1,128)} %copy.92), calls=%async_computation.6 | async-start | bytes 2097152 | tf_op jit(solution)/shard_map/all_to_all | solution.py:24
  58.7 27.5 %all-to-all-start = ((f32[1,128,2048]{2,0,1:T(1,128)}), f32[1,128,2048]{2,0,1:T(1,128)}, u32[]{:S(2)}, u32[]{:S(2)}) async-start(f32[1,128,2048]{2,0,1:T(1,128)} %copy.72), calls=%async_computation | async-start | bytes 2097152 | tf_op jit(solution)/shard_map/all_to_all | solution.py:24
  74.2 6.4 copy-start.12
  86.2 38.3 %all-to-all-start.3 = ((f32[2,128,2,256]{3,0,2,1:T(2,128)}), f32[2,128,2,256]{3,0,2,1:T(2,128)}, u32[]{:S(2)}, u32[]{:S(2)}) async-start(f32[2,128,2,256]{3,0,2,1:T(2,128)} %copy.80), calls=%async_computation.3 | async-start | bytes 1048576 | tf_op jit(solution)/shard_map/all_to_all | solution.py:24
  102.9 5.2 copy-start.11
  102.9 5.2 copy-start.13
  124.4 61.6 %all-to-all-start.7 = ((f32[2,128,2,2048]{3,0,2,1:T(2,128)}), f32[2,128,2,2048]{3,0,2,1:T(2,128)}, u32[]{:S(2)}, u32[]{:S(2)}) async-start(f32[2,128,2,2048]{3,0,2,1:T(2,128)} %copy.95), calls=%async_computation.7 | async-start | bytes 8388608 | tf_op jit(solution)/shard_map/all_to_all | solution.py:24
  186.0 74.6 %all-to-all-start.1 = ((f32[2,128,2,2048]{3,0,2,1:T(2,128)}), f32[2,128,2,2048]{3,0,2,1:T(2,128)}, u32[]{:S(2)}, u32[]{:S(2)}) async-start(f32[2,128,2,2048]{3,0,2,1:T(2,128)} %copy.75), calls=%async_computation.1 | async-start | bytes 8388608 | tf_op jit(solution)/shard_map/all_to_all | solution.py:24
  239.8 1.7 copy-start.1
  241.5 2.2 copy-start.3
  250.3 3.9 copy-start.2
  344.4 61.0 %all-to-all-start.10 = ((f32[2,128,2,2048]{3,0,2,1:T(2,128)}), f32[2,128,2,2048]{3,0,2,1:T(2,128)}, u32[]{:S(2)}, u32[]{:S(2)}) async-start(f32[2,128,2,2048]{3,0,2,1:T(2,128)} %copy.115), calls=%async_computation.10 | async-start | bytes 8388608 | tf_op jit(solution)/shard_map/all_to_all | solution.py:24
  405.4 60.9 %all-to-all-start.4 = ((f32[2,128,2,2048]{3,0,2,1:T(2,128)}), f32[2,128,2,2048]{3,0,2,1:T(2,128)}, u32[]{:S(2)}, u32[]{:S(2)}) async-start(f32[2,128,2,2048]{3,0,2,1:T(2,128)} %copy.88), calls=%async_computation.4 | async-start | bytes 8388608 | tf_op jit(solution)/shard_map/all_to_all | solution.py:24
  466.3 61.5 %all-to-all-start.8 = ((f32[2,128,2,2048]{3,0,2,1:T(2,128)}), f32[2,128,2,2048]{3,0,2,1:T(2,128)}, u32[]{:S(2)}, u32[]{:S(2)}) async-start(f32[2,128,2,2048]{3,0,2,1:T(2,128)} %copy.103), calls=%async_computation.8 | async-start | bytes 8388608 | tf_op jit(solution)/shard_map/all_to_all | solution.py:24
  527.8 29.8 %all-to-all-start.5 = ((f32[2,64,2048]{2,0,1:T(2,128)}), f32[2,64,2048]{2,0,1:T(2,128)}, u32[]{:S(2)}, u32[]{:S(2)}) async-start(f32[2,64,2048]{2,0,1:T(2,128)} %copy.91), calls=%async_computation.5 | async-start | bytes 2097152 | tf_op jit(solution)/shard_map/all_to_all | solution.py:24
  557.6 29.3 %all-to-all-start.9 = ((f32[2,64,2048]{2,0,1:T(2,128)}), f32[2,64,2048]{2,0,1:T(2,128)}, u32[]{:S(2)}, u32[]{:S(2)}) async-start(f32[2,64,2048]{2,0,1:T(2,128)} %copy.106), calls=%async_computation.9 | async-start | bytes 2097152 | tf_op jit(solution)/shard_map/all_to_all | solution.py:24
  584.0 5.9 copy-start.21
  589.9 8.5 copy-start.14
  594.3 1.7 copy-start.9
  594.3 4.1 copy-start.4
  596.0 164.0 %collective-permute-start.1 = (bf16[3,2,2048]{2,1,0:T(2,128)(2,1)S(1)}, bf16[3,2,2048]{2,1,0:T(2,128)(2,1)S(1)}, u32[]{:S(2)}, u32[]{:S(2)}) collective-permute-start(bf16[3,2,2048]{2,1,0:T(2,128)(2,1)S(1)} %slice.228), channel_id=1, source_target_pairs={{2,0},{4,2},{6,4},{8,6},{10,8},{12,10},{14,12},{16,14},{18,16},{20... | collective-permute-start | bytes 73736 | tf_op jit(solution)/shard_map/ppermute | solution.py:15
  601.7 165.7 %all-to-all-start.11 = ((f32[2,64,2048]{2,0,1:T(2,128)}), f32[2,64,2048]{2,0,1:T(2,128)}, u32[]{:S(2)}, u32[]{:S(2)}) async-start(f32[2,64,2048]{2,0,1:T(2,128)} %copy.118), calls=%async_computation.11 | async-start | bytes 2097152 | tf_op jit(solution)/shard_map/all_to_all | solution.py:24
  610.8 626.5 %all-reduce.2.cloned.1.call-start = ((), (), s32[]{:S(2)}) async-start(), calls=%async_computation.13 | async-start | bytes 196608 | tf_op jit(solution)/shard_map/psum | solution.py:161
  760.1 2.3 copy-start.6
  760.1 2.5 copy-start.8
  760.1 2.8 copy-start.10
  760.1 2.8 copy-start.20
  766.8 472.1 %reduce-scatter.2.cloned.1.call-start = ((), (), s32[]{:S(2)}) async-start(), calls=%async_computation.14 | async-start | bytes 196608 | tf_op jit(solution)/shard_map/reduce_scatter | solution.py:104
  (6 other events, 6.9 us)
Sparse Core Ops, SparseCore 0:
  766.9 470.3 all-reduce.1
Sparse Core Ops, SparseCore 1:
  770.5 10.1 reduce-scatter.1
where the time goes:
time: 1260 us; the launch traced here: 1250 us
  waiting for transfers between devices  631 us (50%)
  local copies, waits for them, and re-layouts  182 us (14%)
  blocking collectives  149 us (12%)
  starting transfers between devices  113 us (9%)
  matrix products  102 us (8%)
  other arithmetic  54.2 us (4%)
  between operations  16.7 us (1%)
    psum x1, waiting for transfers between devices, shards(): total_taps, total_skip = lax.psum((tap_terms, skip_term), 'ctx')  467 us
    all_to_all x12, waiting for transfers between devices, regroup(): lax.all_to_all(values, 'ctx', split_axis=1, concat_axis=0, tiled=True)  164 us
    psum x1, blocking collectives, shards(): total_taps, total_skip = lax.psum((tap_terms, skip_term), 'ctx')  149 us
    all_to_all x12, starting transfers between devices, regroup(): lax.all_to_all(values, 'ctx', split_axis=1, concat_axis=0, tiled=True)  106 us
    all_to_all x12, local copies, waits for them, and re-layouts, regroup(): lax.all_to_all(values, 'ctx', split_axis=1, concat_axis=0, tiled=True)  58.4 us
    slice x3, local copies, waits for them, and re-layouts, to_spectrum(): real_in = rows_all[:, :, 0].reshape(extent, 2 * breadth)  29.4 us
  transfers between devices with their start and end apart: 16, of which 7 were waited for; matrix products, arithmetic and copies ran while one was open for 17% of the time, Pallas kernels for 0%

commit v1 on v0

v1 whole, which is shorter than its diff:
```python
import functools
import math

import jax
import jax.numpy as jnp
import ml_dtypes
import numpy as np
from jax import lax
from jax.experimental import pallas as pl
from jax.experimental.pallas import tpu as pltpu
from jax.sharding import PartitionSpec as P

f32 = jnp.float32
bf16 = jnp.bfloat16

BLOCKS = 64
ROWS = 128
COPIES = 8
GROUPS = 256
OWN = GROUPS // BLOCKS
LINES = 72
PERIOD = 2 * BLOCKS * ROWS
SEND_ROWS = OWN * 4 * COPIES + 16
BACK_ROWS = OWN * 2 * COPIES + 16
LEVELS = 32000.0
BIAS = 124.0


def high_low(values):
    high = values.astype(ml_dtypes.bfloat16)
    low = (values - high.astype(np.float64)).astype(ml_dtypes.bfloat16)
    return high, low


def tables():
    k1 = np.arange(65)
    a = np.arange(BLOCKS)
    b = np.arange(ROWS)
    turn = 2.0 * np.pi * (k1[:, None] * a[None, :] % ROWS) / ROWS
    first = np.zeros((2 * LINES, BLOCKS))
    first[:65] = np.cos(turn)
    first[LINES : LINES + 65] = -np.sin(turn)
    weight = np.where((k1 == 0) | (k1 == 64), 1.0, 2.0)[:, None] / PERIOD
    last = np.zeros((BLOCKS, 2 * LINES))
    last[:, :65] = (weight * np.cos(turn)).T
    last[:, LINES : LINES + 65] = (-weight * np.sin(turn)).T
    twiddle = np.zeros((2, LINES, ROWS))
    twiddle[0, :65] = np.cos(2.0 * np.pi * k1[:, None] * b[None, :] / PERIOD)
    twiddle[1, :65] = np.sin(2.0 * np.pi * k1[:, None] * b[None, :] / PERIOD)
    angle = 2.0 * np.pi * (b[:, None] * b[None, :] % ROWS) / ROWS
    cosine, sine = np.cos(angle), np.sin(angle)
    forward = np.block([[cosine, -sine], [sine, cosine]])
    inverse = np.block([[cosine, sine], [-sine, cosine]])
    first_h, first_l = high_low(first)
    last_h, last_l = high_low(last)
    return (
        np.concatenate([first_h, first_h, first_l], axis=1),
        np.concatenate([last_h, last_h, last_l], axis=1),
        twiddle.astype(np.float32),
        np.stack(high_low(forward)),
        np.stack(high_low(inverse)),
    )


def split(values):
    high = values.astype(bf16)
    return high, (values - high.astype(f32)).astype(bf16)


def dot(left, right):
    return jnp.dot(left, right, preferred_element_type=f32)


def encode(values, scale):
    level = jnp.floor(jnp.abs(values) * (LEVELS / scale) + 0.5)
    step = jnp.floor(level * (1.0 / 128.0))
    part = 1.0 + (level - 128.0 * step) * (1.0 / 128.0)
    code = jnp.exp2(step - BIAS) * part
    return jnp.where(values < 0.0, -code, code).astype(bf16)


def decode(code, scale):
    size = jnp.abs(code)
    step = jnp.floor(jnp.log(size) * (1.0 / math.log(2.0)) + 0.002)
    level = 128.0 * (step + BIAS + (size * jnp.exp2(-step) - 1.0))
    value = level * (scale * (1.0 / LEVELS))
    return jnp.where(code < 0.0, -value, value)


def pack_kernel(feat_ref, cot_ref, filt_ref, out_ref, turned, taps):
    for part in range(4):
        source = cot_ref if part == 3 else feat_ref.at[part]
        for j in range(16):
            turned[part, 128 * j : 128 * (j + 1), :] = source[:, 128 * j : 128 * (j + 1)].astype(f32).T
    for j in range(2):
        rows = slice(128 * j, 128 * (j + 1))
        value = filt_ref[:, rows].T
        high = value.astype(bf16).astype(f32)
        rest = value - high
        middle = rest.astype(bf16).astype(f32)
        taps[0, rows, :] = high
        taps[1, rows, :] = middle
        taps[2, rows, :] = (rest - middle).astype(bf16).astype(f32)

    def one(d, _):
        for gi in range(OWN):
            g = OWN * d + gi
            tiles = [turned.at[part][pl.ds(g, COPIES, stride=GROUPS), :] for part in range(4)]
            out_ref[d, 32 * gi : 32 * gi + 16, :] = jnp.concatenate(tiles[:2], axis=0).astype(bf16)
            out_ref[d, 32 * gi + 16 : 32 * gi + 32, :] = jnp.concatenate(tiles[2:], axis=0).astype(bf16)
        pieces = [taps[part, pl.ds(OWN * d, OWN), :] for part in range(3)]
        pieces.append(jnp.zeros((OWN, ROWS), f32))
        out_ref[d, 128:144, :] = jnp.concatenate(pieces, axis=0).astype(bf16)
        return 0

    lax.fori_loop(0, BLOCKS, one, 0)


def conv_kernel(
    in_ref, weight_ref, first_ref, last_ref, twiddle_ref, forward_ref, inverse_ref,
    out_ref, left, right, spec_high, spec_low, lines, filt, cross, extra, taps,
):
    gi = pl.program_id(0)
    chunk = 8
    lane = lax.broadcasted_iota(jnp.int32, (1, 1, ROWS), 2)
    cosine, sine = twiddle_ref[0], twiddle_ref[1]

    def shaped_chunk(a0, carry):
        raw = in_ref[pl.ds(a0, chunk), pl.ds(pl.multiple_of(32 * gi, 32), 32), :].astype(f32)
        signal = raw[:, :24]
        one = pltpu.roll(signal, 1, 2)
        two = pltpu.roll(signal, 2, 2)
        one_before = jnp.concatenate([carry[0][None], one[:-1]], axis=0)
        two_before = jnp.concatenate([carry[1][None], two[:-1]], axis=0)
        shift_one = jnp.where(lane < 1, one_before, one)
        shift_two = jnp.where(lane < 2, two_before, two)
        weights = weight_ref[gi]
        shaped = []
        for i in range(3):
            rows = slice(8 * i, 8 * i + 8)
            shaped.append(
                weights[3 * i] * signal[:, rows]
                + weights[3 * i + 1] * shift_one[:, rows]
                + weights[3 * i + 2] * shift_two[:, rows]
            )
        return raw[:, 24:], (signal, shift_one, shift_two), shaped, (one[-1], two[-1])

    empty = (jnp.zeros((24, ROWS), f32), jnp.zeros((24, ROWS), f32))

    def shape_step(step, carry):
        a0 = chunk * step
        upstream, _, shaped, carry = shaped_chunk(a0, carry)
        rows = pl.ds(pl.multiple_of(COPIES * a0, 64), COPIES * chunk)
        left[rows, :] = (shaped[1] * shaped[2]).reshape(COPIES * chunk, ROWS)
        right[rows, :] = (upstream * shaped[0]).reshape(COPIES * chunk, ROWS)
        return carry

    lax.fori_loop(0, BLOCKS // chunk, shape_step, empty)

    def pick(ref, k):
        return ref[pl.ds(k, BLOCKS, stride=COPIES), :]

    def to_lines(blocks, base):
        both = jnp.concatenate(blocks, axis=1)
        high, low = split(both)
        mid = dot(first_ref[...], jnp.concatenate([high, low, high], axis=0))
        out = []
        for j in range(2):
            real = mid[:LINES, ROWS * j : ROWS * (j + 1)]
            imag = mid[LINES:, ROWS * j : ROWS * (j + 1)]
            out.append(jnp.concatenate([real * cosine + imag * sine, imag * cosine - real * sine], axis=1))
        keep(jnp.concatenate(out, axis=0), base)

    def keep(values, base):
        high, low = split(values)
        spec_high[base : base + 2 * LINES, :] = high
        spec_low[base : base + 2 * LINES, :] = low

    def over_rows(matrix, count):
        high = spec_high[: LINES * count, :]
        return dot(high, matrix[0]) + dot(spec_low[: LINES * count, :], matrix[0]) + dot(high, matrix[1])

    def from_lines(values):
        pieces = []
        for j in range(2):
            real = values[LINES * j : LINES * (j + 1), :ROWS]
            imag = values[LINES * j : LINES * (j + 1), ROWS:]
            pieces.append(jnp.concatenate([real * cosine - imag * sine, imag * cosine + real * sine], axis=0))
        high, low = split(jnp.concatenate(pieces, axis=1))
        both = dot(last_ref[...], jnp.concatenate([high, low, high], axis=0))
        return both[:, :ROWS], both[:, ROWS:]

    @pl.when(gi == 0)
    def _():
        def widen(a, _):
            taps[pl.ds(pl.multiple_of(16 * a, 16), 16), :] = in_ref[a, 128:144, :].astype(f32)
            return 0

        lax.fori_loop(0, BLOCKS, widen, 0)
        blocks = []
        for f in range(OWN):
            parts = [taps[pl.ds(OWN * part + f, BLOCKS, stride=16), :] for part in range(3)]
            blocks.append(parts[0] + parts[1] + parts[2])
        for pair in range(OWN // 2):
            to_lines(blocks[2 * pair : 2 * pair + 2], 2 * LINES * pair)
        filt[...] = over_rows(forward_ref, OWN).reshape(OWN, LINES, 2 * ROWS)
        extra[...] = jnp.zeros_like(extra)

    for pair in range(COPIES // 2):
        to_lines([pick(left, 2 * pair), pick(left, 2 * pair + 1)], 2 * LINES * pair)
    for pair in range(COPIES // 2):
        to_lines([pick(right, 2 * pair), pick(right, 2 * pair + 1)], 2 * LINES * (COPIES // 2 + pair))
    lines[...] = over_rows(forward_ref, 2 * COPIES)

    filt_real, filt_imag = filt[gi, :, :ROWS], filt[gi, :, ROWS:]
    cross_real = jnp.zeros((LINES, ROWS), f32)
    cross_imag = jnp.zeros((LINES, ROWS), f32)
    for pair in range(COPIES // 2):
        forth, back = [], []
        for k in (2 * pair, 2 * pair + 1):
            here = slice(LINES * k, LINES * (k + 1))
            there = slice(LINES * (COPIES + k), LINES * (COPIES + k + 1))
            mix_real, mix_imag = lines[here, :ROWS], lines[here, ROWS:]
            grad_real, grad_imag = lines[there, :ROWS], lines[there, ROWS:]
            forth.append(
                jnp.concatenate(
                    [mix_real * filt_real - mix_imag * filt_imag, mix_real * filt_imag + mix_imag * filt_real], axis=1
                )
            )
            back.append(
                jnp.concatenate(
                    [
                        grad_real * filt_real + grad_imag * filt_imag,
                        grad_imag * filt_real - grad_real * filt_imag,
                    ],
                    axis=1,
                )
            )
            cross_real = cross_real + grad_real * mix_real + grad_imag * mix_imag
            cross_imag = cross_imag + grad_imag * mix_real - grad_real * mix_imag
        keep(jnp.concatenate(forth, axis=0), 2 * LINES * pair)
        keep(jnp.concatenate(back, axis=0), 2 * LINES * (COPIES // 2 + pair))
    cross[gi] = jnp.concatenate([cross_real, cross_imag], axis=1)
    lines[...] = over_rows(inverse_ref, 2 * COPIES)

    skip = weight_ref[gi, 9]
    for target, base in ((left, 0), (right, COPIES)):
        for pair in range(COPIES // 2):
            k = 2 * pair
            low, high = from_lines(lines[LINES * (base + k) : LINES * (base + k + 2), :])
            for j, value in ((0, low), (1, high)):
                place = pl.ds(k + j, BLOCKS, stride=COPIES)
                target[place, :] = value

    def finish(step, state):
        carry, sums = state
        a0 = chunk * step
        upstream, shifts, shaped, carry = shaped_chunk(a0, carry)
        rows = pl.ds(pl.multiple_of(COPIES * a0, 64), COPIES * chunk)
        mixer = shaped[1] * shaped[2]
        grad_conv = upstream * shaped[0]
        conv = left[rows, :].reshape(chunk, COPIES, ROWS) + skip * mixer
        grad_mixer = right[rows, :].reshape(chunk, COPIES, ROWS) + skip * grad_conv
        left[rows, :] = conv.reshape(COPIES * chunk, ROWS)
        right[rows, :] = grad_mixer.reshape(COPIES * chunk, ROWS)
        grads = (upstream * conv, grad_mixer * shaped[2], grad_mixer * shaped[1])
        new = []
        for i in range(3):
            for j in range(3):
                new.append(sums[3 * i + j] + jnp.sum(grads[i] * shifts[j][:, 8 * i : 8 * i + 8], axis=0))
        new.append(sums[9] + jnp.sum(grad_conv * mixer, axis=0))
        return carry, tuple(new)

    zero = jnp.zeros((COPIES, ROWS), f32)
    _, sums = lax.fori_loop(0, BLOCKS // chunk, finish, (empty, (zero,) * 10))

    flat = lane[0]
    totals = zero
    for i in range(10):
        total = jnp.sum(sums[i], axis=1, keepdims=True) * (1.0 / math.sqrt(BLOCKS * ROWS))
        totals = totals + jnp.where(flat == 16 + i, total, 0.0)

    def send(step, _):
        a0 = chunk * step
        rows = pl.ds(pl.multiple_of(COPIES * a0, 64), COPIES * chunk)
        after = pl.ds(pl.multiple_of(jnp.minimum(COPIES * (a0 + chunk), COPIES * (BLOCKS - 1)), COPIES), COPIES)
        keep_last = jnp.where(a0 + chunk < BLOCKS, 1.0, 0.0)
        codes = []
        entry = jnp.broadcast_to(totals, (chunk, COPIES, ROWS))
        for slot, ref in ((0, left), (1, right)):
            value = ref[rows, :].reshape(chunk, COPIES, ROWS)
            largest = jnp.max(jnp.abs(value), axis=2, keepdims=True)
            scale = (jnp.maximum(largest, 1e-30) * (1.0 + 1.0 / 128.0)).astype(bf16).astype(f32)
            codes.append(encode(value, scale))
            following = jnp.concatenate([value[1:], ref[after, :][None] * keep_last], axis=0)
            entry = entry + jnp.where(lane == 26 + slot, scale, 0.0)
            moved = pltpu.roll(following, 28 + 2 * slot, 2)
            entry = entry + jnp.where((lane >= 28 + 2 * slot) & (lane < 30 + 2 * slot), moved, 0.0)
        out_ref[pl.ds(a0, chunk), pl.ds(pl.multiple_of(16 * gi, 16), 16), :] = jnp.concatenate(codes, axis=1)
        extra[rows, :] = extra[rows, :] + pltpu.roll(entry, 32 * gi, 2).reshape(COPIES * chunk, ROWS)
        return 0

    lax.fori_loop(0, BLOCKS // chunk, send, 0)

    @pl.when(gi == OWN - 1)
    def _():
        for pair in range(OWN // 2):
            keep(cross[2 * pair : 2 * pair + 2].reshape(2 * LINES, 2 * ROWS), 2 * LINES * pair)
        temporal = over_rows(inverse_ref, OWN)
        scale = 1.0 / math.sqrt(BLOCKS * ROWS * 2 * COPIES)
        for pair in range(OWN // 2):
            both = from_lines(temporal[2 * LINES * pair : 2 * LINES * (pair + 1)])
            for j in range(2):
                f = 2 * pair + j
                value = both[j] * scale
                for k in range(COPIES):
                    place = pl.ds(k, BLOCKS, stride=COPIES)
                    moved = pltpu.roll(value, (32 * f - 16 * k) % ROWS, 1)
                    inside = (flat >= 32 * f) & (flat < 32 * f + 16)
                    extra[place, :] = jnp.where(inside, moved, extra[place, :])

        def write(a, _):
            value = extra[pl.ds(pl.multiple_of(COPIES * a, COPIES), COPIES), :]
            high = value.astype(bf16).astype(f32)
            out_ref[a, 64:80, :] = jnp.concatenate([high, value - high], axis=0).astype(bf16)
            return 0

        lax.fori_loop(0, BLOCKS, write, 0)


def extras_kernel(in_ref, spread_ref, filt_ref, ext_ref, wide):
    def widen(d, _):
        wide[pl.ds(pl.multiple_of(16 * d, 16), 16), :] = in_ref[d, :, :].astype(f32)
        return 0

    lax.fori_loop(0, BLOCKS, widen, 0)
    for k in range(COPIES):
        both = []
        for part in range(2):
            piece = wide[pl.ds(8 * part + k, BLOCKS, stride=16), :]
            both.append(piece.T.astype(bf16))
        total = jnp.zeros((32, GROUPS), f32)
        for gi in range(OWN):
            rows = slice(32 * gi, 32 * gi + 32)
            for part in range(2):
                total = total + dot(both[part][rows], spread_ref[gi])
        filt_ref[16 * k : 16 * (k + 1), :] = total[:16]
        ext_ref[:, GROUPS * k : GROUPS * (k + 1)] = total[16:]


def finish_kernel(
    in_ref, feat_ref, cot_ref, before_ref, after_ref, weight_ref, ext_ref, mixed_ref, grad_ref, wide
):
    k = pl.program_id(0)

    @pl.when(k == 0)
    def _():
        def widen(d, _):
            wide[pl.ds(pl.multiple_of(64 * d, 64), 64), :] = in_ref[d, :64, :].astype(f32)
            return 0

        lax.fori_loop(0, BLOCKS, widen, 0)

    row = lax.broadcasted_iota(jnp.int32, (ROWS, 1), 0)
    signals = []
    for slot in range(2):
        halves = []
        for half in range(2):
            place = pl.ds(2048 * half + 8 * slot + k, 128, stride=16)
            halves.append(wide[place, :].T)
        signals.append(decode(jnp.concatenate(halves, axis=1), ext_ref[10 + slot : 11 + slot, :]))
    conv, grad_mixer = signals
    upstream = cot_ref[...].astype(f32)
    shaped, shaped_after, weights = [], [], []
    for i in range(3):
        taps = [weight_ref[3 * i + j : 3 * i + j + 1, :] for j in range(3)]
        weights.append(taps)
        value = feat_ref[i].astype(f32)
        before = before_ref[i].astype(f32)
        after = after_ref[i].astype(f32)
        one = jnp.where(row == 0, before[1:2], pltpu.roll(value, 1, 0))
        two = jnp.where(row == 0, before[0:1], jnp.where(row == 1, before[1:2], pltpu.roll(value, 2, 0)))
        shaped.append(taps[0] * value + taps[1] * one + taps[2] * two)
        final, second = value[ROWS - 1 : ROWS], value[ROWS - 2 : ROWS - 1]
        shaped_after.append(
            (
                taps[0] * after[0:1] + taps[1] * final + taps[2] * second,
                taps[0] * after[1:2] + taps[1] * after[0:1] + taps[2] * final,
            )
        )
    mixed_ref[...] = (shaped[0] * conv).astype(bf16)
    grads = (upstream * conv, grad_mixer * shaped[2], grad_mixer * shaped[1])
    upstream_after = after_ref[0].astype(f32)
    for i in range(3):
        grad = grads[i]
        following = []
        for t in range(2):
            conv_t = ext_ref[12 + t : 13 + t, :]
            mixer_t = ext_ref[14 + t : 15 + t, :]
            if i == 0:
                following.append(upstream_after[t : t + 1] * conv_t)
            else:
                following.append(mixer_t * shaped_after[3 - i][t])
        one = jnp.where(row == ROWS - 1, following[0], pltpu.roll(grad, ROWS - 1, 0))
        two = jnp.where(
            row == ROWS - 1,
            following[1],
            jnp.where(row == ROWS - 2, following[0], pltpu.roll(grad, ROWS - 2, 0)),
        )
        grad_ref[i] = weights[i][0] * grad + weights[i][1] * one + weights[i][2] * two


def exchange(values):
    return lax.all_to_all(values, "ctx", split_axis=0, concat_axis=0, tiled=True)


def shift(block, distance):
    route = [(i, i + distance) for i in range(BLOCKS) if 0 <= i + distance < BLOCKS]
    return lax.ppermute(block, "ctx", route)


def shards(features, short_weight, skip, long_filter, cotangent):
    rank = lax.axis_index("ctx")
    half = lax.axis_index("ch")
    breadth = features.shape[2]
    limit = pltpu.CompilerParams(vmem_limit_bytes=56 * 2**20)

    packed = pl.pallas_call(
        pack_kernel,
        out_shape=jax.ShapeDtypeStruct((BLOCKS, SEND_ROWS, ROWS), bf16),
        scratch_shapes=[pltpu.VMEM((4, breadth, ROWS), f32), pltpu.VMEM((3, GROUPS, ROWS), f32)],
        compiler_params=limit,
        name="pack",
    )(features, cotangent, long_filter)

    before = shift(features[:, ROWS - 2 :, :], 1)
    after = shift(jnp.concatenate([cotangent[None, :2], features[1:, :2]], axis=0), -1)

    first, last, twiddle, forward, inverse = tables()
    weights = jnp.concatenate([short_weight.reshape(9, breadth), skip[None]], axis=0)
    own = lax.dynamic_index_in_dim(weights.reshape(10, COPIES, BLOCKS, OWN), rank, 2, keepdims=False)
    own = jnp.broadcast_to(jnp.transpose(own, (2, 0, 1))[..., None], (OWN, 10, COPIES, ROWS))

    gathered = exchange(packed)

    vmem = pl.BlockSpec(memory_space=pltpu.VMEM)
    returned = pl.pallas_call(
        conv_kernel,
        grid=(OWN,),
        in_specs=[vmem] * 7,
        out_specs=vmem,
        out_shape=jax.ShapeDtypeStruct((BLOCKS, BACK_ROWS, ROWS), bf16),
        scratch_shapes=[
            pltpu.VMEM((COPIES * BLOCKS, ROWS), f32),
            pltpu.VMEM((COPIES * BLOCKS, ROWS), f32),
            pltpu.VMEM((2 * COPIES * LINES, 2 * ROWS), bf16),
            pltpu.VMEM((2 * COPIES * LINES, 2 * ROWS), bf16),
            pltpu.VMEM((2 * COPIES * LINES, 2 * ROWS), f32),
            pltpu.VMEM((OWN, LINES, 2 * ROWS), f32),
            pltpu.VMEM((OWN, LINES, 2 * ROWS), f32),
            pltpu.VMEM((COPIES * BLOCKS, ROWS), f32),
            pltpu.VMEM((16 * BLOCKS, ROWS), f32),
        ],
        compiler_params=limit,
        name="conv",
    )(gathered, own, first, last, twiddle, forward, inverse)

    home = exchange(returned)

    spread = np.zeros((OWN, BLOCKS, GROUPS), ml_dtypes.bfloat16)
    for gi in range(OWN):
        spread[gi, np.arange(BLOCKS), OWN * np.arange(BLOCKS) + gi] = 1.0
    raw_filter, ext = pl.pallas_call(
        extras_kernel,
        grid=(1,),
        in_specs=[
            pl.BlockSpec((BLOCKS, 16, ROWS), lambda i: (0, 4, 0)),
            pl.BlockSpec((OWN, BLOCKS, GROUPS), lambda i: (0, 0, 0)),
        ],
        out_specs=[
            pl.BlockSpec((ROWS, GROUPS), lambda i: (0, 0)),
            pl.BlockSpec((16, breadth), lambda i: (0, 0)),
        ],
        out_shape=[
            jax.ShapeDtypeStruct((ROWS, GROUPS), f32),
            jax.ShapeDtypeStruct((16, breadth), f32),
        ],
        scratch_shapes=[pltpu.VMEM((16 * BLOCKS, ROWS), f32)],
        compiler_params=limit,
        name="extras",
    )(home, spread)

    mine = lax.dynamic_slice_in_dim(raw_filter, half * (GROUPS // 2), GROUPS // 2, axis=1)
    other = lax.dynamic_slice_in_dim(raw_filter, (1 - half) * (GROUPS // 2), GROUPS // 2, axis=1)
    arrived = lax.ppermute(other, "ch", [(0, 1), (1, 0)])

    mixed, feature_gradient = pl.pallas_call(
        finish_kernel,
        grid=(COPIES,),
        in_specs=[
            pl.BlockSpec((BLOCKS, BACK_ROWS, ROWS), lambda k: (0, 0, 0)),
            pl.BlockSpec((3, ROWS, GROUPS), lambda k: (0, 0, k)),
            pl.BlockSpec((ROWS, GROUPS), lambda k: (0, k)),
            pl.BlockSpec((3, 2, GROUPS), lambda k: (0, 0, k)),
            pl.BlockSpec((3, 2, GROUPS), lambda k: (0, 0, k)),
            pl.BlockSpec((9, GROUPS), lambda k: (0, k)),
            pl.BlockSpec((16, GROUPS), lambda k: (0, k)),
        ],
        out_specs=[
            pl.BlockSpec((ROWS, GROUPS), lambda k: (0, k)),
            pl.BlockSpec((3, ROWS, GROUPS), lambda k: (0, 0, k)),
        ],
        out_shape=[
            jax.ShapeDtypeStruct((ROWS, breadth), bf16),
            jax.ShapeDtypeStruct((3, ROWS, breadth), f32),
        ],
        scratch_shapes=[pltpu.VMEM((64 * BLOCKS, ROWS), f32)],
        compiler_params=limit,
        name="finish",
    )(home, features, cotangent, before, after, short_weight.reshape(9, breadth), ext)

    grad_short = ext[:9].reshape(3, 3, breadth)
    grad_skip = ext[9]
    return (mixed, feature_gradient, grad_short, grad_skip, mine + arrived)


def solution(mesh):
    return jax.shard_map(
        shards,
        mesh=mesh,
        in_specs=(
            P(None, "ctx", "ch"),
            P(None, None, "ch"),
            P("ch"),
            P("ctx", None),
            P("ctx", "ch"),
        ),
        out_specs=(
            P("ctx", "ch"),
            P(None, "ctx", "ch"),
            P(None, None, "ch"),
            P("ch"),
            P("ctx", "ch"),
        ),
        check_vma=False,
    )
```

time: 1260 us -> 137 us (0.11)
  waiting for transfers between devices: 631 us -> 44 us
  local copies, waits for them, and re-layouts: 182 us -> 15.2 us
  blocking collectives: 149 us -> 0 us
  matrix products: 102 us -> 0 us
  starting transfers between devices: 113 us -> 25.3 us
  other arithmetic: 54.2 us -> 1.69 us
  Pallas kernels: 0 us -> 47.6 us
  between operations: 16.7 us -> 0.74 us
    psum x1 -> x0, waiting for transfers between devices: 467 us -> none  [shards(): total_taps, total_skip = lax.psum((tap_terms, skip_term), 'ctx')]
    psum x1 -> x0, blocking collectives: 149 us -> none  [shards(): total_taps, total_skip = lax.psum((tap_terms, skip_term), 'ctx')]
    all_to_all x12 -> x2, waiting for transfers between devices: 164 us -> 44 us  [exchange(): lax.all_to_all(values, 'ctx', split_axis=0, concat_axis=0, tiled=True)]
    dot_general x36 -> x0, matrix products: 102 us -> none  [the longest x3 12.9 us: to_spectrum(): real_part = jnp.einsum('pk,prc->rkc', cos_blk, columns, precision=exact)]
    all_to_all x12 -> x2, starting transfers between devices: 106 us -> 17.1 us  [exchange(): lax.all_to_all(values, 'ctx', split_axis=0, concat_axis=0, tiled=True)]
    all_to_all x12 -> x0, local copies, waits for them, and re-layouts: 58.4 us -> none  [regroup(): lax.all_to_all(values, 'ctx', split_axis=1, concat_axis=0, tiled=True)]
    another operation x13 -> x0, local copies, waits for them, and re-layouts: 55.4 us -> none  [the longest x3 22 us: from_spectrum(): jnp.stack([real_mid * cos_tw - imag_mid * sin_tw, imag_mid * cos_tw + rea...]
    pallas_call x0 -> x4, Pallas kernels: none -> 47.6 us  [the longest x1 29.4 us: shards(): pl.pallas_call(conv_kernel, grid=(OWN,), in_specs=[vmem] * 7, out_specs=v...]
  transfers between devices with their start and end apart: 16 -> 5, of which waited for: 7 -> 2; matrix products, arithmetic and copies ran while one was open for 17% -> 9% of each run, Pallas kernels for 0% -> 7%
where the time goes in v1:
time: 137 us; the launch traced here: 134 us
  Pallas kernels  47.6 us (35%)
  waiting for transfers between devices  44 us (32%)
  starting transfers between devices  25.3 us (18%)
  local copies, waits for them, and re-layouts  15.2 us (11%)
  other arithmetic  1.69 us (1%)
    all_to_all x2, waiting for transfers between devices, exchange(): lax.all_to_all(values, 'ctx', split_axis=0, concat_axis=0, tiled=True)  44 us
    pallas_call x1, Pallas kernels, shards(): pl.pallas_call(conv_kernel, grid=(OWN,), in_specs=[vmem] * 7, out_specs=v...  29.4 us
    all_to_all x2, starting transfers between devices, exchange(): lax.all_to_all(values, 'ctx', split_axis=0, concat_axis=0, tiled=True)  17.1 us
    pallas_call x1, Pallas kernels, shards(): pl.pallas_call(finish_kernel, grid=(COPIES,), in_specs=[pl.BlockSpec((BLO...  9.16 us
    pallas_call x1, Pallas kernels, shards(): pl.pallas_call(pack_kernel, out_shape=jax.ShapeDtypeStruct((BLOCKS, SEND_...  6.43 us
    ppermute x2, starting transfers between devices, shift(): return lax.ppermute(block, 'ctx', route)  5.56 us
    concatenate x2, local copies, waits for them, and re-layouts, shards(): jnp.concatenate([short_weight.reshape(9, breadth), skip[None]], axis=0)  4.18 us
    unnamed x14, local copies, waits for them, and re-layouts  2.84 us
  transfers between devices with their start and end apart: 5, of which 2 were waited for; matrix products, arithmetic and copies ran while one was open for 9% of the time, Pallas kernels for 7%

profile of v1, /device:TPU:1, one launch (start us, length us, event | category | flops | bytes accessed | tf_op | source)
XLA Modules:
  0.0 134.5 jit_solution(14933595786864965209)
XLA Ops:
  0.6 6.4 %pack.1 = bf16[64,144,128]{2,1,0:T(8,128)(2,1)} custom-call(bf16[3,128,2048]{2,1,0:T(8,128)(2,1)} %feat_ref.3, bf16[128,2048]{1,0:T(8,128)(2,1)} %cot_ref.3, f32[128,256]{1,0:T(8,128)} %filt_ref.1), custom_call_target="tpu_custom_call" | custom-call | tf_op jit(solution)/shard_map/pack/pallas_call | solution.py:428
  7.1 11.0 %all-to-all-start = ((bf16[64,144,128]{2,1,0:T(8,128)(2,1)}), bf16[64,144,128]{2,1,0:T(8,128)(2,1)S(1)}, u32[]{:S(2)}, u32[]{:S(2)}) async-start(bf16[64,144,128]{2,1,0:T(8,128)(2,1)} %pack.1), calls=%async_computation | async-start | bytes 4718592 | tf_op jit(solution)/shard_map/all_to_all | solution.py:414
  18.0 0.0 copy-start.6
  18.1 3.9 %concatenate.11 = f32[9,8,64,4]{3,2,1,0:T(8,128)} reshape(f32[3,3,2048]{2,1,0:T(4,128)S(1)} %copy-done.2) | data formatting | bytes 147456 | tf_op jit(solution)/shard_map/concatenate | solution.py:440
  22.0 0.3 concatenate.12
  22.3 1.0 fusion
  23.3 0.2 copy.25
  23.4 25.6 %all-to-all-done.in_ref = bf16[64,144,128]{2,1,0:T(8,128)(2,1)S(1)} async-done(((bf16[64,144,128]{2,1,0:T(8,128)(2,1)}), bf16[64,144,128]{2,1,0:T(8,128)(2,1)S(1)}, u32[]{:S(2)}, u32[]{:S(2)}) %all-to-all-start) | async-done | bytes 2359328 | tf_op jit(solution)/shard_map/all_to_all | solution.py:414
  49.0 0.9 broadcast_in_dim.4.weight_ref
  49.9 0.6 copy-done.1
  50.5 29.4 %conv.1 = bf16[64,80,128]{2,1,0:T(8,128)(2,1)} custom-call(bf16[64,144,128]{2,1,0:T(8,128)(2,1)} %copy-done.1, f32[4,10,8,128]{3,2,1,0:T(8,128)} %broadcast_in_dim.4.weight_ref, bf16[144,192]{1,0:T(8,128)(2,1)} %constant.33.clone.first_ref, bf16[64,432]{1,0:T(8,128)(2,1)} %constant.34.clone.last_ref, f32[2,72,128]{2,1,0:T(8,128)} %constant.35.clone.twiddle_ref, ...), custom_call_target="tpu_custom_call" | custom-call | tf_op jit(solution)/shard_map/conv/pallas_call | solution.py:447
  79.8 6.1 %all-to-all-start.1 = ((bf16[64,80,128]{2,1,0:T(8,128)(2,1)}), bf16[64,80,128]{2,1,0:T(8,128)(2,1)S(1)}, u32[]{:S(2)}, u32[]{:S(2)}) async-start(bf16[64,80,128]{2,1,0:T(8,128)(2,1)} %conv.1), calls=%async_computation.1 | async-start | bytes 2621440 | tf_op jit(solution)/shard_map/all_to_all | solution.py:414
  85.9 0.9 slice.17
  86.8 0.8 slice_bitcast_fusion
  87.6 18.4 %all-to-all-done.1.in_ref = bf16[64,80,128]{2,1,0:T(8,128)(2,1)S(1)} async-done(((bf16[64,80,128]{2,1,0:T(8,128)(2,1)}), bf16[64,80,128]{2,1,0:T(8,128)(2,1)S(1)}, u32[]{:S(2)}, u32[]{:S(2)}) %all-to-all-start.1) | async-done | bytes 1310752 | tf_op jit(solution)/shard_map/all_to_all | solution.py:414
  106.0 1.1 copy-done
  107.1 2.6 %extras.1 = (f32[128,256]{1,0:T(8,128)}, f32[16,2048]{1,0:T(8,128)}) custom-call(bf16[64,80,128]{2,1,0:T(8,128)(2,1)} %copy-done, bf16[4,64,256]{2,1,0:T(8,128)(2,1)} %constant.38.clone.spread_ref), custom_call_target="tpu_custom_call" | custom-call | tf_op jit(solution)/shard_map/extras/pallas_call | solution.py:473
  109.7 0.9 constant_dynamic-slice_fusion
  110.6 2.6 %collective-permute-start.2 = (f32[128,128]{1,0:T(8,128)S(1)}, f32[128,128]{1,0:T(8,128)S(1)}, u32[]{:S(2)}, u32[]{:S(2)}) collective-permute-start(f32[128,128]{1,0:T(8,128)S(1)} %constant_dynamic-slice_fusion), channel_id=1, source_target_pairs={{0,1},{1,0},{2,3},{3,2},{4,5},{5,4},{6,7},{7,6},{8,9},{9,8},{10,11... | collective-permute-start | bytes 196616 | tf_op jit(solution)/shard_map/ppermute | solution.py:495
  113.2 2.8 %collective-permute-start.1 = (bf16[3,2,2048]{2,1,0:T(2,128)(2,1)S(1)}, bf16[3,2,2048]{2,1,0:T(2,128)(2,1)S(1)}, u32[]{:S(2)}, u32[]{:S(2)}) collective-permute-start(bf16[3,2,2048]{2,1,0:T(2,128)(2,1)S(1)} %pad_maximum_fusion), channel_id=1, source_target_pairs={{2,0},{4,2},{6,4},{8,6},{10,8},{12,10},{14,12},{16,14},{18,16},{20... | collective-permute-start | bytes 73736 | tf_op jit(solution)/shard_map/ppermute | solution.py:419
  116.0 0.9 slice.15
  117.0 2.8 %collective-permute-start = (bf16[3,2,2048]{2,1,0:T(2,128)(2,1)S(1)}, bf16[3,2,2048]{2,1,0:T(2,128)(2,1)S(1)}, u32[]{:S(2)}, u32[]{:S(2)}) collective-permute-start(bf16[3,2,2048]{2,1,0:T(2,128)(2,1)S(1)} %slice.15), channel_id=1, source_target_pairs={{0,2},{2,4},{4,6},{6,8},{8,10},{10,12},{12,14},{14,16},{16,18},{18... | collective-permute-start | bytes 73736 | tf_op jit(solution)/shard_map/ppermute | solution.py:419
  119.7 0.7 reshape.23.weight_ref
  120.4 1.4 %slice.19 = f32[1,2048]{1,0:T(1,128)} slice(f32[16,2048]{1,0:T(8,128)} %get-tuple-element.9.ext_ref), slice={[9:10], [0:2048]} | slice | bytes 16384 | tf_op jit(solution)/shard_map/slice | solution.py:523
  121.9 1.6 %reshape.24 = f32[3,3,2048]{2,1,0:T(4,128)} reshape(f32[9,2048]{1,0:T(8,128)} %bitcast.7) | data formatting | bytes 147456 | tf_op jit(solution)/shard_map/reshape | solution.py:522
  123.4 0.0 collective-permute-done.1.after_ref
  123.4 0.0 collective-permute-done.before_ref
  123.5 0.6 copy-done.4
  124.0 0.6 copy-done.5
  124.7 9.2 %finish.1 = (bf16[128,2048]{1,0:T(8,128)(2,1)}, f32[3,128,2048]{2,1,0:T(8,128)}) custom-call(bf16[64,80,128]{2,1,0:T(8,128)(2,1)} %copy-done, bf16[3,128,2048]{2,1,0:T(8,128)(2,1)} %feat_ref.3, bf16[128,2048]{1,0:T(8,128)(2,1)} %cot_ref.3, bf16[3,2,2048]{2,1,0:T(2,128)(2,1)} %copy-done.5, bf16[3,2,2048]{2,1,0:T(2,128)(2,1)} %copy-done.4, ...), custom_call_target="tpu_custom_call" | custom-call | tf_op jit(solution)/shard_map/finish/pallas_call | solution.py:497
  133.8 0.0 collective-permute-done.2
  133.8 0.6 dynamic-slice_add_fusion
  (10 shorter events, 0.1 us)
Async XLA Ops:
  7.1 11.0 %copy-start.2 = (f32[3,3,2048]{2,1,0:T(4,128)S(1)}, f32[3,3,2048]{2,1,0:T(4,128)}, u32[]{:S(2)}) copy-start(f32[3,3,2048]{2,1,0:T(4,128)} %param.12) | copy-start | bytes 221188
  7.1 41.9 %all-to-all-start = ((bf16[64,144,128]{2,1,0:T(8,128)(2,1)}), bf16[64,144,128]{2,1,0:T(8,128)(2,1)S(1)}, u32[]{:S(2)}, u32[]{:S(2)}) async-start(bf16[64,144,128]{2,1,0:T(8,128)(2,1)} %pack.1), calls=%async_computation | async-start | bytes 4718592 | tf_op jit(solution)/shard_map/all_to_all | solution.py:414
  18.0 4.0 %copy-start.6 = (f32[2048]{0:T(1024)S(1)}, f32[2048]{0:T(1024)}, u32[]{:S(2)}) copy-start(f32[2048]{0:T(1024)} %param.13) | copy-start | bytes 24580
  49.0 1.5 %copy-start.1 = (bf16[64,144,128]{2,1,0:T(8,128)(2,1)}, bf16[64,144,128]{2,1,0:T(8,128)(2,1)S(1)}, u32[]{:S(2)}) copy-start(bf16[64,144,128]{2,1,0:T(8,128)(2,1)S(1)} %all-to-all-done.in_ref) | copy-start | bytes 7077892
  79.8 26.1 %all-to-all-start.1 = ((bf16[64,80,128]{2,1,0:T(8,128)(2,1)}), bf16[64,80,128]{2,1,0:T(8,128)(2,1)S(1)}, u32[]{:S(2)}, u32[]{:S(2)}) async-start(bf16[64,80,128]{2,1,0:T(8,128)(2,1)} %conv.1), calls=%async_computation.1 | async-start | bytes 2621440 | tf_op jit(solution)/shard_map/all_to_all | solution.py:414
  106.0 1.1 copy-start
  109.7 24.2 %copy-start.3 = (f32[128,256]{1,0:T(8,128)S(1)}, f32[128,256]{1,0:T(8,128)}, u32[]{:S(2)}) copy-start(f32[128,256]{1,0:T(8,128)} %get-tuple-element.12) | copy-start | bytes 393220
  110.6 23.2 %collective-permute-start.2 = (f32[128,128]{1,0:T(8,128)S(1)}, f32[128,128]{1,0:T(8,128)S(1)}, u32[]{:S(2)}, u32[]{:S(2)}) collective-permute-start(f32[128,128]{1,0:T(8,128)S(1)} %constant_dynamic-slice_fusion), channel_id=1, source_target_pairs={{0,1},{1,0},{2,3},{3,2},{4,5},{5,4},{6,7},{7,6},{8,9},{9,8},{10,11... | collective-permute-start | bytes 196616 | tf_op jit(solution)/shard_map/ppermute | solution.py:495
  113.2 10.2 %collective-permute-start.1 = (bf16[3,2,2048]{2,1,0:T(2,128)(2,1)S(1)}, bf16[3,2,2048]{2,1,0:T(2,128)(2,1)S(1)}, u32[]{:S(2)}, u32[]{:S(2)}) collective-permute-start(bf16[3,2,2048]{2,1,0:T(2,128)(2,1)S(1)} %pad_maximum_fusion), channel_id=1, source_target_pairs={{2,0},{4,2},{6,4},{8,6},{10,8},{12,10},{14,12},{16,14},{18,16},{20... | collective-permute-start | bytes 73736 | tf_op jit(solution)/shard_map/ppermute | solution.py:419
  117.0 6.5 %collective-permute-start = (bf16[3,2,2048]{2,1,0:T(2,128)(2,1)S(1)}, bf16[3,2,2048]{2,1,0:T(2,128)(2,1)S(1)}, u32[]{:S(2)}, u32[]{:S(2)}) collective-permute-start(bf16[3,2,2048]{2,1,0:T(2,128)(2,1)S(1)} %slice.15), channel_id=1, source_target_pairs={{0,2},{2,4},{4,6},{6,8},{8,10},{10,12},{12,14},{14,16},{16,18},{18... | collective-permute-start | bytes 73736 | tf_op jit(solution)/shard_map/ppermute | solution.py:419
  123.4 0.6 copy-start.4
  124.0 0.6 copy-start.5

commit v2 on v0

v2 whole, which is shorter than its diff:
```python
import functools
import math

import jax
import jax.numpy as jnp
import ml_dtypes
import numpy as np
from jax import lax
from jax.experimental import pallas as pl
from jax.experimental.pallas import tpu as pltpu
from jax.sharding import PartitionSpec as P

f32 = jnp.float32
bf16 = jnp.bfloat16

BLOCKS = 64
ROWS = 128
COPIES = 8
GROUPS = 256
OWN = GROUPS // BLOCKS
LINES = 72
PERIOD = 2 * BLOCKS * ROWS
SIGNAL_ROWS = OWN * 4 * COPIES
SEND_ROWS = SIGNAL_ROWS + 2 * OWN
RESULT_ROWS = OWN * 2 * COPIES
BACK_ROWS = RESULT_ROWS + 2 * COPIES
AFTER, SCALE, TOTAL, FILTER = 0, 4, 6, 16
LEVELS = 32000.0
BIAS = 124.0
GANG = 8
SPACING = GROUPS + 1
LIMIT = pltpu.CompilerParams(vmem_limit_bytes=56 * 2**20)


def high_low(values):
    high = values.astype(ml_dtypes.bfloat16)
    low = (values - high.astype(np.float64)).astype(ml_dtypes.bfloat16)
    return high, low


def tables():
    k1 = np.arange(65)
    a = np.arange(BLOCKS)
    b = np.arange(ROWS)
    turn = 2.0 * np.pi * (k1[:, None] * a[None, :] % ROWS) / ROWS
    first = np.zeros((2 * LINES, BLOCKS))
    first[:65] = np.cos(turn)
    first[LINES : LINES + 65] = -np.sin(turn)
    weight = np.where((k1 == 0) | (k1 == 64), 1.0, 2.0)[:, None] / PERIOD
    last = np.zeros((BLOCKS, 2 * LINES))
    last[:, :65] = (weight * np.cos(turn)).T
    last[:, LINES : LINES + 65] = (-weight * np.sin(turn)).T
    twiddle = np.zeros((2, LINES, ROWS))
    twiddle[0, :65] = np.cos(2.0 * np.pi * k1[:, None] * b[None, :] / PERIOD)
    twiddle[1, :65] = np.sin(2.0 * np.pi * k1[:, None] * b[None, :] / PERIOD)
    angle = 2.0 * np.pi * (b[:, None] * b[None, :] % ROWS) / ROWS
    cosine, sine = np.cos(angle), np.sin(angle)
    forward = np.block([[cosine, -sine], [sine, cosine]])
    inverse = np.block([[cosine, sine], [-sine, cosine]])
    first_h, first_l = high_low(first)
    last_h, last_l = high_low(last)
    forward_h, forward_l = high_low(forward)
    inverse_h, inverse_l = high_low(inverse)
    return (
        np.concatenate([first_h, first_h, first_l], axis=1),
        np.concatenate([last_h, last_h, last_l], axis=1),
        twiddle.astype(np.float32),
        np.concatenate([forward_h, forward_h, forward_l], axis=0),
        np.concatenate([inverse_h, inverse_h, inverse_l], axis=0),
    )


def split(values):
    high = values.astype(bf16)
    return high, (values - high.astype(f32)).astype(bf16)


def dot(left, right):
    return jnp.dot(left, right, preferred_element_type=f32)


def encode(values, scale):
    level = jnp.floor(jnp.abs(values) * (LEVELS / scale) + 0.5)
    step = jnp.floor(level * (1.0 / 128.0))
    part = 1.0 + (level - 128.0 * step) * (1.0 / 128.0)
    code = jnp.exp2(step - BIAS) * part
    return jnp.where(values < 0.0, -code, code).astype(bf16)


def decode(code, scale):
    size = jnp.abs(code)
    step = jnp.floor(jnp.log(size) * (1.0 / math.log(2.0)) + 0.002)
    level = 128.0 * (step + BIAS + (size * jnp.exp2(-step) - 1.0))
    value = level * (scale * (1.0 / LEVELS))
    return jnp.where(code < 0.0, -value, value)


def pack_kernel(
    feat_ref, cot_ref, filt_ref, out_ref, feat, cot, filt, packed, turned, taps, feat_sem, cot_sem, filt_sem, out_sem
):
    arriving = []
    for k in range(COPIES):
        lanes = pl.ds(GROUPS * k, GROUPS)
        arriving.append(
            (
                pltpu.make_async_copy(feat_ref.at[:, :, lanes], feat.at[k], feat_sem.at[k]),
                pltpu.make_async_copy(cot_ref.at[:, lanes], cot.at[k], cot_sem.at[k]),
            )
        )
    filter_copy = pltpu.make_async_copy(filt_ref, filt, filt_sem)
    filter_copy.start()
    for copies in arriving:
        for copy in copies:
            copy.start()

    filter_copy.wait()
    value = filt[...].T
    high = value.astype(bf16).astype(f32)
    taps[0] = high
    taps[1] = value - high
    for k in range(COPIES):
        for copy in arriving[k]:
            copy.wait()
        for part in range(4):
            source = cot[k] if part == 3 else feat[k, part]
            turned[part, SPACING * k : SPACING * k + GROUPS, :] = source.astype(f32).T

    def one(d, _):
        for gi in range(OWN):
            n = OWN * d + gi
            tiles = [turned.at[part][pl.ds(n, COPIES, stride=SPACING), :] for part in range(4)]
            packed[d, 32 * gi : 32 * gi + 16, :] = jnp.concatenate(tiles[:2], axis=0).astype(bf16)
            packed[d, 32 * gi + 16 : 32 * gi + 32, :] = jnp.concatenate(tiles[2:], axis=0).astype(bf16)
        pieces = [taps[part, pl.ds(OWN * d, OWN), :] for part in range(2)]
        packed[d, SIGNAL_ROWS:SEND_ROWS, :] = jnp.concatenate(pieces, axis=0).astype(bf16)
        return 0

    leaving = []
    share = BLOCKS // 4
    for j in range(4):
        lax.fori_loop(share * j, share * (j + 1), one, 0, unroll=4)
        place = pl.ds(share * j, share)
        leaving.append(pltpu.make_async_copy(packed.at[place], out_ref.at[place], out_sem.at[j]))
        leaving[-1].start()
    for copy in leaving:
        copy.wait()


def conv_kernel(
    in_ref, taps_ref, weight_ref, first_ref, last_ref, twiddle_ref, forward_ref, inverse_ref, out_ref,
    raw_buf, code_buf, in_sem, out_sem,
    left, right, shift_one, shift_two, spec_high, spec_low, lines, filt, cross, extra, taps, totals, own,
):
    chunk = 8
    steps = BLOCKS // chunk
    lane = lax.broadcasted_iota(jnp.int32, (1, 1, ROWS), 2)
    flat = lane[0]
    cosine, sine = twiddle_ref[0], twiddle_ref[1]

    def arriving(gi):
        rows = pl.ds(pl.multiple_of(4 * COPIES * gi, 4 * COPIES), 4 * COPIES)
        return pltpu.make_async_copy(in_ref.at[:, rows, :], raw_buf.at[gi], in_sem.at[gi])

    def leaving(gi):
        rows = pl.ds(pl.multiple_of(2 * COPIES * gi, 2 * COPIES), 2 * COPIES)
        return pltpu.make_async_copy(code_buf.at[gi], out_ref.at[:, rows, :], out_sem.at[gi])

    for gi in range(OWN):
        arriving(gi).start()

    def tile_rows(a0):
        return pl.ds(pl.multiple_of(COPIES * a0, 64), COPIES * chunk)

    def raw_chunk(gi, a0):
        return raw_buf[gi, pl.ds(a0, chunk)].astype(f32)

    def shape(weights, signals):
        shaped = []
        for i in range(3):
            rows = slice(8 * i, 8 * i + 8)
            shaped.append(sum(weights[3 * i + j] * signals[j][:, rows] for j in range(3)))
        return shaped

    def pick(ref, k):
        return ref[pl.ds(k, BLOCKS, stride=COPIES), :]

    def to_lines(blocks, base):
        both = jnp.concatenate(blocks, axis=1)
        high, low = split(both)
        mid = dot(first_ref[...], jnp.concatenate([high, low, high], axis=0))
        out = []
        for j in range(2):
            real = mid[:LINES, ROWS * j : ROWS * (j + 1)]
            imag = mid[LINES:, ROWS * j : ROWS * (j + 1)]
            out.append(jnp.concatenate([real * cosine + imag * sine, imag * cosine - real * sine], axis=1))
        keep(jnp.concatenate(out, axis=0), base)

    def keep(values, base):
        high, low = split(values)
        spec_high[base : base + 2 * LINES, :] = high
        spec_low[base : base + 2 * LINES, :] = low

    def over_rows(matrix, begin, count):
        rows = slice(LINES * begin, LINES * (begin + count))
        high = spec_high[rows, :]
        return dot(jnp.concatenate([high, spec_low[rows, :], high], axis=1), matrix[...])

    def from_lines(values):
        pieces = []
        for j in range(2):
            real = values[LINES * j : LINES * (j + 1), :ROWS]
            imag = values[LINES * j : LINES * (j + 1), ROWS:]
            pieces.append(jnp.concatenate([real * cosine - imag * sine, imag * cosine + real * sine], axis=0))
        high, low = split(jnp.concatenate(pieces, axis=1))
        both = dot(last_ref[...], jnp.concatenate([high, low, high], axis=0))
        return both[:, :ROWS], both[:, ROWS:]

    def main(gi, _):
        weights = [weight_ref[gi, i] for i in range(10)]
        arriving(gi).wait()

        def shape_step(step, carry):
            a0 = chunk * step
            raw = raw_chunk(gi, a0)
            signal = raw[:, :24]
            one = pltpu.roll(signal, 1, 2)
            two = pltpu.roll(signal, 2, 2)
            one_before = jnp.concatenate([carry[0][None], one[:-1]], axis=0)
            two_before = jnp.concatenate([carry[1][None], two[:-1]], axis=0)
            delayed = (jnp.where(lane < 1, one_before, one), jnp.where(lane < 2, two_before, two))
            shift_one[pl.ds(a0, chunk)] = delayed[0]
            shift_two[pl.ds(a0, chunk)] = delayed[1]
            shaped = shape(weights, (signal,) + delayed)
            left[tile_rows(a0), :] = (shaped[1] * shaped[2]).reshape(COPIES * chunk, ROWS)
            right[tile_rows(a0), :] = (raw[:, 24:] * shaped[0]).reshape(COPIES * chunk, ROWS)
            return one[-1], two[-1]

        empty = jnp.zeros((24, ROWS), f32)
        lax.fori_loop(0, steps, shape_step, (empty, empty), unroll=8)

        for base, ref in ((0, left), (COPIES, right)):
            for k in range(0, COPIES, GANG):
                for j in range(k, k + GANG, 2):
                    to_lines([pick(ref, j), pick(ref, j + 1)], LINES * (base + j))
                lines[LINES * (base + k) : LINES * (base + k + GANG), :] = over_rows(forward_ref, base + k, GANG)

        filt_real, filt_imag = filt[gi, :, :ROWS], filt[gi, :, ROWS:]
        cross_real = jnp.zeros((LINES, ROWS), f32)
        cross_imag = jnp.zeros((LINES, ROWS), f32)
        for pair in range(COPIES // 2):
            forth, back = [], []
            for k in (2 * pair, 2 * pair + 1):
                here = slice(LINES * k, LINES * (k + 1))
                there = slice(LINES * (COPIES + k), LINES * (COPIES + k + 1))
                mix_real, mix_imag = lines[here, :ROWS], lines[here, ROWS:]
                grad_real, grad_imag = lines[there, :ROWS], lines[there, ROWS:]
                forth.append(
                    jnp.concatenate(
                        [mix_real * filt_real - mix_imag * filt_imag, mix_real * filt_imag + mix_imag * filt_real], axis=1
                    )
                )
                back.append(
                    jnp.concatenate(
                        [
                            grad_real * filt_real + grad_imag * filt_imag,
                            grad_imag * filt_real - grad_real * filt_imag,
                        ],
                        axis=1,
                    )
                )
                cross_real = cross_real + grad_real * mix_real + grad_imag * mix_imag
                cross_imag = cross_imag + grad_imag * mix_real - grad_real * mix_imag
            keep(jnp.concatenate(forth, axis=0), 2 * LINES * pair)
            keep(jnp.concatenate(back, axis=0), 2 * LINES * (COPIES // 2 + pair))
        cross[gi] = jnp.concatenate([cross_real, cross_imag], axis=1)
        for k in range(0, COPIES, GANG):
            for target, base in ((left, 0), (right, COPIES)):
                values = over_rows(inverse_ref, base + k, GANG)
                for j in range(0, GANG, 2):
                    pair = from_lines(values[LINES * j : LINES * (j + 2), :])
                    for i in range(2):
                        target[pl.ds(k + j + i, BLOCKS, stride=COPIES), :] = pair[i]

        def finish(step, sums):
            a0 = chunk * step
            rows = tile_rows(a0)
            raw = raw_chunk(gi, a0)
            upstream = raw[:, 24:]
            signals = (raw[:, :24], shift_one[pl.ds(a0, chunk)], shift_two[pl.ds(a0, chunk)])
            shaped = shape(weights, signals)
            mixer = shaped[1] * shaped[2]
            grad_conv = upstream * shaped[0]
            conv = left[rows, :].reshape(chunk, COPIES, ROWS) + weights[9] * mixer
            grad_mixer = right[rows, :].reshape(chunk, COPIES, ROWS) + weights[9] * grad_conv
            grads = (upstream * conv, grad_mixer * shaped[2], grad_mixer * shaped[1])
            new = []
            for i in range(3):
                for j in range(3):
                    new.append(sums[3 * i + j] + jnp.sum(grads[i] * signals[j][:, 8 * i : 8 * i + 8], axis=0))
            new.append(sums[9] + jnp.sum(grad_conv * mixer, axis=0))

            codes = []
            entry = jnp.zeros((COPIES, ROWS), f32)
            for slot, value in ((0, conv), (1, grad_mixer)):
                largest = jnp.max(jnp.max(jnp.abs(value), axis=0), axis=1, keepdims=True)
                scale = (jnp.maximum(largest, 1e-30) * (1.0 + 1.0 / 128.0)).astype(bf16).astype(f32)
                codes.append(encode(value, scale))
                entry = entry + jnp.where(flat == SCALE + slot, scale, 0.0)
            code_buf[gi, pl.ds(a0, chunk)] = jnp.concatenate(codes, axis=1)
            ahead = jnp.where(lane < 2, conv, jnp.where(lane < 4, pltpu.roll(grad_mixer, 2, 2), 0.0))
            ahead = pltpu.roll(ahead, 32 * gi, 2)
            extra[pl.ds(a0, chunk)] = extra[pl.ds(a0, chunk)] + ahead
            entry = pltpu.roll(entry, 32 * gi, 1)
            extra[pl.ds(a0 + 1, chunk)] = extra[pl.ds(a0 + 1, chunk)] + entry[None]
            return tuple(new)

        zero = jnp.zeros((COPIES, ROWS), f32)
        sums = lax.fori_loop(0, steps, finish, (zero,) * 10, unroll=8)

        total = zero
        for i in range(10):
            value = jnp.sum(sums[i], axis=1, keepdims=True) * (1.0 / math.sqrt(BLOCKS * ROWS))
            total = total + jnp.where(flat == TOTAL + i, value, 0.0)
        totals[gi] = pltpu.roll(total, 32 * gi, 1)
        leaving(gi).start()
        return 0

    def wrap_up():
        for f in range(0, OWN, 2):
            keep(cross[f : f + 2].reshape(2 * LINES, 2 * ROWS), LINES * f)
        temporal = over_rows(inverse_ref, 0, OWN)
        scale = 1.0 / math.sqrt(BLOCKS * ROWS * 2 * COPIES)
        for f in range(0, OWN, 2):
            both = from_lines(temporal[LINES * f : LINES * (f + 2)])
            for j in range(2):
                value = both[j] * scale
                for k in range(COPIES):
                    moved = pltpu.roll(value, (32 * (f + j) + FILTER - 16 * k) % ROWS, 1)
                    own.at[f + j][pl.ds(k, BLOCKS, stride=COPIES), :] = moved
        every = totals[0] + totals[1] + totals[2] + totals[3]

        def write(step, _):
            a0 = chunk * step
            value = extra[pl.ds(a0 + 1, chunk)] + every[None]
            for f in range(OWN):
                inside = (lane >= 32 * f + FILTER) & (lane < 32 * f + 32)
                value = jnp.where(inside, own[f, tile_rows(a0), :].reshape(chunk, COPIES, ROWS), value)
            high = value.astype(bf16).astype(f32)
            code_buf[OWN, pl.ds(a0, chunk)] = jnp.concatenate([high, value - high], axis=1).astype(bf16)
            return 0

        lax.fori_loop(0, steps, write, 0, unroll=2)

    def widen(a, _):
        taps[pl.ds(pl.multiple_of(2 * OWN * a, 2 * OWN), 2 * OWN), :] = taps_ref[a].astype(f32)
        return 0

    lax.fori_loop(0, BLOCKS, widen, 0, unroll=8)
    blocks = []
    for f in range(OWN):
        parts = [taps[pl.ds(OWN * part + f, BLOCKS, stride=2 * OWN), :] for part in range(2)]
        blocks.append(parts[0] + parts[1])
    for f in range(0, OWN, 2):
        to_lines(blocks[f : f + 2], LINES * f)
    filt[...] = over_rows(forward_ref, 0, OWN).reshape(OWN, LINES, 2 * ROWS)
    extra[...] = jnp.zeros_like(extra)
    lax.fori_loop(0, OWN, main, 0)
    wrap_up()
    leaving(OWN).start()
    for gi in range(OWN + 1):
        leaving(gi).wait()


def extras_kernel(in_ref, spread_ref, mine_ref, other_ref, ext_ref, wide):
    half = lax.axis_index("ch")

    def widen(d, _):
        wide[pl.ds(pl.multiple_of(16 * d, 16), 16), :] = in_ref[d].astype(f32)
        return 0

    lax.fori_loop(0, BLOCKS, widen, 0, unroll=8)
    for k in range(COPIES):
        total = jnp.zeros((32, GROUPS), f32)
        for part in range(2):
            turned = wide[pl.ds(8 * part + k, BLOCKS, stride=16), :].T.astype(bf16)
            for gi in range(OWN):
                total = total + dot(turned[32 * gi : 32 * gi + 32], spread_ref[gi])
        low, high = total[FILTER:, : GROUPS // 2], total[FILTER:, GROUPS // 2 :]
        mine_ref[16 * k : 16 * (k + 1), :] = jnp.where(half == 0, low, high)
        other_ref[16 * k : 16 * (k + 1), :] = jnp.where(half == 0, high, low)
        ext_ref[k] = total[:FILTER]


def finish_kernel(
    in_ref, feat_ref, cot_ref, before_ref, after_ref, weight_ref, ext_ref, mixed_ref, grad_ref, short_ref, skip_ref,
    codes, feat, cot, mixed, grad, wide, code_sem, feat_sem, cot_sem, mixed_sem, grad_sem,
):
    row = lax.broadcasted_iota(jnp.int32, (ROWS, 1), 0)
    share = BLOCKS // 4

    def code_copy(j):
        place = pl.ds(share * j, share)
        return pltpu.make_async_copy(in_ref.at[place, pl.ds(0, RESULT_ROWS), :], codes.at[place], code_sem.at[j])

    def lanes_of(k):
        return pl.ds(pl.multiple_of(GROUPS * k, GROUPS), GROUPS)

    def inputs(k):
        return (
            pltpu.make_async_copy(feat_ref.at[:, :, lanes_of(k)], feat.at[k], feat_sem.at[k]),
            pltpu.make_async_copy(cot_ref.at[:, lanes_of(k)], cot.at[k], cot_sem.at[k]),
        )

    def results(k):
        return (
            pltpu.make_async_copy(mixed.at[k], mixed_ref.at[:, lanes_of(k)], mixed_sem.at[k]),
            pltpu.make_async_copy(grad.at[k], grad_ref.at[:, :, lanes_of(k)], grad_sem.at[k]),
        )

    for j in range(4):
        code_copy(j).start()
    for k in range(COPIES):
        for copy in inputs(k):
            copy.start()
    for j in range(4):
        code_copy(j).wait()

        def widen(d, _):
            place = pl.ds(pl.multiple_of(RESULT_ROWS * d, RESULT_ROWS), RESULT_ROWS)
            wide[place, :] = codes[d].astype(f32)
            return 0

        lax.fori_loop(share * j, share * (j + 1), widen, 0, unroll=8)

    def one(k, _):
        lanes = lanes_of(k)
        for copy in inputs(k):
            copy.wait()
        for i in range(3):
            short_ref[i, :, lanes] = ext_ref[k, TOTAL + 3 * i : TOTAL + 3 * i + 3, :]
        skip_ref[:, lanes] = ext_ref[k, TOTAL + 9 : TOTAL + 10, :]
        signals = []
        for slot in range(2):
            code = wide[pl.ds(8 * slot + k, GROUPS, stride=16), :].T
            signals.append(decode(code, ext_ref[k, SCALE + slot : SCALE + slot + 1, :]))
        conv, grad_mixer = signals
        upstream = cot[k].astype(f32)
        shaped, shaped_after, weights = [], [], []
        for i in range(3):
            taps = [weight_ref[i, j : j + 1, lanes] for j in range(3)]
            weights.append(taps)
            value = feat[k, i].astype(f32)
            before = before_ref[i, :, lanes].astype(f32)
            after = after_ref[i, :, lanes].astype(f32)
            one = jnp.where(row == 0, before[1:2], pltpu.roll(value, 1, 0))
            two = jnp.where(row == 0, before[0:1], jnp.where(row == 1, before[1:2], pltpu.roll(value, 2, 0)))
            shaped.append(taps[0] * value + taps[1] * one + taps[2] * two)
            final, second = value[ROWS - 1 : ROWS], value[ROWS - 2 : ROWS - 1]
            shaped_after.append(
                (
                    taps[0] * after[0:1] + taps[1] * final + taps[2] * second,
                    taps[0] * after[1:2] + taps[1] * after[0:1] + taps[2] * final,
                )
            )
        mixed[k] = (shaped[0] * conv).astype(bf16)
        grads = (upstream * conv, grad_mixer * shaped[2], grad_mixer * shaped[1])
        upstream_after = after_ref[0, :, lanes].astype(f32)
        for i in range(3):
            slope = grads[i]
            following = []
            for t in range(2):
                conv_t = ext_ref[k, AFTER + t : AFTER + t + 1, :]
                mixer_t = ext_ref[k, AFTER + 2 + t : AFTER + 3 + t, :]
                if i == 0:
                    following.append(upstream_after[t : t + 1] * conv_t)
                else:
                    following.append(mixer_t * shaped_after[3 - i][t])
            one = jnp.where(row == ROWS - 1, following[0], pltpu.roll(slope, ROWS - 1, 0))
            two = jnp.where(
                row == ROWS - 1,
                following[1],
                jnp.where(row == ROWS - 2, following[0], pltpu.roll(slope, ROWS - 2, 0)),
            )
            grad[k, i] = weights[i][0] * slope + weights[i][1] * one + weights[i][2] * two
        for copy in results(k):
            copy.start()
        return 0

    lax.fori_loop(0, COPIES, one, 0)
    for k in range(COPIES):
        for copy in results(k):
            copy.wait()


def exchange(values):
    return lax.all_to_all(values, "ctx", split_axis=0, concat_axis=0, tiled=True)


def shift(block, distance):
    route = [(i, i + distance) for i in range(BLOCKS) if 0 <= i + distance < BLOCKS]
    return lax.ppermute(block, "ctx", route)


def pack(features, cotangent, long_filter):
    anywhere = pl.BlockSpec(memory_space=pl.ANY)
    return pl.pallas_call(
        pack_kernel,
        in_specs=[anywhere] * 3,
        out_specs=anywhere,
        out_shape=jax.ShapeDtypeStruct((BLOCKS, SEND_ROWS, ROWS), bf16),
        scratch_shapes=[
            pltpu.VMEM((COPIES, 3, ROWS, GROUPS), bf16),
            pltpu.VMEM((COPIES, ROWS, GROUPS), bf16),
            pltpu.VMEM((ROWS, GROUPS), f32),
            pltpu.VMEM((BLOCKS, SEND_ROWS, ROWS), bf16),
            pltpu.VMEM((4, COPIES * SPACING, ROWS), f32),
            pltpu.VMEM((2, GROUPS, ROWS), f32),
            pltpu.SemaphoreType.DMA((COPIES,)),
            pltpu.SemaphoreType.DMA((COPIES,)),
            pltpu.SemaphoreType.DMA,
            pltpu.SemaphoreType.DMA((4,)),
        ],
        compiler_params=LIMIT,
        name="pack",
    )(features, cotangent, long_filter)


def convolve(gathered, own):
    constants = tables()
    anywhere = pl.BlockSpec(memory_space=pl.ANY)
    whole = lambda array: pl.BlockSpec(array.shape, lambda i: (0,) * array.ndim)
    return pl.pallas_call(
        conv_kernel,
        grid=(1,),
        in_specs=[
            anywhere,
            pl.BlockSpec((BLOCKS, 2 * OWN, ROWS), lambda i: (0, SIGNAL_ROWS // (2 * OWN), 0)),
            whole(own),
        ]
        + [whole(array) for array in constants],
        out_specs=anywhere,
        out_shape=jax.ShapeDtypeStruct((BLOCKS, BACK_ROWS, ROWS), bf16),
        scratch_shapes=[
            pltpu.VMEM((OWN, BLOCKS, 4 * COPIES, ROWS), bf16),
            pltpu.VMEM((OWN + 1, BLOCKS, 2 * COPIES, ROWS), bf16),
            pltpu.SemaphoreType.DMA((OWN,)),
            pltpu.SemaphoreType.DMA((OWN + 1,)),
            pltpu.VMEM((COPIES * BLOCKS, ROWS), f32),
            pltpu.VMEM((COPIES * BLOCKS, ROWS), f32),
            pltpu.VMEM((BLOCKS, 24, ROWS), f32),
            pltpu.VMEM((BLOCKS, 24, ROWS), f32),
            pltpu.VMEM((2 * COPIES * LINES, 2 * ROWS), bf16),
            pltpu.VMEM((2 * COPIES * LINES, 2 * ROWS), bf16),
            pltpu.VMEM((2 * COPIES * LINES, 2 * ROWS), f32),
            pltpu.VMEM((OWN, LINES, 2 * ROWS), f32),
            pltpu.VMEM((OWN, LINES, 2 * ROWS), f32),
            pltpu.VMEM((BLOCKS + 1, COPIES, ROWS), f32),
            pltpu.VMEM((2 * OWN * BLOCKS, ROWS), f32),
            pltpu.VMEM((OWN, COPIES, ROWS), f32),
            pltpu.VMEM((OWN, COPIES * BLOCKS, ROWS), f32),
        ],
        compiler_params=LIMIT,
        name="conv",
    )(gathered, gathered, own, *constants)


def unpack_extras(home):
    spread = np.zeros((OWN, BLOCKS, GROUPS), ml_dtypes.bfloat16)
    for gi in range(OWN):
        spread[gi, np.arange(BLOCKS), OWN * np.arange(BLOCKS) + gi] = 1.0
    return pl.pallas_call(
        extras_kernel,
        grid=(1,),
        in_specs=[
            pl.BlockSpec((BLOCKS, 2 * COPIES, ROWS), lambda i: (0, RESULT_ROWS // (2 * COPIES), 0)),
            pl.BlockSpec((OWN, BLOCKS, GROUPS), lambda i: (0, 0, 0)),
        ],
        out_specs=[
            pl.BlockSpec((ROWS, GROUPS // 2), lambda i: (0, 0)),
            pl.BlockSpec((ROWS, GROUPS // 2), lambda i: (0, 0)),
            pl.BlockSpec((COPIES, FILTER, GROUPS), lambda i: (0, 0, 0)),
        ],
        out_shape=[
            jax.ShapeDtypeStruct((ROWS, GROUPS // 2), f32),
            jax.ShapeDtypeStruct((ROWS, GROUPS // 2), f32),
            jax.ShapeDtypeStruct((COPIES, FILTER, GROUPS), f32),
        ],
        scratch_shapes=[pltpu.VMEM((16 * BLOCKS, ROWS), f32)],
        compiler_params=LIMIT,
        name="extras",
    )(home, spread)


def finish(home, features, cotangent, before, after, short_weight, ext):
    breadth = features.shape[2]
    anywhere = pl.BlockSpec(memory_space=pl.ANY)
    whole = lambda *shape: pl.BlockSpec(shape, lambda i: (0,) * len(shape))
    return pl.pallas_call(
        finish_kernel,
        grid=(1,),
        in_specs=[anywhere] * 3 + [whole(*array.shape) for array in (before, after, short_weight, ext)],
        out_specs=[anywhere, anywhere, whole(3, 3, breadth), whole(1, breadth)],
        out_shape=[
            jax.ShapeDtypeStruct((ROWS, breadth), bf16),
            jax.ShapeDtypeStruct((3, ROWS, breadth), f32),
            jax.ShapeDtypeStruct((3, 3, breadth), f32),
            jax.ShapeDtypeStruct((1, breadth), f32),
        ],
        scratch_shapes=[
            pltpu.VMEM((BLOCKS, RESULT_ROWS, ROWS), bf16),
            pltpu.VMEM((COPIES, 3, ROWS, GROUPS), bf16),
            pltpu.VMEM((COPIES, ROWS, GROUPS), bf16),
            pltpu.VMEM((COPIES, ROWS, GROUPS), bf16),
            pltpu.VMEM((COPIES, 3, ROWS, GROUPS), f32),
            pltpu.VMEM((RESULT_ROWS * BLOCKS, ROWS), f32),
            pltpu.SemaphoreType.DMA((4,)),
        ]
        + [pltpu.SemaphoreType.DMA((COPIES,))] * 4,
        compiler_params=LIMIT,
        name="finish",
    )(home, features, cotangent, before, after, short_weight, ext)


def shards(features, short_weight, skip, long_filter, cotangent):
    rank = lax.axis_index("ctx")
    breadth = features.shape[2]

    gathered = exchange(pack(features, cotangent, long_filter))

    before = shift(features[:, ROWS - 2 :, :], 1)
    after = shift(jnp.concatenate([cotangent[None, :2], features[1:, :2]], axis=0), -1)

    weights = jnp.concatenate([short_weight.reshape(9, breadth), skip[None]], axis=0)
    own = lax.dynamic_index_in_dim(weights.reshape(10, COPIES, BLOCKS, OWN), rank, 2, keepdims=False)
    own = jnp.broadcast_to(jnp.transpose(own, (2, 0, 1))[..., None], (OWN, 10, COPIES, ROWS))

    gathered, own, before, after = lax.optimization_barrier((gathered, own, before, after))
    home = exchange(convolve(gathered, own))

    mine, other, ext = unpack_extras(home)
    arrived = lax.ppermute(other, "ch", [(0, 1), (1, 0)])
    mixed, feature_gradient, grad_short, grad_skip = finish(
        home, features, cotangent, before, after, short_weight, ext
    )
    return (mixed, feature_gradient, grad_short, grad_skip.reshape(breadth), mine + arrived)


def solution(mesh):
    return jax.shard_map(
        shards,
        mesh=mesh,
        in_specs=(
            P(None, "ctx", "ch"),
            P(None, None, "ch"),
            P("ch"),
            P("ctx", None),
            P("ctx", "ch"),
        ),
        out_specs=(
            P("ctx", "ch"),
            P(None, "ctx", "ch"),
            P(None, None, "ch"),
            P("ch"),
            P("ctx", "ch"),
        ),
        check_vma=False,
    )
```

time: 1260 us -> 106 us (0.08)
  waiting for transfers between devices: 631 us -> 16.4 us
  local copies, waits for them, and re-layouts: 182 us -> 8.31 us
  blocking collectives: 149 us -> 25.8 us
  matrix products: 102 us -> 0 us
  starting transfers between devices: 113 us -> 19.1 us
  other arithmetic: 54.2 us -> 1.68 us
  Pallas kernels: 0 us -> 33.7 us
  between operations: 16.7 us -> 0.77 us
    psum x1 -> x0, waiting for transfers between devices: 467 us -> none  [shards(): total_taps, total_skip = lax.psum((tap_terms, skip_term), 'ctx')]
    all_to_all x12 -> x1, waiting for transfers between devices: 164 us -> 3.2 us  [exchange(): lax.all_to_all(values, 'ctx', split_axis=0, concat_axis=0, tiled=True)]
    psum x1 -> x0, blocking collectives: 149 us -> none  [shards(): total_taps, total_skip = lax.psum((tap_terms, skip_term), 'ctx')]
    dot_general x36 -> x0, matrix products: 102 us -> none  [the longest x3 12.9 us: to_spectrum(): real_part = jnp.einsum('pk,prc->rkc', cos_blk, columns, precision=exact)]
    all_to_all x12 -> x1, starting transfers between devices: 106 us -> 11 us  [exchange(): lax.all_to_all(values, 'ctx', split_axis=0, concat_axis=0, tiled=True)]
    all_to_all x12 -> x0, local copies, waits for them, and re-layouts: 58.4 us -> none  [regroup(): lax.all_to_all(values, 'ctx', split_axis=1, concat_axis=0, tiled=True)]
    another operation x13 -> x0, local copies, waits for them, and re-layouts: 55.4 us -> none  [the longest x3 22 us: from_spectrum(): jnp.stack([real_mid * cos_tw - imag_mid * sin_tw, imag_mid * cos_tw + rea...]
    pallas_call x0 -> x4, Pallas kernels: none -> 33.7 us  [the longest x1 17.7 us: convolve(): pl.pallas_call(conv_kernel, grid=(1,), in_specs=[anywhere, pl.BlockSpec((...]
  transfers between devices with their start and end apart: 16 -> 4, of which waited for: 7 -> 3; matrix products, arithmetic and copies ran while one was open for 17% -> 7% of each run, Pallas kernels for 0% -> 9%
where the time goes in v2:
time: 106 us
  Pallas kernels  33.7 us (32%)
  blocking collectives  25.8 us (24%)
  starting transfers between devices  19.1 us (18%)
  waiting for transfers between devices  16.4 us (15%)
  local copies, waits for them, and re-layouts  8.31 us (8%)
  other arithmetic  1.68 us (2%)
    all_to_all x1, blocking collectives, exchange(): lax.all_to_all(values, 'ctx', split_axis=0, concat_axis=0, tiled=True)  25.8 us
    pallas_call x1, Pallas kernels, convolve(): pl.pallas_call(conv_kernel, grid=(1,), in_specs=[anywhere, pl.BlockSpec((...  17.7 us
    ppermute x2, waiting for transfers between devices, shift(): return lax.ppermute(block, 'ctx', route)  13.2 us
    all_to_all x1, starting transfers between devices, exchange(): lax.all_to_all(values, 'ctx', split_axis=0, concat_axis=0, tiled=True)  11 us
    pallas_call x1, Pallas kernels, finish(): pl.pallas_call(finish_kernel, grid=(1,), in_specs=[anywhere] * 3 + [whole...  9.25 us
    ppermute x2, starting transfers between devices, shift(): return lax.ppermute(block, 'ctx', route)  5.46 us
    pallas_call x1, Pallas kernels, pack(): pl.pallas_call(pack_kernel, in_specs=[anywhere] * 3, out_specs=anywhere,...  4.47 us
    concatenate x2, local copies, waits for them, and re-layouts, shards(): jnp.concatenate([short_weight.reshape(9, breadth), skip[None]], axis=0)  4.16 us
  transfers between devices with their start and end apart: 4, of which 3 were waited for; matrix products, arithmetic and copies ran while one was open for 7% of the time, Pallas kernels for 9%

profile of v2, /device:TPU:1, one launch (start us, length us, event | category | flops | bytes accessed | tf_op | source)
XLA Modules:
  0.0 105.7 jit_solution(3959487892342658868)
XLA Ops:
  0.6 4.5 %pack.1 = bf16[64,136,128]{2,1,0:T(8,128)(2,1)} custom-call(bf16[3,128,2048]{2,1,0:T(8,128)(2,1)} %feat_ref.3, bf16[128,2048]{1,0:T(8,128)(2,1)} %cot_ref.3, f32[128,256]{1,0:T(8,128)} %filt_ref.1), custom_call_target="tpu_custom_call" | custom-call | tf_op jit(solution)/shard_map/pack/pallas_call | solution.py:506
  5.1 0.0 copy-start.5
  5.1 0.0 copy-start.1
  5.1 11.0 %all-to-all-start = ((bf16[64,136,128]{2,1,0:T(8,128)(2,1)}), bf16[64,136,128]{2,1,0:T(8,128)(2,1)S(1)}, u32[]{:S(2)}, u32[]{:S(2)}) async-start(bf16[64,136,128]{2,1,0:T(8,128)(2,1)} %pack.1), calls=%async_computation | async-start | bytes 4456448 | tf_op jit(solution)/shard_map/all_to_all | solution.py:496
  16.1 0.9 slice.9
  17.1 3.5 %collective-permute-start = (bf16[3,2,2048]{2,1,0:T(2,128)(2,1)S(1)}, bf16[3,2,2048]{2,1,0:T(2,128)(2,1)S(1)}, u32[]{:S(2)}, u32[]{:S(2)}) collective-permute-start(bf16[3,2,2048]{2,1,0:T(2,128)(2,1)S(1)} %slice.9), channel_id=1, source_target_pairs={{0,2},{2,4},{4,6},{6,8},{8,10},{10,12},{12,14},{14,16},{16,18},{18... | collective-permute-start | bytes 73736 | tf_op jit(solution)/shard_map/ppermute | solution.py:501
  20.6 0.9 slice.11
  21.5 0.8 slice_bitcast_fusion
  22.3 1.9 %collective-permute-start.1 = (bf16[3,2,2048]{2,1,0:T(2,128)(2,1)S(1)}, bf16[3,2,2048]{2,1,0:T(2,128)(2,1)S(1)}, u32[]{:S(2)}, u32[]{:S(2)}) collective-permute-start(bf16[3,2,2048]{2,1,0:T(2,128)(2,1)S(1)} %pad_maximum_fusion), channel_id=1, source_target_pairs={{2,0},{4,2},{6,4},{8,6},{10,8},{12,10},{14,12},{16,14},{18,16},{20... | collective-permute-start | bytes 73736 | tf_op jit(solution)/shard_map/ppermute | solution.py:501
  24.2 0.0 copy-done.5
  24.2 0.3 concatenate.12
  24.5 0.0 copy-done.1
  24.5 3.9 %concatenate.11 = f32[9,8,64,4]{3,2,1,0:T(8,128)} reshape(f32[3,3,2048]{2,1,0:T(4,128)S(1)} %copy-done.1) | data formatting | bytes 147456 | tf_op jit(solution)/shard_map/concatenate | solution.py:633
  28.4 1.0 fusion
  29.4 0.2 copy.25
  29.6 10.9 %collective-permute-done.before_ref = bf16[3,2,2048]{2,1,0:T(2,128)(2,1)S(1)} collective-permute-done((bf16[3,2,2048]{2,1,0:T(2,128)(2,1)S(1)}, bf16[3,2,2048]{2,1,0:T(2,128)(2,1)S(1)}, u32[]{:S(2)}, u32[]{:S(2)}) %collective-permute-start) | collective-permute-done | bytes 24608 | tf_op jit(solution)/shard_map/ppermute | solution.py:501
  40.4 0.0 copy-start.3
  40.4 2.3 %collective-permute-done.1.after_ref = bf16[3,2,2048]{2,1,0:T(2,128)(2,1)S(1)} collective-permute-done((bf16[3,2,2048]{2,1,0:T(2,128)(2,1)S(1)}, bf16[3,2,2048]{2,1,0:T(2,128)(2,1)S(1)}, u32[]{:S(2)}, u32[]{:S(2)}) %collective-permute-start.1) | collective-permute-done | bytes 24608 | tf_op jit(solution)/shard_map/ppermute | solution.py:501
  42.7 0.0 copy-start.4
  42.7 3.2 %all-to-all-done.in_ref.taps_ref = bf16[64,136,128]{2,1,0:T(8,128)(2,1)S(1)} async-done(((bf16[64,136,128]{2,1,0:T(8,128)(2,1)}), bf16[64,136,128]{2,1,0:T(8,128)(2,1)S(1)}, u32[]{:S(2)}, u32[]{:S(2)}) %all-to-all-start) | async-done | bytes 2228256 | tf_op jit(solution)/shard_map/all_to_all | solution.py:496
  46.0 0.9 broadcast_in_dim.4.weight_ref
  46.9 0.5 copy-done
  47.4 17.7 %conv.1 = bf16[64,80,128]{2,1,0:T(8,128)(2,1)} custom-call(bf16[64,136,128]{2,1,0:T(8,128)(2,1)} %copy-done, bf16[64,136,128]{2,1,0:T(8,128)(2,1)} %copy-done, f32[4,10,8,128]{3,2,1,0:T(8,128)} %broadcast_in_dim.4.weight_ref, bf16[144,192]{1,0:T(8,128)(2,1)} %constant.24.clone.first_ref, bf16[64,432]{1,0:T(8,128)(2,1)} %constant.25.clone.last_ref, ...), custom_call_target="tpu_custom_call" | custom-call | tf_op jit(solution)/shard_map/conv/pallas_call | solution.py:532
  65.1 0.0 copy-done.3
  65.1 0.0 copy-done.4
  65.1 25.8 %all_to_all.10.in_ref = bf16[64,80,128]{2,1,0:T(8,128)(2,1)} all-to-all(bf16[64,80,128]{2,1,0:T(8,128)(2,1)} %conv.1), channel_id=1, replica_groups=mesh['ctx'=64,'ch'=2] {'ctx'}, dimensions={0} | all-to-all | bytes 2621440 | tf_op jit(solution)/shard_map/all_to_all | solution.py:496
  90.9 2.2 %extras.1 = (f32[128,128]{1,0:T(8,128)}, f32[128,128]{1,0:T(8,128)}, f32[8,16,256]{2,1,0:T(8,128)}) custom-call(bf16[64,80,128]{2,1,0:T(8,128)(2,1)} %all_to_all.10.in_ref, bf16[4,64,256]{2,1,0:T(8,128)(2,1)} %constant.29.clone.spread_ref), custom_call_target="tpu_custom_call" | custom-call | tf_op jit(solution)/shard_map/extras/pallas_call | solution.py:571
  93.2 2.6 %collective-permute-start.2 = (f32[128,128]{1,0:T(8,128)}, f32[128,128]{1,0:T(8,128)S(1)}, u32[]{:S(2)}, u32[]{:S(2)}) collective-permute-start(f32[128,128]{1,0:T(8,128)} %get-tuple-element.26), channel_id=1, source_target_pairs={{0,1},{1,0},{2,3},{3,2},{4,5},{5,4},{6,7},{7,6},{8,9},{9,8},{10,11... | collective-permute-start | bytes 196616 | tf_op jit(solution)/shard_map/ppermute | solution.py:641
  95.8 9.2 %finish.1 = (bf16[128,2048]{1,0:T(8,128)(2,1)}, f32[3,128,2048]{2,1,0:T(8,128)}, f32[3,3,2048]{2,1,0:T(4,128)}, f32[1,2048]{1,0:T(1,128)}) custom-call(bf16[64,80,128]{2,1,0:T(8,128)(2,1)} %all_to_all.10.in_ref, bf16[3,128,2048]{2,1,0:T(8,128)(2,1)} %feat_ref.3, bf16[128,2048]{1,0:T(8,128)(2,1)} %cot_ref.3, bf16[3,2,2048]{2,1,0:T(2,128)(2,1)} %copy-done.3, ...), custom_call_target="tpu_custom_call" | custom-call | tf_op jit(solution)/shard_map/finish/pallas_call | solution.py:598
  105.0 0.0 collective-permute-done.2
  105.1 0.0 copy-done.2
  105.1 0.6 add.8
  (3 shorter events, 0.0 us)
Async XLA Ops:
  5.1 19.1 %copy-start.5 = (f32[2048]{0:T(1024)S(1)}, f32[2048]{0:T(1024)}, u32[]{:S(2)}) copy-start(f32[2048]{0:T(1024)} %param.13) | copy-start | bytes 24580
  5.1 19.4 %copy-start.1 = (f32[3,3,2048]{2,1,0:T(4,128)S(1)}, f32[3,3,2048]{2,1,0:T(4,128)}, u32[]{:S(2)}) copy-start(f32[3,3,2048]{2,1,0:T(4,128)} %weight_ref.1) | copy-start | bytes 221188
  5.1 40.8 %all-to-all-start = ((bf16[64,136,128]{2,1,0:T(8,128)(2,1)}), bf16[64,136,128]{2,1,0:T(8,128)(2,1)S(1)}, u32[]{:S(2)}, u32[]{:S(2)}) async-start(bf16[64,136,128]{2,1,0:T(8,128)(2,1)} %pack.1), calls=%async_computation | async-start | bytes 4456448 | tf_op jit(solution)/shard_map/all_to_all | solution.py:496
  17.1 23.4 %collective-permute-start = (bf16[3,2,2048]{2,1,0:T(2,128)(2,1)S(1)}, bf16[3,2,2048]{2,1,0:T(2,128)(2,1)S(1)}, u32[]{:S(2)}, u32[]{:S(2)}) collective-permute-start(bf16[3,2,2048]{2,1,0:T(2,128)(2,1)S(1)} %slice.9), channel_id=1, source_target_pairs={{0,2},{2,4},{4,6},{6,8},{8,10},{10,12},{12,14},{14,16},{16,18},{18... | collective-permute-start | bytes 73736 | tf_op jit(solution)/shard_map/ppermute | solution.py:501
  22.3 20.5 %collective-permute-start.1 = (bf16[3,2,2048]{2,1,0:T(2,128)(2,1)S(1)}, bf16[3,2,2048]{2,1,0:T(2,128)(2,1)S(1)}, u32[]{:S(2)}, u32[]{:S(2)}) collective-permute-start(bf16[3,2,2048]{2,1,0:T(2,128)(2,1)S(1)} %pad_maximum_fusion), channel_id=1, source_target_pairs={{2,0},{4,2},{6,4},{8,6},{10,8},{12,10},{14,12},{16,14},{18,16},{20... | collective-permute-start | bytes 73736 | tf_op jit(solution)/shard_map/ppermute | solution.py:501
  40.4 24.7 %copy-start.3 = (bf16[3,2,2048]{2,1,0:T(2,128)(2,1)}, bf16[3,2,2048]{2,1,0:T(2,128)(2,1)S(1)}, u32[]{:S(2)}) copy-start(bf16[3,2,2048]{2,1,0:T(2,128)(2,1)S(1)} %collective-permute-done.before_ref) | copy-start | bytes 73732
  42.7 22.4 %copy-start.4 = (bf16[3,2,2048]{2,1,0:T(2,128)(2,1)}, bf16[3,2,2048]{2,1,0:T(2,128)(2,1)S(1)}, u32[]{:S(2)}) copy-start(bf16[3,2,2048]{2,1,0:T(2,128)(2,1)S(1)} %collective-permute-done.1.after_ref) | copy-start | bytes 73732
  45.9 1.4 %copy-start = (bf16[64,136,128]{2,1,0:T(8,128)(2,1)}, bf16[64,136,128]{2,1,0:T(8,128)(2,1)S(1)}, u32[]{:S(2)}) copy-start(bf16[64,136,128]{2,1,0:T(8,128)(2,1)S(1)} %all-to-all-done.in_ref.taps_ref) | copy-start | bytes 6684676
  93.2 11.9 %copy-start.2 = (f32[128,128]{1,0:T(8,128)S(1)}, f32[128,128]{1,0:T(8,128)}, u32[]{:S(2)}) copy-start(f32[128,128]{1,0:T(8,128)} %get-tuple-element.25) | copy-start | bytes 196612
  93.2 11.9 %collective-permute-start.2 = (f32[128,128]{1,0:T(8,128)}, f32[128,128]{1,0:T(8,128)S(1)}, u32[]{:S(2)}, u32[]{:S(2)}) collective-permute-start(f32[128,128]{1,0:T(8,128)} %get-tuple-element.26), channel_id=1, source_target_pairs={{0,1},{1,0},{2,3},{3,2},{4,5},{5,4},{6,7},{7,6},{8,9},{9,8},{10,11... | collective-permute-start | bytes 196616 | tf_op jit(solution)/shard_map/ppermute | solution.py:641

commit v3 on v2

--- a/solution.py
+++ b/solution.py
@@ -25,11 +25,12 @@
 RESULT_ROWS = OWN * 2 * COPIES
 BACK_ROWS = RESULT_ROWS + 2 * COPIES
 AFTER, SCALE, TOTAL, FILTER = 0, 4, 6, 16
-LEVELS = 32000.0
-BIAS = 124.0
+LEVELS = 250.0
+BIAS = 125.0
 GANG = 8
 SPACING = GROUPS + 1
-LIMIT = pltpu.CompilerParams(vmem_limit_bytes=56 * 2**20)
+LIMIT = pltpu.CompilerParams(vmem_limit_bytes=32 * 2**20)
+ROOMY = pltpu.CompilerParams(vmem_limit_bytes=60 * 2**20)
 
 
 def high_low(values):
@@ -56,17 +57,14 @@
     angle = 2.0 * np.pi * (b[:, None] * b[None, :] % ROWS) / ROWS
     cosine, sine = np.cos(angle), np.sin(angle)
     forward = np.block([[cosine, -sine], [sine, cosine]])
-    inverse = np.block([[cosine, sine], [-sine, cosine]])
     first_h, first_l = high_low(first)
     last_h, last_l = high_low(last)
     forward_h, forward_l = high_low(forward)
-    inverse_h, inverse_l = high_low(inverse)
     return (
         np.concatenate([first_h, first_h, first_l], axis=1),
         np.concatenate([last_h, last_h, last_l], axis=1),
         twiddle.astype(np.float32),
         np.concatenate([forward_h, forward_h, forward_l], axis=0),
-        np.concatenate([inverse_h, inverse_h, inverse_l], axis=0),
     )
 
 
@@ -80,18 +78,13 @@
 
 
 def encode(values, scale):
-    level = jnp.floor(jnp.abs(values) * (LEVELS / scale) + 0.5)
-    step = jnp.floor(level * (1.0 / 128.0))
-    part = 1.0 + (level - 128.0 * step) * (1.0 / 128.0)
-    code = jnp.exp2(step - BIAS) * part
+    code = jnp.exp2(jnp.abs(values) * (LEVELS / scale) - BIAS)
     return jnp.where(values < 0.0, -code, code).astype(bf16)
 
 
 def decode(code, scale):
-    size = jnp.abs(code)
-    step = jnp.floor(jnp.log(size) * (1.0 / math.log(2.0)) + 0.002)
-    level = 128.0 * (step + BIAS + (size * jnp.exp2(-step) - 1.0))
-    value = level * (scale * (1.0 / LEVELS))
+    step = scale * (1.0 / LEVELS)
+    value = jnp.log(jnp.abs(code)) * (step * (1.0 / math.log(2.0))) + step * BIAS
     return jnp.where(code < 0.0, -value, value)
 
 
@@ -147,9 +140,9 @@
 
 
 def conv_kernel(
-    in_ref, taps_ref, weight_ref, first_ref, last_ref, twiddle_ref, forward_ref, inverse_ref, out_ref,
+    in_ref, taps_ref, weight_ref, first_ref, last_ref, twiddle_ref, forward_ref, out_ref,
     raw_buf, code_buf, in_sem, out_sem,
-    left, right, shift_one, shift_two, spec_high, spec_low, lines, filt, cross, extra, taps, totals, own,
+    left, right, shift_one, shift_two, formed, spec_high, spec_low, lines, filt, cross, extra, taps, totals, own,
 ):
     chunk = 8
     steps = BLOCKS // chunk
@@ -168,11 +161,17 @@
     for gi in range(OWN):
         arriving(gi).start()
 
+    rank = lax.axis_index("ctx")
+    column = lax.broadcasted_iota(jnp.int32, (1, GROUPS), 1)
+    own_weights = []
+    for gi in range(OWN):
+        mine = column == OWN * rank + gi
+        own_weights.append(
+            [jnp.sum(jnp.where(mine, weight_ref[i], 0.0), axis=1, keepdims=True) for i in range(10)]
+        )
+
     def tile_rows(a0):
         return pl.ds(pl.multiple_of(COPIES * a0, 64), COPIES * chunk)
-
-    def raw_chunk(gi, a0):
-        return raw_buf[gi, pl.ds(a0, chunk)].astype(f32)
 
     def shape(weights, signals):
         shaped = []
@@ -200,49 +199,108 @@
         spec_high[base : base + 2 * LINES, :] = high
         spec_low[base : base + 2 * LINES, :] = low
 
-    def over_rows(matrix, begin, count):
+    def over_rows(begin, count):
         rows = slice(LINES * begin, LINES * (begin + count))
         high = spec_high[rows, :]
-        return dot(jnp.concatenate([high, spec_low[rows, :], high], axis=1), matrix[...])
+        return dot(jnp.concatenate([high, spec_low[rows, :], high], axis=1), forward_ref[...])
 
     def from_lines(values):
         pieces = []
         for j in range(2):
-            real = values[LINES * j : LINES * (j + 1), :ROWS]
-            imag = values[LINES * j : LINES * (j + 1), ROWS:]
+            imag = values[LINES * j : LINES * (j + 1), :ROWS]
+            real = values[LINES * j : LINES * (j + 1), ROWS:]
             pieces.append(jnp.concatenate([real * cosine - imag * sine, imag * cosine + real * sine], axis=0))
         high, low = split(jnp.concatenate(pieces, axis=1))
         both = dot(last_ref[...], jnp.concatenate([high, low, high], axis=0))
         return both[:, :ROWS], both[:, ROWS:]
 
-    def main(gi, _):
-        weights = [weight_ref[gi, i] for i in range(10)]
-        arriving(gi).wait()
-
-        def shape_step(step, carry):
-            a0 = chunk * step
-            raw = raw_chunk(gi, a0)
+    def spin(values, amount):
+        return pltpu.roll(values, amount, values.ndim - 1) if amount else values
+
+    def shape_steps(gi):
+        weights = own_weights[gi]
+        carry = [jnp.zeros((24, ROWS), f32)] * 2
+        mix, grad, ones, twos, forms = (ref.at[gi % 2] for ref in (left, right, shift_one, shift_two, formed))
+
+        def step(a0):
+            if a0 == 0:
+                arriving(gi).wait()
+            raw = raw_buf[gi, a0 : a0 + chunk].astype(f32)
             signal = raw[:, :24]
             one = pltpu.roll(signal, 1, 2)
             two = pltpu.roll(signal, 2, 2)
             one_before = jnp.concatenate([carry[0][None], one[:-1]], axis=0)
             two_before = jnp.concatenate([carry[1][None], two[:-1]], axis=0)
             delayed = (jnp.where(lane < 1, one_before, one), jnp.where(lane < 2, two_before, two))
-            shift_one[pl.ds(a0, chunk)] = delayed[0]
-            shift_two[pl.ds(a0, chunk)] = delayed[1]
+            ones[a0 : a0 + chunk] = delayed[0]
+            twos[a0 : a0 + chunk] = delayed[1]
             shaped = shape(weights, (signal,) + delayed)
-            left[tile_rows(a0), :] = (shaped[1] * shaped[2]).reshape(COPIES * chunk, ROWS)
-            right[tile_rows(a0), :] = (raw[:, 24:] * shaped[0]).reshape(COPIES * chunk, ROWS)
-            return one[-1], two[-1]
-
-        empty = jnp.zeros((24, ROWS), f32)
-        lax.fori_loop(0, steps, shape_step, (empty, empty), unroll=8)
-
-        for base, ref in ((0, left), (COPIES, right)):
+            forms[a0 : a0 + chunk] = jnp.concatenate(shaped, axis=1)
+            rows = slice(COPIES * a0, COPIES * (a0 + chunk))
+            mix[rows, :] = (shaped[1] * shaped[2]).reshape(COPIES * chunk, ROWS)
+            grad[rows, :] = (raw[:, 24:] * shaped[0]).reshape(COPIES * chunk, ROWS)
+            carry[:] = [one[-1], two[-1]]
+
+        return [functools.partial(step, a0) for a0 in range(0, BLOCKS, chunk)]
+
+    def finish_steps(gi):
+        weights = own_weights[gi]
+        sums = [jnp.zeros((COPIES, ROWS), f32)] * 10
+        last_entry = [jnp.zeros((COPIES, ROWS), f32)]
+        mix, grad, ones, twos, forms = (ref.at[gi % 2] for ref in (left, right, shift_one, shift_two, formed))
+
+        def step(a0):
+            rows = slice(COPIES * a0, COPIES * (a0 + chunk))
+            raw = raw_buf[gi, a0 : a0 + chunk].astype(f32)
+            upstream = raw[:, 24:]
+            signals = (raw[:, :24], ones[a0 : a0 + chunk], twos[a0 : a0 + chunk])
+            shaped = [forms[a0 : a0 + chunk, 8 * i : 8 * i + 8] for i in range(3)]
+            mixer = shaped[1] * shaped[2]
+            grad_conv = upstream * shaped[0]
+            conv = mix[rows, :].reshape(chunk, COPIES, ROWS) + weights[9] * mixer
+            grad_mixer = grad[rows, :].reshape(chunk, COPIES, ROWS) + weights[9] * grad_conv
+            grads = (upstream * conv, grad_mixer * shaped[2], grad_mixer * shaped[1])
+            for i in range(3):
+                for j in range(3):
+                    sums[3 * i + j] += jnp.sum(grads[i] * signals[j][:, 8 * i : 8 * i + 8], axis=0)
+            sums[9] += jnp.sum(grad_conv * mixer, axis=0)
+
+            codes = []
+            entry = jnp.zeros((COPIES, ROWS), f32)
+            for slot, value in ((0, conv), (1, grad_mixer)):
+                largest = jnp.max(jnp.max(jnp.abs(value), axis=0), axis=1, keepdims=True)
+                scale = (jnp.maximum(largest, 1e-30) * (1.0 + 1.0 / 128.0)).astype(bf16).astype(f32)
+                codes.append(encode(value, scale))
+                entry = entry + jnp.where(flat == 32 * gi + SCALE + slot, scale, 0.0)
+            code_buf[gi, a0 : a0 + chunk] = jnp.concatenate(codes, axis=1)
+            ahead = jnp.where(lane < 2, conv, jnp.where(lane < 4, pltpu.roll(grad_mixer, 2, 2), 0.0))
+            entries = [last_entry[0][None]] + [entry[None]] * (chunk - 1)
+            update = spin(ahead, 32 * gi) + jnp.concatenate(entries, axis=0)
+            extra[a0 : a0 + chunk] = update if gi == 0 else extra[a0 : a0 + chunk] + update
+            last_entry[0] = entry
+            if a0 + chunk == BLOCKS:
+                extra[BLOCKS] = entry if gi == 0 else extra[BLOCKS] + entry
+                leaving(gi).start()
+                total = jnp.zeros((COPIES, ROWS), f32)
+                for i in range(10):
+                    value = jnp.sum(sums[i], axis=1, keepdims=True) * (1.0 / math.sqrt(BLOCKS * ROWS))
+                    total = total + jnp.where(flat == 32 * gi + TOTAL + i, value, 0.0)
+                totals[gi] = total
+
+        return [functools.partial(step, a0) for a0 in range(0, BLOCKS, chunk)]
+
+    def take(steps):
+        if steps:
+            steps.pop(0)()
+
+    def main(gi, before, after):
+        mix, grad = left.at[gi % 2], right.at[gi % 2]
+        for base, ref in ((0, mix), (COPIES, grad)):
             for k in range(0, COPIES, GANG):
                 for j in range(k, k + GANG, 2):
                     to_lines([pick(ref, j), pick(ref, j + 1)], LINES * (base + j))
-                lines[LINES * (base + k) : LINES * (base + k + GANG), :] = over_rows(forward_ref, base + k, GANG)
+                    take(before)
+                lines[LINES * (base + k) : LINES * (base + k + GANG), :] = over_rows(base + k, GANG)
 
         filt_real, filt_imag = filt[gi, :, :ROWS], filt[gi, :, ROWS:]
         cross_real = jnp.zeros((LINES, ROWS), f32)
@@ -256,14 +314,14 @@
                 grad_real, grad_imag = lines[there, :ROWS], lines[there, ROWS:]
                 forth.append(
                     jnp.concatenate(
-                        [mix_real * filt_real - mix_imag * filt_imag, mix_real * filt_imag + mix_imag * filt_real], axis=1
+                        [mix_real * filt_imag + mix_imag * filt_real, mix_real * filt_real - mix_imag * filt_imag], axis=1
                     )
                 )
                 back.append(
                     jnp.concatenate(
                         [
+                            grad_imag * filt_real - grad_real * filt_imag,
                             grad_real * filt_real + grad_imag * filt_imag,
-                            grad_imag * filt_real - grad_real * filt_imag,
                         ],
                         axis=1,
                     )
@@ -272,63 +330,20 @@
                 cross_imag = cross_imag + grad_imag * mix_real - grad_real * mix_imag
             keep(jnp.concatenate(forth, axis=0), 2 * LINES * pair)
             keep(jnp.concatenate(back, axis=0), 2 * LINES * (COPIES // 2 + pair))
-        cross[gi] = jnp.concatenate([cross_real, cross_imag], axis=1)
+        cross[gi] = jnp.concatenate([cross_imag, cross_real], axis=1)
         for k in range(0, COPIES, GANG):
-            for target, base in ((left, 0), (right, COPIES)):
-                values = over_rows(inverse_ref, base + k, GANG)
+            for target, base in ((mix, 0), (grad, COPIES)):
+                values = over_rows(base + k, GANG)
                 for j in range(0, GANG, 2):
                     pair = from_lines(values[LINES * j : LINES * (j + 2), :])
                     for i in range(2):
                         target[pl.ds(k + j + i, BLOCKS, stride=COPIES), :] = pair[i]
-
-        def finish(step, sums):
-            a0 = chunk * step
-            rows = tile_rows(a0)
-            raw = raw_chunk(gi, a0)
-            upstream = raw[:, 24:]
-            signals = (raw[:, :24], shift_one[pl.ds(a0, chunk)], shift_two[pl.ds(a0, chunk)])
-            shaped = shape(weights, signals)
-            mixer = shaped[1] * shaped[2]
-            grad_conv = upstream * shaped[0]
-            conv = left[rows, :].reshape(chunk, COPIES, ROWS) + weights[9] * mixer
-            grad_mixer = right[rows, :].reshape(chunk, COPIES, ROWS) + weights[9] * grad_conv
-            grads = (upstream * conv, grad_mixer * shaped[2], grad_mixer * shaped[1])
-            new = []
-            for i in range(3):
-                for j in range(3):
-                    new.append(sums[3 * i + j] + jnp.sum(grads[i] * signals[j][:, 8 * i : 8 * i + 8], axis=0))
-            new.append(sums[9] + jnp.sum(grad_conv * mixer, axis=0))
-
-            codes = []
-            entry = jnp.zeros((COPIES, ROWS), f32)
-            for slot, value in ((0, conv), (1, grad_mixer)):
-                largest = jnp.max(jnp.max(jnp.abs(value), axis=0), axis=1, keepdims=True)
-                scale = (jnp.maximum(largest, 1e-30) * (1.0 + 1.0 / 128.0)).astype(bf16).astype(f32)
-                codes.append(encode(value, scale))
-                entry = entry + jnp.where(flat == SCALE + slot, scale, 0.0)
-            code_buf[gi, pl.ds(a0, chunk)] = jnp.concatenate(codes, axis=1)
-            ahead = jnp.where(lane < 2, conv, jnp.where(lane < 4, pltpu.roll(grad_mixer, 2, 2), 0.0))
-            ahead = pltpu.roll(ahead, 32 * gi, 2)
-            extra[pl.ds(a0, chunk)] = extra[pl.ds(a0, chunk)] + ahead
-            entry = pltpu.roll(entry, 32 * gi, 1)
-            extra[pl.ds(a0 + 1, chunk)] = extra[pl.ds(a0 + 1, chunk)] + entry[None]
-            return tuple(new)
-
-        zero = jnp.zeros((COPIES, ROWS), f32)
-        sums = lax.fori_loop(0, steps, finish, (zero,) * 10, unroll=8)
-
-        total = zero
-        for i in range(10):
-            value = jnp.sum(sums[i], axis=1, keepdims=True) * (1.0 / math.sqrt(BLOCKS * ROWS))
-            total = total + jnp.where(flat == TOTAL + i, value, 0.0)
-        totals[gi] = pltpu.roll(total, 32 * gi, 1)
-        leaving(gi).start()
-        return 0
-
-    def wrap_up():
+                    take(after)
+
+    def filter_gradient():
         for f in range(0, OWN, 2):
             keep(cross[f : f + 2].reshape(2 * LINES, 2 * ROWS), LINES * f)
-        temporal = over_rows(inverse_ref, 0, OWN)
+        temporal = over_rows(0, OWN)
         scale = 1.0 / math.sqrt(BLOCKS * ROWS * 2 * COPIES)
         for f in range(0, OWN, 2):
             both = from_lines(temporal[LINES * f : LINES * (f + 2)])
@@ -337,6 +352,8 @@
                 for k in range(COPIES):
                     moved = pltpu.roll(value, (32 * (f + j) + FILTER - 16 * k) % ROWS, 1)
                     own.at[f + j][pl.ds(k, BLOCKS, stride=COPIES), :] = moved
+
+    def wrap_up():
         every = totals[0] + totals[1] + totals[2] + totals[3]
 
         def write(step, _):
@@ -349,7 +366,7 @@
             code_buf[OWN, pl.ds(a0, chunk)] = jnp.concatenate([high, value - high], axis=1).astype(bf16)
             return 0
 
-        lax.fori_loop(0, steps, write, 0, unroll=2)
+        lax.fori_loop(0, steps, write, 0, unroll=4)
 
     def widen(a, _):
         taps[pl.ds(pl.multiple_of(2 * OWN * a, 2 * OWN), 2 * OWN), :] = taps_ref[a].astype(f32)
@@ -362,9 +379,17 @@
         blocks.append(parts[0] + parts[1])
     for f in range(0, OWN, 2):
         to_lines(blocks[f : f + 2], LINES * f)
-    filt[...] = over_rows(forward_ref, 0, OWN).reshape(OWN, LINES, 2 * ROWS)
-    extra[...] = jnp.zeros_like(extra)
-    lax.fori_loop(0, OWN, main, 0)
+    filt[...] = over_rows(0, OWN).reshape(OWN, LINES, 2 * ROWS)
+    for step in shape_steps(0):
+        step()
+    before = []
+    for gi in range(OWN):
+        after = shape_steps(gi + 1) if gi + 1 < OWN else []
+        main(gi, before, after)
+        before = finish_steps(gi)
+    filter_gradient()
+    for step in before:
+        step()
     wrap_up()
     leaving(OWN).start()
     for gi in range(OWN + 1):
@@ -379,23 +404,23 @@
         return 0
 
     lax.fori_loop(0, BLOCKS, widen, 0, unroll=8)
+    turned = [wide[pl.ds(n, BLOCKS, stride=16), :].T.astype(bf16) for n in range(2 * COPIES)]
+    total = jnp.zeros((2 * COPIES * 32, GROUPS), f32)
+    for gi in range(OWN):
+        rows = slice(32 * gi, 32 * gi + 32)
+        total = total + dot(jnp.concatenate([piece[rows] for piece in turned], axis=0), spread_ref[gi])
     for k in range(COPIES):
-        total = jnp.zeros((32, GROUPS), f32)
-        for part in range(2):
-            turned = wide[pl.ds(8 * part + k, BLOCKS, stride=16), :].T.astype(bf16)
-            for gi in range(OWN):
-                total = total + dot(turned[32 * gi : 32 * gi + 32], spread_ref[gi])
-        low, high = total[FILTER:, : GROUPS // 2], total[FILTER:, GROUPS // 2 :]
+        value = total[32 * k : 32 * k + 32] + total[32 * (COPIES + k) : 32 * (COPIES + k) + 32]
+        low, high = value[FILTER:, : GROUPS // 2], value[FILTER:, GROUPS // 2 :]
         mine_ref[16 * k : 16 * (k + 1), :] = jnp.where(half == 0, low, high)
         other_ref[16 * k : 16 * (k + 1), :] = jnp.where(half == 0, high, low)
-        ext_ref[k] = total[:FILTER]
+        ext_ref[k] = value[:FILTER]
 
 
 def finish_kernel(
     in_ref, feat_ref, cot_ref, before_ref, after_ref, weight_ref, ext_ref, mixed_ref, grad_ref, short_ref, skip_ref,
-    codes, feat, cot, mixed, grad, wide, code_sem, feat_sem, cot_sem, mixed_sem, grad_sem,
+    codes, feat, cot, mixed, grad, wide, turned, padded, slopes, code_sem, feat_sem, cot_sem, mixed_sem, grad_sem,
 ):
-    row = lax.broadcasted_iota(jnp.int32, (ROWS, 1), 0)
     share = BLOCKS // 4
 
     def code_copy(j):
@@ -439,49 +464,37 @@
         for i in range(3):
             short_ref[i, :, lanes] = ext_ref[k, TOTAL + 3 * i : TOTAL + 3 * i + 3, :]
         skip_ref[:, lanes] = ext_ref[k, TOTAL + 9 : TOTAL + 10, :]
-        signals = []
+        scales = [ext_ref[k, SCALE + slot : SCALE + slot + 1, :] for slot in range(2)]
         for slot in range(2):
-            code = wide[pl.ds(8 * slot + k, GROUPS, stride=16), :].T
-            signals.append(decode(code, ext_ref[k, SCALE + slot : SCALE + slot + 1, :]))
-        conv, grad_mixer = signals
-        upstream = cot[k].astype(f32)
-        shaped, shaped_after, weights = [], [], []
+            turned[slot] = wide[pl.ds(8 * slot + k, GROUPS, stride=16), :].T
+        taps = [[weight_ref[i, j : j + 1, lanes] for j in range(3)] for i in range(3)]
         for i in range(3):
-            taps = [weight_ref[i, j : j + 1, lanes] for j in range(3)]
-            weights.append(taps)
-            value = feat[k, i].astype(f32)
-            before = before_ref[i, :, lanes].astype(f32)
-            after = after_ref[i, :, lanes].astype(f32)
-            one = jnp.where(row == 0, before[1:2], pltpu.roll(value, 1, 0))
-            two = jnp.where(row == 0, before[0:1], jnp.where(row == 1, before[1:2], pltpu.roll(value, 2, 0)))
-            shaped.append(taps[0] * value + taps[1] * one + taps[2] * two)
-            final, second = value[ROWS - 1 : ROWS], value[ROWS - 2 : ROWS - 1]
-            shaped_after.append(
-                (
-                    taps[0] * after[0:1] + taps[1] * final + taps[2] * second,
-                    taps[0] * after[1:2] + taps[1] * after[0:1] + taps[2] * final,
+            padded[i, 6:8, :] = before_ref[i, :, lanes].astype(f32)
+            padded[i, 8 : 8 + ROWS, :] = feat[k, i].astype(f32)
+            padded[i, 8 + ROWS : 10 + ROWS, :] = after_ref[i, :, lanes].astype(f32)
+
+        def shape(i, begin, size):
+            return sum(taps[i][j] * padded[i, 8 + begin - j : 8 + begin - j + size, :] for j in range(3))
+
+        size = 16
+        for begin in range(0, ROWS, size):
+            rows = slice(begin, begin + size)
+            conv, grad_mixer = (decode(turned[slot, rows, :], scales[slot]) for slot in range(2))
+            upstream = cot[k, rows, :].astype(f32)
+            mixed[k, rows, :] = (shape(0, begin, size) * conv).astype(bf16)
+            slopes[0, rows, :] = upstream * conv
+            slopes[1, rows, :] = grad_mixer * shape(2, begin, size)
+            slopes[2, rows, :] = grad_mixer * shape(1, begin, size)
+        following = slice(ROWS, ROWS + 2)
+        grad_mixer = ext_ref[k, AFTER + 2 : AFTER + 4, :]
+        slopes[0, following, :] = padded[0, 8 + ROWS : 10 + ROWS, :] * ext_ref[k, AFTER : AFTER + 2, :]
+        slopes[1, following, :] = grad_mixer * shape(2, ROWS, 2)
+        slopes[2, following, :] = grad_mixer * shape(1, ROWS, 2)
+        for i in range(3):
+            for begin in range(0, ROWS, size):
+                grad[k, i, begin : begin + size, :] = sum(
+                    taps[i][j] * slopes[i, begin + j : begin + j + size, :] for j in range(3)
                 )
-            )
-        mixed[k] = (shaped[0] * conv).astype(bf16)
-        grads = (upstream * conv, grad_mixer * shaped[2], grad_mixer * shaped[1])
-        upstream_after = after_ref[0, :, lanes].astype(f32)
-        for i in range(3):
-            slope = grads[i]
-            following = []
-            for t in range(2):
-                conv_t = ext_ref[k, AFTER + t : AFTER + t + 1, :]
-                mixer_t = ext_ref[k, AFTER + 2 + t : AFTER + 3 + t, :]
-                if i == 0:
-                    following.append(upstream_after[t : t + 1] * conv_t)
-                else:
-                    following.append(mixer_t * shaped_after[3 - i][t])
-            one = jnp.where(row == ROWS - 1, following[0], pltpu.roll(slope, ROWS - 1, 0))
-            two = jnp.where(
-                row == ROWS - 1,
-                following[1],
-                jnp.where(row == ROWS - 2, following[0], pltpu.roll(slope, ROWS - 2, 0)),
-            )
-            grad[k, i] = weights[i][0] * slope + weights[i][1] * one + weights[i][2] * two
         for copy in results(k):
             copy.start()
         return 0
@@ -520,7 +533,7 @@
             pltpu.SemaphoreType.DMA,
             pltpu.SemaphoreType.DMA((4,)),
         ],
-        compiler_params=LIMIT,
+        compiler_params=ROOMY,
         name="pack",
     )(features, cotangent, long_filter)
 
@@ -545,10 +558,11 @@
             pltpu.VMEM((OWN + 1, BLOCKS, 2 * COPIES, ROWS), bf16),
             pltpu.SemaphoreType.DMA((OWN,)),
             pltpu.SemaphoreType.DMA((OWN + 1,)),
-            pltpu.VMEM((COPIES * BLOCKS, ROWS), f32),
-            pltpu.VMEM((COPIES * BLOCKS, ROWS), f32),
-            pltpu.VMEM((BLOCKS, 24, ROWS), f32),
-            pltpu.VMEM((BLOCKS, 24, ROWS), f32),
+            pltpu.VMEM((2, COPIES * BLOCKS, ROWS), f32),
+            pltpu.VMEM((2, COPIES * BLOCKS, ROWS), f32),
+            pltpu.VMEM((2, BLOCKS, 24, ROWS), f32),
+            pltpu.VMEM((2, BLOCKS, 24, ROWS), f32),
+            pltpu.VMEM((2, BLOCKS, 24, ROWS), f32),
             pltpu.VMEM((2 * COPIES * LINES, 2 * ROWS), bf16),
             pltpu.VMEM((2 * COPIES * LINES, 2 * ROWS), bf16),
             pltpu.VMEM((2 * COPIES * LINES, 2 * ROWS), f32),
@@ -613,6 +627,9 @@
             pltpu.VMEM((COPIES, ROWS, GROUPS), bf16),
             pltpu.VMEM((COPIES, 3, ROWS, GROUPS), f32),
             pltpu.VMEM((RESULT_ROWS * BLOCKS, ROWS), f32),
+            pltpu.VMEM((2, ROWS, GROUPS), f32),
+            pltpu.VMEM((3, ROWS + 16, GROUPS), f32),
+            pltpu.VMEM((3, ROWS + 8, GROUPS), f32),
             pltpu.SemaphoreType.DMA((4,)),
         ]
         + [pltpu.SemaphoreType.DMA((COPIES,))] * 4,
@@ -622,7 +639,6 @@
 
 
 def shards(features, short_weight, skip, long_filter, cotangent):
-    rank = lax.axis_index("ctx")
     breadth = features.shape[2]
 
     gathered = exchange(pack(features, cotangent, long_filter))
@@ -631,11 +647,10 @@
     after = shift(jnp.concatenate([cotangent[None, :2], features[1:, :2]], axis=0), -1)
 
     weights = jnp.concatenate([short_weight.reshape(9, breadth), skip[None]], axis=0)
-    own = lax.dynamic_index_in_dim(weights.reshape(10, COPIES, BLOCKS, OWN), rank, 2, keepdims=False)
-    own = jnp.broadcast_to(jnp.transpose(own, (2, 0, 1))[..., None], (OWN, 10, COPIES, ROWS))
-
-    gathered, own, before, after = lax.optimization_barrier((gathered, own, before, after))
-    home = exchange(convolve(gathered, own))
+    weights = weights.reshape(10, COPIES, GROUPS)
+
+    gathered, weights, before, after = lax.optimization_barrier((gathered, weights, before, after))
+    home = exchange(convolve(gathered, weights))
 
     mine, other, ext = unpack_extras(home)
     arrived = lax.ppermute(other, "ch", [(0, 1), (1, 0)])

time: 106 us -> 97.7 us (0.922)
  Pallas kernels: 33.7 us -> 26.4 us
  local copies, waits for them, and re-layouts: 8.31 us -> 3.14 us
  waiting for transfers between devices: 16.4 us -> 19.5 us
    pallas_call x1, Pallas kernels: 17.7 us -> 13.5 us  [convolve(): pl.pallas_call(conv_kernel, grid=(1,), in_specs=[anywhere, pl.BlockSpec((...]
    concatenate x2, local copies, waits for them, and re-layouts: 4.16 us -> 0.69 us  [shards(): jnp.concatenate([short_weight.reshape(9, breadth), skip[None]], axis=0)]
    ppermute x2, waiting for transfers between devices: 13.2 us -> 16.3 us  [shift(): return lax.ppermute(block, 'ctx', route)]
    pallas_call x1, Pallas kernels: 2.23 us -> 0.6 us  [unpack_extras(): pl.pallas_call(extras_kernel, grid=(1,), in_specs=[pl.BlockSpec((BLOCKS,...]
    pallas_call x1, Pallas kernels: 9.25 us -> 7.86 us  [finish(): pl.pallas_call(finish_kernel, grid=(1,), in_specs=[anywhere] * 3 + [whole...]
  transfers between devices with their start and end apart: 4 -> 4, of which waited for: 3 -> 3; matrix products, arithmetic and copies ran while one was open for 7% -> 5% of each run, Pallas kernels for 9% -> 8%
where the time goes in v3:
time: 97.7 us; the launch traced here: 97.2 us
  Pallas kernels  26.4 us (27%)
  blocking collectives  25.8 us (26%)
  waiting for transfers between devices  19.5 us (20%)
  starting transfers between devices  19.3 us (20%)
  local copies, waits for them, and re-layouts  3.14 us (3%)
  other arithmetic  2.17 us (2%)
    all_to_all x1, blocking collectives, exchange(): lax.all_to_all(values, 'ctx', split_axis=0, concat_axis=0, tiled=True)  25.8 us
    ppermute x2, waiting for transfers between devices, shift(): return lax.ppermute(block, 'ctx', route)  16.3 us
    pallas_call x1, Pallas kernels, convolve(): pl.pallas_call(conv_kernel, grid=(1,), in_specs=[anywhere, pl.BlockSpec((...  13.5 us
    all_to_all x1, starting transfers between devices, exchange(): lax.all_to_all(values, 'ctx', split_axis=0, concat_axis=0, tiled=True)  11 us
    pallas_call x1, Pallas kernels, finish(): pl.pallas_call(finish_kernel, grid=(1,), in_specs=[anywhere] * 3 + [whole...  7.86 us
    ppermute x2, starting transfers between devices, shift(): return lax.ppermute(block, 'ctx', route)  5.62 us
    pallas_call x1, Pallas kernels, pack(): pl.pallas_call(pack_kernel, in_specs=[anywhere] * 3, out_specs=anywhere,...  4.45 us
    all_to_all x1, waiting for transfers between devices, exchange(): lax.all_to_all(values, 'ctx', split_axis=0, concat_axis=0, tiled=True)  3.2 us
  transfers between devices with their start and end apart: 4, of which 3 were waited for; matrix products, arithmetic and copies ran while one was open for 5% of the time, Pallas kernels for 8%

profile of v3, /device:TPU:1, one launch (start us, length us, event | category | flops | bytes accessed | tf_op | source)
XLA Modules:
  0.0 97.2 jit_solution(15211920863711136564)
XLA Ops:
  0.6 4.5 %pack.1 = bf16[64,136,128]{2,1,0:T(8,128)(2,1)} custom-call(bf16[3,128,2048]{2,1,0:T(8,128)(2,1)} %feat_ref.3, bf16[128,2048]{1,0:T(8,128)(2,1)} %cot_ref.3, f32[128,256]{1,0:T(8,128)} %filt_ref.1), custom_call_target="tpu_custom_call" | custom-call | tf_op jit(solution)/shard_map/pack/pallas_call | solution.py:519
  5.1 0.0 copy-start.1
  5.1 0.0 copy-start.8
  5.1 0.0 copy-start.3
  5.1 0.0 copy-start.2
  5.1 0.0 copy-start.5
  5.2 0.0 copy-start.6
  5.2 0.0 copy-start.7
  5.2 11.0 %all-to-all-start = ((bf16[64,136,128]{2,1,0:T(8,128)(2,1)}), bf16[64,136,128]{2,1,0:T(8,128)(2,1)S(1)}, u32[]{:S(2)}, u32[]{:S(2)}) async-start(bf16[64,136,128]{2,1,0:T(8,128)(2,1)} %pack.1), calls=%async_computation | async-start | bytes 4456448 | tf_op jit(solution)/shard_map/all_to_all | solution.py:509
  16.2 1.5 %slice.9 = bf16[3,2,2048]{2,1,0:T(2,128)(2,1)} slice(bf16[3,128,2048]{2,1,0:T(8,128)(2,1)} %feat_ref.3), slice={[0:3], [126:128], [0:2048]} | slice | bytes 49152 | tf_op jit(solution)/shard_map/slice | solution.py:646
  17.7 3.5 %collective-permute-start = (bf16[3,2,2048]{2,1,0:T(2,128)(2,1)}, bf16[3,2,2048]{2,1,0:T(2,128)(2,1)}, u32[]{:S(2)}, u32[]{:S(2)}) collective-permute-start(bf16[3,2,2048]{2,1,0:T(2,128)(2,1)} %slice.9), channel_id=1, source_target_pairs={{0,2},{2,4},{4,6},{6,8},{8,10},{10,12},{12,14},{14,16},{16,18},{18... | collective-permute-start | bytes 73736 | tf_op jit(solution)/shard_map/ppermute | solution.py:514
  21.2 0.9 slice.11
  22.1 0.0 copy-done.1
  22.1 0.6 pad_maximum_fusion.1
  22.8 2.1 %collective-permute-start.1 = (bf16[3,2,2048]{2,1,0:T(2,128)(2,1)}, bf16[3,2,2048]{2,1,0:T(2,128)(2,1)}, u32[]{:S(2)}, u32[]{:S(2)}) collective-permute-start(bf16[3,2,2048]{2,1,0:T(2,128)(2,1)} %pad_maximum_fusion.1), channel_id=1, source_target_pairs={{2,0},{4,2},{6,4},{8,6},{10,8},{12,10},{14,12},{16,14},{18,16},{20... | collective-permute-start | bytes 73736 | tf_op jit(solution)/shard_map/ppermute | solution.py:514
  24.9 0.0 copy-done.8
  24.9 0.0 copy-done.3
  24.9 0.7 concatenate.11
  25.6 0.9 pad_maximum_fusion.weight_ref
  26.5 14.0 %collective-permute-done.before_ref = bf16[3,2,2048]{2,1,0:T(2,128)(2,1)} collective-permute-done((bf16[3,2,2048]{2,1,0:T(2,128)(2,1)}, bf16[3,2,2048]{2,1,0:T(2,128)(2,1)}, u32[]{:S(2)}, u32[]{:S(2)}) %collective-permute-start) | collective-permute-done | bytes 24608 | tf_op jit(solution)/shard_map/ppermute | solution.py:514
  40.5 2.3 %collective-permute-done.1.after_ref = bf16[3,2,2048]{2,1,0:T(2,128)(2,1)} collective-permute-done((bf16[3,2,2048]{2,1,0:T(2,128)(2,1)}, bf16[3,2,2048]{2,1,0:T(2,128)(2,1)}, u32[]{:S(2)}, u32[]{:S(2)}) %collective-permute-start.1) | collective-permute-done | bytes 24608 | tf_op jit(solution)/shard_map/ppermute | solution.py:514
  42.8 3.2 %all-to-all-done.in_ref.taps_ref = bf16[64,136,128]{2,1,0:T(8,128)(2,1)S(1)} async-done(((bf16[64,136,128]{2,1,0:T(8,128)(2,1)}), bf16[64,136,128]{2,1,0:T(8,128)(2,1)S(1)}, u32[]{:S(2)}, u32[]{:S(2)}) %all-to-all-start) | async-done | bytes 2228256 | tf_op jit(solution)/shard_map/all_to_all | solution.py:509
  46.0 0.0 copy-done.2
  46.0 13.5 %conv.1 = bf16[64,80,128]{2,1,0:T(8,128)(2,1)S(1)} custom-call(bf16[64,136,128]{2,1,0:T(8,128)(2,1)S(1)} %all-to-all-done.in_ref.taps_ref, bf16[64,136,128]{2,1,0:T(8,128)(2,1)S(1)} %all-to-all-done.in_ref.taps_ref, f32[10,8,256]{2,1,0:T(8,128)S(1)} %pad_maximum_fusion.weight_ref, bf16[144,192]{1,0:T(8,128)(2,1)S(1)} %copy-done.6, ...), custom_call_target="tpu_custom_call" | custom-call | tf_op jit(solution)/shard_map/conv/pallas_call | solution.py:545
  59.5 0.0 copy-start.4
  59.5 0.0 copy-start
  59.5 25.8 %all_to_all.10.in_ref = bf16[64,80,128]{2,1,0:T(8,128)(2,1)S(1)} all-to-all(bf16[64,80,128]{2,1,0:T(8,128)(2,1)S(1)} %conv.1), channel_id=1, replica_groups=mesh['ctx'=64,'ch'=2] {'ctx'}, dimensions={0} | all-to-all | bytes 2621440 | tf_op jit(solution)/shard_map/all_to_all | solution.py:509
  85.3 0.6 extras.1
  86.0 2.7 %collective-permute-start.2 = (f32[128,128]{1,0:T(8,128)S(1)}, f32[128,128]{1,0:T(8,128)S(1)}, u32[]{:S(2)}, u32[]{:S(2)}) collective-permute-start(f32[128,128]{1,0:T(8,128)S(1)} %get-tuple-element.26), channel_id=1, source_target_pairs={{0,1},{1,0},{2,3},{3,2},{4,5},{5,4},{6,7},{7,6},{8,9},{9,8},{10,11... | collective-permute-start | bytes 196616 | tf_op jit(solution)/shard_map/ppermute | solution.py:656
  88.7 7.9 %finish.1 = (bf16[128,2048]{1,0:T(8,128)(2,1)}, f32[3,128,2048]{2,1,0:T(8,128)}, f32[3,3,2048]{2,1,0:T(4,128)}, f32[1,2048]{1,0:T(1,128)}) custom-call(bf16[64,80,128]{2,1,0:T(8,128)(2,1)S(1)} %all_to_all.10.in_ref, bf16[3,128,2048]{2,1,0:T(8,128)(2,1)S(1)} %copy-done, bf16[128,2048]{1,0:T(8,128)(2,1)S(1)} %copy-done.1, ...), custom_call_target="tpu_custom_call" | custom-call | tf_op jit(solution)/shard_map/finish/pallas_call | solution.py:612
  96.5 0.0 collective-permute-done.2
  96.5 0.6 add.3
  (7 shorter events, 0.0 us)
Async XLA Ops:
  5.1 17.0 %copy-start.1 = (bf16[128,2048]{1,0:T(8,128)(2,1)S(1)}, bf16[128,2048]{1,0:T(8,128)(2,1)}, u32[]{:S(2)}) copy-start(bf16[128,2048]{1,0:T(8,128)(2,1)} %cot_ref.3) | copy-start | bytes 1572868
  5.1 19.8 %copy-start.8 = (f32[2048]{0:T(1024)S(1)}, f32[2048]{0:T(1024)}, u32[]{:S(2)}) copy-start(f32[2048]{0:T(1024)} %param.12) | copy-start | bytes 24580
  5.1 19.8 %copy-start.3 = (f32[3,3,2048]{2,1,0:T(4,128)S(1)}, f32[3,3,2048]{2,1,0:T(4,128)}, u32[]{:S(2)}) copy-start(f32[3,3,2048]{2,1,0:T(4,128)} %weight_ref.1) | copy-start | bytes 221188
  5.1 40.9 %copy-start.2 = (bf16[768,256]{1,0:T(8,128)(2,1)S(1)}, bf16[768,256]{1,0:T(8,128)(2,1)}, u32[]{:S(2)}) copy-start(bf16[768,256]{1,0:T(8,128)(2,1)} %constant.13.clone.forward_ref) | copy-start | bytes 1179652
  5.1 40.9 %copy-start.5 = (f32[2,72,128]{2,1,0:T(8,128)S(1)}, f32[2,72,128]{2,1,0:T(8,128)}, u32[]{:S(2)}) copy-start(f32[2,72,128]{2,1,0:T(8,128)} %constant.12.clone.twiddle_ref) | copy-start | bytes 221188
  5.2 40.8 %copy-start.6 = (bf16[144,192]{1,0:T(8,128)(2,1)S(1)}, bf16[144,192]{1,0:T(8,128)(2,1)}, u32[]{:S(2)}) copy-start(bf16[144,192]{1,0:T(8,128)(2,1)} %constant.10.clone.first_ref) | copy-start | bytes 165892
  5.2 40.8 %copy-start.7 = (bf16[64,432]{1,0:T(8,128)(2,1)S(1)}, bf16[64,432]{1,0:T(8,128)(2,1)}, u32[]{:S(2)}) copy-start(bf16[64,432]{1,0:T(8,128)(2,1)} %constant.11.clone.last_ref) | copy-start | bytes 165892
  5.2 40.8 %all-to-all-start = ((bf16[64,136,128]{2,1,0:T(8,128)(2,1)}), bf16[64,136,128]{2,1,0:T(8,128)(2,1)S(1)}, u32[]{:S(2)}, u32[]{:S(2)}) async-start(bf16[64,136,128]{2,1,0:T(8,128)(2,1)} %pack.1), calls=%async_computation | async-start | bytes 4456448 | tf_op jit(solution)/shard_map/all_to_all | solution.py:509
  17.7 22.8 %collective-permute-start = (bf16[3,2,2048]{2,1,0:T(2,128)(2,1)}, bf16[3,2,2048]{2,1,0:T(2,128)(2,1)}, u32[]{:S(2)}, u32[]{:S(2)}) collective-permute-start(bf16[3,2,2048]{2,1,0:T(2,128)(2,1)} %slice.9), channel_id=1, source_target_pairs={{0,2},{2,4},{4,6},{6,8},{8,10},{10,12},{12,14},{14,16},{16,18},{18... | collective-permute-start | bytes 73736 | tf_op jit(solution)/shard_map/ppermute | solution.py:514
  22.8 20.0 %collective-permute-start.1 = (bf16[3,2,2048]{2,1,0:T(2,128)(2,1)}, bf16[3,2,2048]{2,1,0:T(2,128)(2,1)}, u32[]{:S(2)}, u32[]{:S(2)}) collective-permute-start(bf16[3,2,2048]{2,1,0:T(2,128)(2,1)} %pad_maximum_fusion.1), channel_id=1, source_target_pairs={{2,0},{4,2},{6,4},{8,6},{10,8},{12,10},{14,12},{16,14},{18,16},{20... | collective-permute-start | bytes 73736 | tf_op jit(solution)/shard_map/ppermute | solution.py:514
  59.5 25.9 %copy-start.4 = (bf16[4,64,256]{2,1,0:T(8,128)(2,1)S(1)}, bf16[4,64,256]{2,1,0:T(8,128)(2,1)}, u32[]{:S(2)}) copy-start(bf16[4,64,256]{2,1,0:T(8,128)(2,1)} %constant.14.clone.spread_ref) | copy-start | bytes 393220
  59.5 29.2 %copy-start = (bf16[3,128,2048]{2,1,0:T(8,128)(2,1)S(1)}, bf16[3,128,2048]{2,1,0:T(8,128)(2,1)}, u32[]{:S(2)}) copy-start(bf16[3,128,2048]{2,1,0:T(8,128)(2,1)} %feat_ref.3) | copy-start | bytes 4718596
  86.0 10.6 %collective-permute-start.2 = (f32[128,128]{1,0:T(8,128)S(1)}, f32[128,128]{1,0:T(8,128)S(1)}, u32[]{:S(2)}, u32[]{:S(2)}) collective-permute-start(f32[128,128]{1,0:T(8,128)S(1)} %get-tuple-element.26), channel_id=1, source_target_pairs={{0,1},{1,0},{2,3},{3,2},{4,5},{5,4},{6,7},{7,6},{8,9},{9,8},{10,11... | collective-permute-start | bytes 196616 | tf_op jit(solution)/shard_map/ppermute | solution.py:656

commit v4 on v3

--- a/solution.py
+++ b/solution.py
@@ -24,7 +24,8 @@
 SEND_ROWS = SIGNAL_ROWS + 2 * OWN
 RESULT_ROWS = OWN * 2 * COPIES
 BACK_ROWS = RESULT_ROWS + 2 * COPIES
-AFTER, SCALE, TOTAL, FILTER = 0, 4, 6, 16
+AFTER, TOTAL, SPLIT = 0, 6, 16
+BEFORE, SCALE, FILTER_SCALE = 16, 22, 24
 LEVELS = 250.0
 BIAS = 125.0
 GANG = 8
@@ -79,7 +80,11 @@
 
 def encode(values, scale):
     code = jnp.exp2(jnp.abs(values) * (LEVELS / scale) - BIAS)
-    return jnp.where(values < 0.0, -code, code).astype(bf16)
+    return jnp.where(values < 0.0, -code, code)
+
+
+def scale_of(largest):
+    return (jnp.maximum(largest, 1e-30) * (1.0 + 1.0 / 128.0)).astype(bf16).astype(f32)
 
 
 def decode(code, scale):
@@ -142,7 +147,7 @@
 def conv_kernel(
     in_ref, taps_ref, weight_ref, first_ref, last_ref, twiddle_ref, forward_ref, out_ref,
     raw_buf, code_buf, in_sem, out_sem,
-    left, right, shift_one, shift_two, formed, spec_high, spec_low, lines, filt, cross, extra, taps, totals, own,
+    left, right, shift_one, shift_two, formed, spec_high, spec_low, lines, filt, cross, extra, exact, taps, totals, own, own_scale,
 ):
     chunk = 8
     steps = BLOCKS // chunk
@@ -246,7 +251,6 @@
     def finish_steps(gi):
         weights = own_weights[gi]
         sums = [jnp.zeros((COPIES, ROWS), f32)] * 10
-        last_entry = [jnp.zeros((COPIES, ROWS), f32)]
         mix, grad, ones, twos, forms = (ref.at[gi % 2] for ref in (left, right, shift_one, shift_two, formed))
 
         def step(a0):
@@ -268,18 +272,22 @@
             codes = []
             entry = jnp.zeros((COPIES, ROWS), f32)
             for slot, value in ((0, conv), (1, grad_mixer)):
-                largest = jnp.max(jnp.max(jnp.abs(value), axis=0), axis=1, keepdims=True)
-                scale = (jnp.maximum(largest, 1e-30) * (1.0 + 1.0 / 128.0)).astype(bf16).astype(f32)
-                codes.append(encode(value, scale))
+                scale = scale_of(jnp.max(jnp.max(jnp.abs(value), axis=0), axis=1, keepdims=True))
+                codes.append(encode(value, scale).astype(bf16))
                 entry = entry + jnp.where(flat == 32 * gi + SCALE + slot, scale, 0.0)
             code_buf[gi, a0 : a0 + chunk] = jnp.concatenate(codes, axis=1)
-            ahead = jnp.where(lane < 2, conv, jnp.where(lane < 4, pltpu.roll(grad_mixer, 2, 2), 0.0))
-            entries = [last_entry[0][None]] + [entry[None]] * (chunk - 1)
-            update = spin(ahead, 32 * gi) + jnp.concatenate(entries, axis=0)
-            extra[a0 : a0 + chunk] = update if gi == 0 else extra[a0 : a0 + chunk] + update
-            last_entry[0] = entry
+            ahead = jnp.zeros((chunk, COPIES, ROWS), f32)
+            behind = jnp.broadcast_to(entry, (chunk, COPIES, ROWS))
+            for i in range(3):
+                place = 32 * gi + AFTER + 2 * i
+                ahead = jnp.where((lane >= place) & (lane < place + 2), spin(grads[i], place), ahead)
+                place = 32 * gi + BEFORE + 2 * i
+                moved = spin(signals[2][:, 8 * i : 8 * i + 8], place)
+                behind = jnp.where((lane >= place) & (lane < place + 2), moved, behind)
+            here = slice(a0, a0 + chunk)
+            extra[here] = ahead if gi == 0 else extra[here] + ahead
+            exact[here] = behind if gi == 0 else exact[here] + behind
             if a0 + chunk == BLOCKS:
-                extra[BLOCKS] = entry if gi == 0 else extra[BLOCKS] + entry
                 leaving(gi).start()
                 total = jnp.zeros((COPIES, ROWS), f32)
                 for i in range(10):
@@ -345,13 +353,23 @@
             keep(cross[f : f + 2].reshape(2 * LINES, 2 * ROWS), LINES * f)
         temporal = over_rows(0, OWN)
         scale = 1.0 / math.sqrt(BLOCKS * ROWS * 2 * COPIES)
+        values = []
         for f in range(0, OWN, 2):
-            both = from_lines(temporal[LINES * f : LINES * (f + 2)])
-            for j in range(2):
-                value = both[j] * scale
-                for k in range(COPIES):
-                    moved = pltpu.roll(value, (32 * (f + j) + FILTER - 16 * k) % ROWS, 1)
-                    own.at[f + j][pl.ds(k, BLOCKS, stride=COPIES), :] = moved
+            values.extend(from_lines(temporal[LINES * f : LINES * (f + 2)]))
+        codes = []
+        scales = jnp.zeros((BLOCKS, ROWS), f32)
+        for f in range(OWN):
+            value = values[f] * scale
+            size = scale_of(jnp.max(jnp.abs(value), axis=1, keepdims=True))
+            codes.append(encode(value, size))
+            scales = jnp.where(flat == 32 * f + FILTER_SCALE, size, scales)
+        for k in range(COPIES):
+            moved = jnp.zeros((BLOCKS, ROWS), f32)
+            for f in range(OWN):
+                inside = (flat >= 32 * f + SPLIT) & (flat < 32 * f + 32)
+                moved = jnp.where(inside, spin(codes[f], (32 * f + SPLIT - 16 * k) % ROWS), moved)
+            own[pl.ds(k, BLOCKS, stride=COPIES), :] = moved
+            own_scale[pl.ds(k, BLOCKS, stride=COPIES), :] = scales
 
     def wrap_up():
         every = totals[0] + totals[1] + totals[2] + totals[3]
@@ -359,14 +377,14 @@
         def write(step, _):
             a0 = chunk * step
             value = extra[pl.ds(a0 + 1, chunk)] + every[None]
-            for f in range(OWN):
-                inside = (lane >= 32 * f + FILTER) & (lane < 32 * f + 32)
-                value = jnp.where(inside, own[f, tile_rows(a0), :].reshape(chunk, COPIES, ROWS), value)
             high = value.astype(bf16).astype(f32)
-            code_buf[OWN, pl.ds(a0, chunk)] = jnp.concatenate([high, value - high], axis=1).astype(bf16)
+            code = own[tile_rows(a0), :].reshape(chunk, COPIES, ROWS)
+            single = exact[pl.ds(a0, chunk)] + own_scale[tile_rows(a0), :].reshape(chunk, COPIES, ROWS)
+            both = [jnp.where(lane % 32 < SPLIT, high, code), jnp.where(lane % 32 < SPLIT, value - high, single)]
+            code_buf[OWN, pl.ds(a0, chunk)] = jnp.concatenate(both, axis=1).astype(bf16)
             return 0
 
-        lax.fori_loop(0, steps, write, 0, unroll=4)
+        lax.fori_loop(0, steps, write, 0, unroll=8)
 
     def widen(a, _):
         taps[pl.ds(pl.multiple_of(2 * OWN * a, 2 * OWN), 2 * OWN), :] = taps_ref[a].astype(f32)
@@ -380,6 +398,7 @@
     for f in range(0, OWN, 2):
         to_lines(blocks[f : f + 2], LINES * f)
     filt[...] = over_rows(0, OWN).reshape(OWN, LINES, 2 * ROWS)
+    extra[BLOCKS] = jnp.zeros((COPIES, ROWS), f32)
     for step in shape_steps(0):
         step()
     before = []
@@ -410,16 +429,28 @@
         rows = slice(32 * gi, 32 * gi + 32)
         total = total + dot(jnp.concatenate([piece[rows] for piece in turned], axis=0), spread_ref[gi])
     for k in range(COPIES):
-        value = total[32 * k : 32 * k + 32] + total[32 * (COPIES + k) : 32 * (COPIES + k) + 32]
-        low, high = value[FILTER:, : GROUPS // 2], value[FILTER:, GROUPS // 2 :]
+        first = total[32 * k : 32 * k + 32]
+        second = total[32 * (COPIES + k) : 32 * (COPIES + k) + 32]
+        value = decode(first[SPLIT:], second[FILTER_SCALE : FILTER_SCALE + 1])
+        low, high = value[:, : GROUPS // 2], value[:, GROUPS // 2 :]
         mine_ref[16 * k : 16 * (k + 1), :] = jnp.where(half == 0, low, high)
         other_ref[16 * k : 16 * (k + 1), :] = jnp.where(half == 0, high, low)
-        ext_ref[k] = value[:FILTER]
+        ext_ref[k, :SPLIT, :] = first[:SPLIT] + second[:SPLIT]
+        ext_ref[k, SPLIT:, :] = second[SPLIT:]
+
+
+def prepare_kernel(feat_ref, weight_ref, out_ref):
+    row = lax.broadcasted_iota(jnp.int32, (ROWS, 1), 0)
+    for i in range(3):
+        value = feat_ref[i].astype(f32)
+        one = jnp.where(row < 1, 0.0, pltpu.roll(value, 1, 0))
+        two = jnp.where(row < 2, 0.0, pltpu.roll(value, 2, 0))
+        out_ref[i] = weight_ref[i, 0:1, :] * value + weight_ref[i, 1:2, :] * one + weight_ref[i, 2:3, :] * two
 
 
 def finish_kernel(
-    in_ref, feat_ref, cot_ref, before_ref, after_ref, weight_ref, ext_ref, mixed_ref, grad_ref, short_ref, skip_ref,
-    codes, feat, cot, mixed, grad, wide, turned, padded, slopes, code_sem, feat_sem, cot_sem, mixed_sem, grad_sem,
+    in_ref, shaped_ref, cot_ref, weight_ref, ext_ref, mixed_ref, grad_ref, short_ref, skip_ref,
+    codes, shaped, cot, mixed, grad, wide, turned, code_sem, shaped_sem, cot_sem, mixed_sem, grad_sem,
 ):
     share = BLOCKS // 4
 
@@ -432,7 +463,7 @@
 
     def inputs(k):
         return (
-            pltpu.make_async_copy(feat_ref.at[:, :, lanes_of(k)], feat.at[k], feat_sem.at[k]),
+            pltpu.make_async_copy(shaped_ref.at[:, :, lanes_of(k)], shaped.at[k], shaped_sem.at[k]),
             pltpu.make_async_copy(cot_ref.at[:, lanes_of(k)], cot.at[k], cot_sem.at[k]),
         )
 
@@ -456,6 +487,9 @@
             return 0
 
         lax.fori_loop(share * j, share * (j + 1), widen, 0, unroll=8)
+
+    size = 16
+    row = lax.broadcasted_iota(jnp.int32, (size, 1), 0)
 
     def one(k, _):
         lanes = lanes_of(k)
@@ -468,33 +502,29 @@
         for slot in range(2):
             turned[slot] = wide[pl.ds(8 * slot + k, GROUPS, stride=16), :].T
         taps = [[weight_ref[i, j : j + 1, lanes] for j in range(3)] for i in range(3)]
+
+        following = [ext_ref[k, AFTER + 2 * i : AFTER + 2 * i + 2, :] for i in range(3)]
+        lead = []
         for i in range(3):
-            padded[i, 6:8, :] = before_ref[i, :, lanes].astype(f32)
-            padded[i, 8 : 8 + ROWS, :] = feat[k, i].astype(f32)
-            padded[i, 8 + ROWS : 10 + ROWS, :] = after_ref[i, :, lanes].astype(f32)
-
-        def shape(i, begin, size):
-            return sum(taps[i][j] * padded[i, 8 + begin - j : 8 + begin - j + size, :] for j in range(3))
-
-        size = 16
-        for begin in range(0, ROWS, size):
+            second, final = (ext_ref[k, BEFORE + 2 * i + j : BEFORE + 2 * i + j + 1, :] for j in range(2))
+            lead.append((taps[i][1] * final + taps[i][2] * second, taps[i][2] * final))
+        for begin in reversed(range(0, ROWS, size)):
             rows = slice(begin, begin + size)
             conv, grad_mixer = (decode(turned[slot, rows, :], scales[slot]) for slot in range(2))
-            upstream = cot[k, rows, :].astype(f32)
-            mixed[k, rows, :] = (shape(0, begin, size) * conv).astype(bf16)
-            slopes[0, rows, :] = upstream * conv
-            slopes[1, rows, :] = grad_mixer * shape(2, begin, size)
-            slopes[2, rows, :] = grad_mixer * shape(1, begin, size)
-        following = slice(ROWS, ROWS + 2)
-        grad_mixer = ext_ref[k, AFTER + 2 : AFTER + 4, :]
-        slopes[0, following, :] = padded[0, 8 + ROWS : 10 + ROWS, :] * ext_ref[k, AFTER : AFTER + 2, :]
-        slopes[1, following, :] = grad_mixer * shape(2, ROWS, 2)
-        slopes[2, following, :] = grad_mixer * shape(1, ROWS, 2)
-        for i in range(3):
-            for begin in range(0, ROWS, size):
-                grad[k, i, begin : begin + size, :] = sum(
-                    taps[i][j] * slopes[i, begin + j : begin + j + size, :] for j in range(3)
-                )
+            forms = [shaped[k, i, rows, :] for i in range(3)]
+            if begin == 0:
+                for i in range(3):
+                    forms[i] = forms[i] + jnp.where(row == 0, lead[i][0], jnp.where(row == 1, lead[i][1], 0.0))
+            query, key, value = forms
+            mixed[k, rows, :] = (query * conv).astype(bf16)
+            slopes = (cot[k, rows, :].astype(f32) * conv, grad_mixer * value, grad_mixer * key)
+            for i in range(3):
+                slope, after = slopes[i], following[i]
+                one = jnp.where(row == size - 1, after[0:1], pltpu.roll(slope, size - 1, 0))
+                two = jnp.where(row >= size - 2, pltpu.roll(one, size - 1, 0), pltpu.roll(slope, size - 2, 0))
+                two = jnp.where(row == size - 1, after[1:2], two)
+                grad[k, i, rows, :] = taps[i][0] * slope + taps[i][1] * one + taps[i][2] * two
+            following = [slope[:2] for slope in slopes]
         for copy in results(k):
             copy.start()
         return 0
@@ -507,11 +537,6 @@
 
 def exchange(values):
     return lax.all_to_all(values, "ctx", split_axis=0, concat_axis=0, tiled=True)
-
-
-def shift(block, distance):
-    route = [(i, i + distance) for i in range(BLOCKS) if 0 <= i + distance < BLOCKS]
-    return lax.ppermute(block, "ctx", route)
 
 
 def pack(features, cotangent, long_filter):
@@ -569,9 +594,11 @@
             pltpu.VMEM((OWN, LINES, 2 * ROWS), f32),
             pltpu.VMEM((OWN, LINES, 2 * ROWS), f32),
             pltpu.VMEM((BLOCKS + 1, COPIES, ROWS), f32),
+            pltpu.VMEM((BLOCKS, COPIES, ROWS), f32),
             pltpu.VMEM((2 * OWN * BLOCKS, ROWS), f32),
             pltpu.VMEM((OWN, COPIES, ROWS), f32),
-            pltpu.VMEM((OWN, COPIES * BLOCKS, ROWS), f32),
+            pltpu.VMEM((COPIES * BLOCKS, ROWS), f32),
+            pltpu.VMEM((COPIES * BLOCKS, ROWS), f32),
         ],
         compiler_params=LIMIT,
         name="conv",
@@ -592,12 +619,12 @@
         out_specs=[
             pl.BlockSpec((ROWS, GROUPS // 2), lambda i: (0, 0)),
             pl.BlockSpec((ROWS, GROUPS // 2), lambda i: (0, 0)),
-            pl.BlockSpec((COPIES, FILTER, GROUPS), lambda i: (0, 0, 0)),
+            pl.BlockSpec((COPIES, 32, GROUPS), lambda i: (0, 0, 0)),
         ],
         out_shape=[
             jax.ShapeDtypeStruct((ROWS, GROUPS // 2), f32),
             jax.ShapeDtypeStruct((ROWS, GROUPS // 2), f32),
-            jax.ShapeDtypeStruct((COPIES, FILTER, GROUPS), f32),
+            jax.ShapeDtypeStruct((COPIES, 32, GROUPS), f32),
         ],
         scratch_shapes=[pltpu.VMEM((16 * BLOCKS, ROWS), f32)],
         compiler_params=LIMIT,
@@ -605,14 +632,29 @@
     )(home, spread)
 
 
-def finish(home, features, cotangent, before, after, short_weight, ext):
+def prepare(features, short_weight):
     breadth = features.shape[2]
+    deep = lambda k: (0, 0, k)
+    width = 2 * GROUPS
+    return pl.pallas_call(
+        prepare_kernel,
+        grid=(breadth // width,),
+        in_specs=[pl.BlockSpec((3, ROWS, width), deep), pl.BlockSpec((3, 3, width), deep)],
+        out_specs=pl.BlockSpec((3, ROWS, width), deep),
+        out_shape=jax.ShapeDtypeStruct((3, ROWS, breadth), f32),
+        compiler_params=LIMIT,
+        name="prepare",
+    )(features, short_weight)
+
+
+def finish(home, shaped, cotangent, short_weight, ext):
+    breadth = shaped.shape[2]
     anywhere = pl.BlockSpec(memory_space=pl.ANY)
     whole = lambda *shape: pl.BlockSpec(shape, lambda i: (0,) * len(shape))
     return pl.pallas_call(
         finish_kernel,
         grid=(1,),
-        in_specs=[anywhere] * 3 + [whole(*array.shape) for array in (before, after, short_weight, ext)],
+        in_specs=[anywhere] * 3 + [whole(*array.shape) for array in (short_weight, ext)],
         out_specs=[anywhere, anywhere, whole(3, 3, breadth), whole(1, breadth)],
         out_shape=[
             jax.ShapeDtypeStruct((ROWS, breadth), bf16),
@@ -622,20 +664,18 @@
         ],
         scratch_shapes=[
             pltpu.VMEM((BLOCKS, RESULT_ROWS, ROWS), bf16),
-            pltpu.VMEM((COPIES, 3, ROWS, GROUPS), bf16),
+            pltpu.VMEM((COPIES, 3, ROWS, GROUPS), f32),
             pltpu.VMEM((COPIES, ROWS, GROUPS), bf16),
             pltpu.VMEM((COPIES, ROWS, GROUPS), bf16),
             pltpu.VMEM((COPIES, 3, ROWS, GROUPS), f32),
             pltpu.VMEM((RESULT_ROWS * BLOCKS, ROWS), f32),
             pltpu.VMEM((2, ROWS, GROUPS), f32),
-            pltpu.VMEM((3, ROWS + 16, GROUPS), f32),
-            pltpu.VMEM((3, ROWS + 8, GROUPS), f32),
             pltpu.SemaphoreType.DMA((4,)),
         ]
         + [pltpu.SemaphoreType.DMA((COPIES,))] * 4,
         compiler_params=LIMIT,
         name="finish",
-    )(home, features, cotangent, before, after, short_weight, ext)
+    )(home, shaped, cotangent, short_weight, ext)
 
 
 def shards(features, short_weight, skip, long_filter, cotangent):
@@ -643,20 +683,17 @@
 
     gathered = exchange(pack(features, cotangent, long_filter))
 
-    before = shift(features[:, ROWS - 2 :, :], 1)
-    after = shift(jnp.concatenate([cotangent[None, :2], features[1:, :2]], axis=0), -1)
-
     weights = jnp.concatenate([short_weight.reshape(9, breadth), skip[None]], axis=0)
     weights = weights.reshape(10, COPIES, GROUPS)
 
-    gathered, weights, before, after = lax.optimization_barrier((gathered, weights, before, after))
+    shaped = prepare(features, short_weight)
+
+    gathered, weights, shaped = lax.optimization_barrier((gathered, weights, shaped))
     home = exchange(convolve(gathered, weights))
 
     mine, other, ext = unpack_extras(home)
     arrived = lax.ppermute(other, "ch", [(0, 1), (1, 0)])
-    mixed, feature_gradient, grad_short, grad_skip = finish(
-        home, features, cotangent, before, after, short_weight, ext
-    )
+    mixed, feature_gradient, grad_short, grad_skip = finish(home, shaped, cotangent, short_weight, ext)
     return (mixed, feature_gradient, grad_short, grad_skip.reshape(breadth), mine + arrived)
 
 

time: 97.7 us -> 95 us (0.972)
  starting transfers between devices: 19.3 us -> 13.7 us
  waiting for transfers between devices: 19.5 us -> 24.9 us
  other arithmetic: 2.17 us -> 0.65 us
    all_to_all x1, waiting for transfers between devices: 3.2 us -> 24.9 us  [exchange(): lax.all_to_all(values, 'ctx', split_axis=0, concat_axis=0, tiled=True)]
    ppermute x2 -> x0, waiting for transfers between devices: 16.3 us -> none  [shift(): return lax.ppermute(block, 'ctx', route)]
    ppermute x2 -> x0, starting transfers between devices: 5.62 us -> none  [shift(): return lax.ppermute(block, 'ctx', route)]
    unnamed x18 -> x22, local copies, waits for them, and re-layouts: 0.06 us -> 3.11 us
    pallas_call x1, Pallas kernels: 7.86 us -> 5.37 us  [finish(): pl.pallas_call(finish_kernel, grid=(1,), in_specs=[anywhere] * 3 + [whole...]
    slice x2 -> x0, local copies, waits for them, and re-layouts: 2.39 us -> none  [the longest x1 1.53 us: shards(): before = shift(features[:, ROWS - 2:, :], 1)]
    pallas_call x0 -> x1, Pallas kernels: none -> 1.44 us  [prepare(): pl.pallas_call(prepare_kernel, grid=(breadth // width,), in_specs=[pl.Blo...]
  transfers between devices with their start and end apart: 4 -> 2, of which waited for: 3 -> 1; matrix products, arithmetic and copies ran while one was open for 5% -> 0% of each run, Pallas kernels for 8% -> 7%
where the time goes in v4:
time: 95 us; the launch traced here: 94.7 us
  blocking collectives  26 us (27%)
  Pallas kernels  25.5 us (27%)
  waiting for transfers between devices  24.9 us (26%)
  starting transfers between devices  13.7 us (14%)
  local copies, waits for them, and re-layouts  3.16 us (3%)
    all_to_all x1, blocking collectives, exchange(): lax.all_to_all(values, 'ctx', split_axis=0, concat_axis=0, tiled=True)  26 us
    all_to_all x1, waiting for transfers between devices, exchange(): lax.all_to_all(values, 'ctx', split_axis=0, concat_axis=0, tiled=True)  24.9 us
    pallas_call x1, Pallas kernels, convolve(): pl.pallas_call(conv_kernel, grid=(1,), in_specs=[anywhere, pl.BlockSpec((...  13.6 us
    all_to_all x1, starting transfers between devices, exchange(): lax.all_to_all(values, 'ctx', split_axis=0, concat_axis=0, tiled=True)  11 us
    pallas_call x1, Pallas kernels, finish(): pl.pallas_call(finish_kernel, grid=(1,), in_specs=[anywhere] * 3 + [whole...  5.37 us
    pallas_call x1, Pallas kernels, pack(): pl.pallas_call(pack_kernel, in_specs=[anywhere] * 3, out_specs=anywhere,...  4.46 us
    unnamed x22, local copies, waits for them, and re-layouts  3.11 us
    ppermute x1, starting transfers between devices, shards(): arrived = lax.ppermute(other, 'ch', [(0, 1), (1, 0)])  2.69 us
  transfers between devices with their start and end apart: 2, of which 1 were waited for; matrix products, arithmetic and copies ran while one was open for 0% of the time, Pallas kernels for 7%

profile of v4, /device:TPU:1, one launch (start us, length us, event | category | flops | bytes accessed | tf_op | source)
XLA Modules:
  0.0 94.7 jit_solution(5894468960209770254)
XLA Ops:
  0.6 4.5 %pack.1 = bf16[64,136,128]{2,1,0:T(8,128)(2,1)} custom-call(bf16[3,128,2048]{2,1,0:T(8,128)(2,1)} %feat_ref.3, bf16[128,2048]{1,0:T(8,128)(2,1)} %cot_ref.3, f32[128,256]{1,0:T(8,128)} %filt_ref.1), custom_call_target="tpu_custom_call" | custom-call | tf_op jit(solution)/shard_map/pack/pallas_call | solution.py:544
  5.1 0.0 copy-start.4
  5.1 11.0 %all-to-all-start = ((bf16[64,136,128]{2,1,0:T(8,128)(2,1)}), bf16[64,136,128]{2,1,0:T(8,128)(2,1)S(1)}, u32[]{:S(2)}, u32[]{:S(2)}) async-start(bf16[64,136,128]{2,1,0:T(8,128)(2,1)} %pack.1), calls=%async_computation | async-start | bytes 4456448 | tf_op jit(solution)/shard_map/all_to_all | solution.py:539
  16.1 0.0 copy-done.4
  16.1 0.1 concatenate.8
  16.2 0.0 copy-start.2
  16.2 1.4 %copy-done.2 = bf16[3,128,2048]{2,1,0:T(8,128)(2,1)S(1)} copy-done((bf16[3,128,2048]{2,1,0:T(8,128)(2,1)S(1)}, bf16[3,128,2048]{2,1,0:T(8,128)(2,1)}, u32[]{:S(2)}) %copy-start.2) | copy-done | bytes 1572888
  17.6 0.0 copy-start.10
  17.6 0.0 copy-start.5
  17.6 0.0 copy-start.9
  17.6 1.4 %prepare.1.shaped_ref = f32[3,128,2048]{2,1,0:T(8,128)S(1)} custom-call(bf16[3,128,2048]{2,1,0:T(8,128)(2,1)S(1)} %copy-done.2, f32[3,3,2048]{2,1,0:T(4,128)S(1)} %copy-done.4), custom_call_target="tpu_custom_call" | custom-call | tf_op jit(solution)/shard_map/prepare/pallas_call | solution.py:639
  19.1 0.0 copy-start
  19.1 1.7 %copy-done = f32[3,128,2048]{2,1,0:T(8,128)} copy-done((f32[3,128,2048]{2,1,0:T(8,128)}, f32[3,128,2048]{2,1,0:T(8,128)S(1)}, u32[]{:S(2)}) %copy-start) | copy-done | bytes 3145752
  20.7 0.0 copy-done.10
  20.7 24.9 %all-to-all-done.in_ref.taps_ref = bf16[64,136,128]{2,1,0:T(8,128)(2,1)S(1)} async-done(((bf16[64,136,128]{2,1,0:T(8,128)(2,1)}), bf16[64,136,128]{2,1,0:T(8,128)(2,1)S(1)}, u32[]{:S(2)}, u32[]{:S(2)}) %all-to-all-start) | async-done | bytes 2228256 | tf_op jit(solution)/shard_map/all_to_all | solution.py:539
  45.7 0.0 copy-done.5
  45.7 0.0 copy-done.7
  45.7 0.0 copy-done.8
  45.7 0.0 copy-done.9
  45.7 0.0 copy-start.6
  45.7 13.6 %conv.1 = bf16[64,80,128]{2,1,0:T(8,128)(2,1)S(1)} custom-call(bf16[64,136,128]{2,1,0:T(8,128)(2,1)S(1)} %all-to-all-done.in_ref.taps_ref, bf16[64,136,128]{2,1,0:T(8,128)(2,1)S(1)} %all-to-all-done.in_ref.taps_ref, f32[10,8,256]{2,1,0:T(8,128)S(1)} %pad_maximum_fusion.weight_ref, bf16[144,192]{1,0:T(8,128)(2,1)S(1)} %copy-done.8, ...), custom_call_target="tpu_custom_call" | custom-call | tf_op jit(solution)/shard_map/conv/pallas_call | solution.py:570
  59.3 0.0 copy-start.1
  59.3 0.0 copy-start.3
  59.3 26.0 %all_to_all.10.in_ref = bf16[64,80,128]{2,1,0:T(8,128)(2,1)S(1)} all-to-all(bf16[64,80,128]{2,1,0:T(8,128)(2,1)S(1)} %conv.1), channel_id=1, replica_groups=mesh['ctx'=64,'ch'=2] {'ctx'}, dimensions={0} | all-to-all | bytes 2621440 | tf_op jit(solution)/shard_map/all_to_all | solution.py:539
  85.3 0.0 copy-done.6
  85.3 0.6 extras.1
  85.9 2.7 %collective-permute-start = (f32[128,128]{1,0:T(8,128)S(1)}, f32[128,128]{1,0:T(8,128)S(1)}, u32[]{:S(2)}, u32[]{:S(2)}) collective-permute-start(f32[128,128]{1,0:T(8,128)S(1)} %get-tuple-element.24), channel_id=1, source_target_pairs={{0,1},{1,0},{2,3},{3,2},{4,5},{5,4},{6,7},{7,6},{8,9},{9,8},{10,11... | collective-permute-start | bytes 196616 | tf_op jit(solution)/shard_map/ppermute | solution.py:695
  88.6 0.0 copy-done.1
  88.6 0.0 copy-done.3
  88.6 5.4 %finish.1 = (bf16[128,2048]{1,0:T(8,128)(2,1)}, f32[3,128,2048]{2,1,0:T(8,128)}, f32[3,3,2048]{2,1,0:T(4,128)}, f32[1,2048]{1,0:T(1,128)}) custom-call(bf16[64,80,128]{2,1,0:T(8,128)(2,1)S(1)} %all_to_all.10.in_ref, f32[3,128,2048]{2,1,0:T(8,128)S(1)} %copy-done.1, bf16[128,2048]{1,0:T(8,128)(2,1)S(1)} %copy-done.3, f32[3,3,2048]{2,1,0:T(4,128)S(1)} %copy-done.4, ...), custom_call_target="tpu_custom_call" | custom-call | tf_op jit(solution)/shard_map/finish/pallas_call | solution.py:654
  94.0 0.0 collective-permute-done
  94.0 0.6 add.3
  (4 shorter events, 0.0 us)
Async XLA Ops:
  5.1 11.0 %copy-start.4 = (f32[3,3,2048]{2,1,0:T(4,128)S(1)}, f32[3,3,2048]{2,1,0:T(4,128)}, u32[]{:S(2)}) copy-start(f32[3,3,2048]{2,1,0:T(4,128)} %weight_ref.3) | copy-start | bytes 221188
  5.1 40.5 %all-to-all-start = ((bf16[64,136,128]{2,1,0:T(8,128)(2,1)}), bf16[64,136,128]{2,1,0:T(8,128)(2,1)S(1)}, u32[]{:S(2)}, u32[]{:S(2)}) async-start(bf16[64,136,128]{2,1,0:T(8,128)(2,1)} %pack.1), calls=%async_computation | async-start | bytes 4456448 | tf_op jit(solution)/shard_map/all_to_all | solution.py:539
  16.2 1.4 %copy-start.2 = (bf16[3,128,2048]{2,1,0:T(8,128)(2,1)S(1)}, bf16[3,128,2048]{2,1,0:T(8,128)(2,1)}, u32[]{:S(2)}) copy-start(bf16[3,128,2048]{2,1,0:T(8,128)(2,1)} %feat_ref.3) | copy-start | bytes 4718596
  17.6 3.1 %copy-start.10 = (f32[2048]{0:T(1024)S(1)}, f32[2048]{0:T(1024)}, u32[]{:S(2)}) copy-start(f32[2048]{0:T(1024)} %param.12) | copy-start | bytes 24580
  17.6 28.1 %copy-start.5 = (bf16[768,256]{1,0:T(8,128)(2,1)S(1)}, bf16[768,256]{1,0:T(8,128)(2,1)}, u32[]{:S(2)}) copy-start(bf16[768,256]{1,0:T(8,128)(2,1)} %constant.13.clone.forward_ref) | copy-start | bytes 1179652
  17.6 28.1 %copy-start.7 = (f32[2,72,128]{2,1,0:T(8,128)S(1)}, f32[2,72,128]{2,1,0:T(8,128)}, u32[]{:S(2)}) copy-start(f32[2,72,128]{2,1,0:T(8,128)} %constant.12.clone.twiddle_ref) | copy-start | bytes 221188
  17.6 28.1 %copy-start.8 = (bf16[144,192]{1,0:T(8,128)(2,1)S(1)}, bf16[144,192]{1,0:T(8,128)(2,1)}, u32[]{:S(2)}) copy-start(bf16[144,192]{1,0:T(8,128)(2,1)} %constant.10.clone.first_ref) | copy-start | bytes 165892
  17.6 28.1 %copy-start.9 = (bf16[64,432]{1,0:T(8,128)(2,1)S(1)}, bf16[64,432]{1,0:T(8,128)(2,1)}, u32[]{:S(2)}) copy-start(bf16[64,432]{1,0:T(8,128)(2,1)} %constant.11.clone.last_ref) | copy-start | bytes 165892
  19.1 1.7 %copy-start = (f32[3,128,2048]{2,1,0:T(8,128)}, f32[3,128,2048]{2,1,0:T(8,128)S(1)}, u32[]{:S(2)}) copy-start(f32[3,128,2048]{2,1,0:T(8,128)S(1)} %prepare.1.shaped_ref) | copy-start | bytes 9437188
  45.7 39.7 %copy-start.6 = (bf16[4,64,256]{2,1,0:T(8,128)(2,1)S(1)}, bf16[4,64,256]{2,1,0:T(8,128)(2,1)}, u32[]{:S(2)}) copy-start(bf16[4,64,256]{2,1,0:T(8,128)(2,1)} %constant.14.clone.spread_ref) | copy-start | bytes 393220
  59.3 29.4 %copy-start.1 = (f32[3,128,2048]{2,1,0:T(8,128)S(1)}, f32[3,128,2048]{2,1,0:T(8,128)}, u32[]{:S(2)}) copy-start(f32[3,128,2048]{2,1,0:T(8,128)} %copy-done) | copy-start | bytes 9437188
  59.3 29.3 %copy-start.3 = (bf16[128,2048]{1,0:T(8,128)(2,1)S(1)}, bf16[128,2048]{1,0:T(8,128)(2,1)}, u32[]{:S(2)}) copy-start(bf16[128,2048]{1,0:T(8,128)(2,1)} %cot_ref.3) | copy-start | bytes 1572868
  85.9 8.1 %collective-permute-start = (f32[128,128]{1,0:T(8,128)S(1)}, f32[128,128]{1,0:T(8,128)S(1)}, u32[]{:S(2)}, u32[]{:S(2)}) collective-permute-start(f32[128,128]{1,0:T(8,128)S(1)} %get-tuple-element.24), channel_id=1, source_target_pairs={{0,1},{1,0},{2,3},{3,2},{4,5},{5,4},{6,7},{7,6},{8,9},{9,8},{10,11... | collective-permute-start | bytes 196616 | tf_op jit(solution)/shard_map/ppermute | solution.py:695

commit v5 on v4

--- a/solution.py
+++ b/solution.py
@@ -450,51 +450,41 @@
 
 def finish_kernel(
     in_ref, shaped_ref, cot_ref, weight_ref, ext_ref, mixed_ref, grad_ref, short_ref, skip_ref,
-    codes, shaped, cot, mixed, grad, wide, turned, code_sem, shaped_sem, cot_sem, mixed_sem, grad_sem,
+    mixed, grad, wide, turned, mixed_sem, grad_sem,
 ):
-    share = BLOCKS // 4
-
-    def code_copy(j):
-        place = pl.ds(share * j, share)
-        return pltpu.make_async_copy(in_ref.at[place, pl.ds(0, RESULT_ROWS), :], codes.at[place], code_sem.at[j])
-
     def lanes_of(k):
         return pl.ds(pl.multiple_of(GROUPS * k, GROUPS), GROUPS)
 
-    def inputs(k):
-        return (
-            pltpu.make_async_copy(shaped_ref.at[:, :, lanes_of(k)], shaped.at[k], shaped_sem.at[k]),
-            pltpu.make_async_copy(cot_ref.at[:, lanes_of(k)], cot.at[k], cot_sem.at[k]),
-        )
+    def wide_lanes(k):
+        return pl.ds(pl.multiple_of(2 * GROUPS * k, 2 * GROUPS), 2 * GROUPS)
 
     def results(k):
         return (
-            pltpu.make_async_copy(mixed.at[k], mixed_ref.at[:, lanes_of(k)], mixed_sem.at[k]),
-            pltpu.make_async_copy(grad.at[k], grad_ref.at[:, :, lanes_of(k)], grad_sem.at[k]),
+            pltpu.make_async_copy(mixed.at[k], mixed_ref.at[:, wide_lanes(k)], mixed_sem.at[k]),
+            pltpu.make_async_copy(grad.at[k], grad_ref.at[:, :, wide_lanes(k)], grad_sem.at[k]),
         )
 
-    for j in range(4):
-        code_copy(j).start()
-    for k in range(COPIES):
-        for copy in inputs(k):
-            copy.start()
-    for j in range(4):
-        code_copy(j).wait()
-
-        def widen(d, _):
-            place = pl.ds(pl.multiple_of(RESULT_ROWS * d, RESULT_ROWS), RESULT_ROWS)
-            wide[place, :] = codes[d].astype(f32)
-            return 0
-
-        lax.fori_loop(share * j, share * (j + 1), widen, 0, unroll=8)
+    def widen(d, _):
+        place = pl.ds(pl.multiple_of(RESULT_ROWS * d, RESULT_ROWS), RESULT_ROWS)
+        wide[place, :] = in_ref[d, :RESULT_ROWS, :].astype(f32)
+        return 0
+
+    lax.fori_loop(0, BLOCKS, widen, 0, unroll=8)
 
     size = 16
     row = lax.broadcasted_iota(jnp.int32, (size, 1), 0)
 
-    def one(k, _):
+    def one(k0, _):
+        for part in range(2):
+            half(k0, part)
+        for copy in results(k0):
+            copy.start()
+        return 0
+
+    def half(k0, part):
+        k = 2 * k0 + part
         lanes = lanes_of(k)
-        for copy in inputs(k):
-            copy.wait()
+        spot = slice(GROUPS * part, GROUPS * (part + 1))
         for i in range(3):
             short_ref[i, :, lanes] = ext_ref[k, TOTAL + 3 * i : TOTAL + 3 * i + 3, :]
         skip_ref[:, lanes] = ext_ref[k, TOTAL + 9 : TOTAL + 10, :]
@@ -511,26 +501,23 @@
         for begin in reversed(range(0, ROWS, size)):
             rows = slice(begin, begin + size)
             conv, grad_mixer = (decode(turned[slot, rows, :], scales[slot]) for slot in range(2))
-            forms = [shaped[k, i, rows, :] for i in range(3)]
+            forms = [shaped_ref[i, rows, lanes] for i in range(3)]
             if begin == 0:
                 for i in range(3):
                     forms[i] = forms[i] + jnp.where(row == 0, lead[i][0], jnp.where(row == 1, lead[i][1], 0.0))
             query, key, value = forms
-            mixed[k, rows, :] = (query * conv).astype(bf16)
-            slopes = (cot[k, rows, :].astype(f32) * conv, grad_mixer * value, grad_mixer * key)
+            mixed[k0, rows, spot] = (query * conv).astype(bf16)
+            slopes = (cot_ref[rows, lanes].astype(f32) * conv, grad_mixer * value, grad_mixer * key)
             for i in range(3):
                 slope, after = slopes[i], following[i]
                 one = jnp.where(row == size - 1, after[0:1], pltpu.roll(slope, size - 1, 0))
                 two = jnp.where(row >= size - 2, pltpu.roll(one, size - 1, 0), pltpu.roll(slope, size - 2, 0))
                 two = jnp.where(row == size - 1, after[1:2], two)
-                grad[k, i, rows, :] = taps[i][0] * slope + taps[i][1] * one + taps[i][2] * two
+                grad[k0, i, rows, spot] = taps[i][0] * slope + taps[i][1] * one + taps[i][2] * two
             following = [slope[:2] for slope in slopes]
-        for copy in results(k):
-            copy.start()
-        return 0
-
-    lax.fori_loop(0, COPIES, one, 0)
-    for k in range(COPIES):
+
+    lax.fori_loop(0, COPIES // 2, one, 0)
+    for k in range(COPIES // 2):
         for copy in results(k):
             copy.wait()
 
@@ -551,7 +538,7 @@
             pltpu.VMEM((COPIES, ROWS, GROUPS), bf16),
             pltpu.VMEM((ROWS, GROUPS), f32),
             pltpu.VMEM((BLOCKS, SEND_ROWS, ROWS), bf16),
-            pltpu.VMEM((4, COPIES * SPACING, ROWS), f32),
+            pltpu.VMEM((4, (COPIES + 1) * SPACING, ROWS), f32),
             pltpu.VMEM((2, GROUPS, ROWS), f32),
             pltpu.SemaphoreType.DMA((COPIES,)),
             pltpu.SemaphoreType.DMA((COPIES,)),
@@ -583,8 +570,8 @@
             pltpu.VMEM((OWN + 1, BLOCKS, 2 * COPIES, ROWS), bf16),
             pltpu.SemaphoreType.DMA((OWN,)),
             pltpu.SemaphoreType.DMA((OWN + 1,)),
-            pltpu.VMEM((2, COPIES * BLOCKS, ROWS), f32),
-            pltpu.VMEM((2, COPIES * BLOCKS, ROWS), f32),
+            pltpu.VMEM((2, COPIES * (BLOCKS + 1), ROWS), f32),
+            pltpu.VMEM((2, COPIES * (BLOCKS + 1), ROWS), f32),
             pltpu.VMEM((2, BLOCKS, 24, ROWS), f32),
             pltpu.VMEM((2, BLOCKS, 24, ROWS), f32),
             pltpu.VMEM((2, BLOCKS, 24, ROWS), f32),
@@ -595,10 +582,10 @@
             pltpu.VMEM((OWN, LINES, 2 * ROWS), f32),
             pltpu.VMEM((BLOCKS + 1, COPIES, ROWS), f32),
             pltpu.VMEM((BLOCKS, COPIES, ROWS), f32),
-            pltpu.VMEM((2 * OWN * BLOCKS, ROWS), f32),
+            pltpu.VMEM((2 * OWN * (BLOCKS + 1), ROWS), f32),
             pltpu.VMEM((OWN, COPIES, ROWS), f32),
-            pltpu.VMEM((COPIES * BLOCKS, ROWS), f32),
-            pltpu.VMEM((COPIES * BLOCKS, ROWS), f32),
+            pltpu.VMEM((COPIES * (BLOCKS + 1), ROWS), f32),
+            pltpu.VMEM((COPIES * (BLOCKS + 1), ROWS), f32),
         ],
         compiler_params=LIMIT,
         name="conv",
@@ -626,7 +613,7 @@
             jax.ShapeDtypeStruct((ROWS, GROUPS // 2), f32),
             jax.ShapeDtypeStruct((COPIES, 32, GROUPS), f32),
         ],
-        scratch_shapes=[pltpu.VMEM((16 * BLOCKS, ROWS), f32)],
+        scratch_shapes=[pltpu.VMEM((16 * (BLOCKS + 1), ROWS), f32)],
         compiler_params=LIMIT,
         name="extras",
     )(home, spread)
@@ -650,12 +637,11 @@
 def finish(home, shaped, cotangent, short_weight, ext):
     breadth = shaped.shape[2]
     anywhere = pl.BlockSpec(memory_space=pl.ANY)
-    whole = lambda *shape: pl.BlockSpec(shape, lambda i: (0,) * len(shape))
+    vmem = pl.BlockSpec(memory_space=pltpu.VMEM)
     return pl.pallas_call(
         finish_kernel,
-        grid=(1,),
-        in_specs=[anywhere] * 3 + [whole(*array.shape) for array in (short_weight, ext)],
-        out_specs=[anywhere, anywhere, whole(3, 3, breadth), whole(1, breadth)],
+        in_specs=[vmem] * 5,
+        out_specs=[anywhere, anywhere, vmem, vmem],
         out_shape=[
             jax.ShapeDtypeStruct((ROWS, breadth), bf16),
             jax.ShapeDtypeStruct((3, ROWS, breadth), f32),
@@ -663,16 +649,13 @@
             jax.ShapeDtypeStruct((1, breadth), f32),
         ],
         scratch_shapes=[
-            pltpu.VMEM((BLOCKS, RESULT_ROWS, ROWS), bf16),
-            pltpu.VMEM((COPIES, 3, ROWS, GROUPS), f32),
-            pltpu.VMEM((COPIES, ROWS, GROUPS), bf16),
-            pltpu.VMEM((COPIES, ROWS, GROUPS), bf16),
-            pltpu.VMEM((COPIES, 3, ROWS, GROUPS), f32),
-            pltpu.VMEM((RESULT_ROWS * BLOCKS, ROWS), f32),
+            pltpu.VMEM((COPIES // 2, ROWS, 2 * GROUPS), bf16),
+            pltpu.VMEM((COPIES // 2, 3, ROWS, 2 * GROUPS), f32),
+            pltpu.VMEM((RESULT_ROWS * BLOCKS + 16, ROWS), f32),
             pltpu.VMEM((2, ROWS, GROUPS), f32),
-            pltpu.SemaphoreType.DMA((4,)),
-        ]
-        + [pltpu.SemaphoreType.DMA((COPIES,))] * 4,
+            pltpu.SemaphoreType.DMA((COPIES,)),
+            pltpu.SemaphoreType.DMA((COPIES,)),
+        ],
         compiler_params=LIMIT,
         name="finish",
     )(home, shaped, cotangent, short_weight, ext)

time: 95 us -> 94.2 us (level)
  transfers between devices with their start and end apart: 2 -> 2, of which waited for: 1 -> 1; matrix products, arithmetic and copies ran while one was open for 0% -> 0% of each run, Pallas kernels for 7% -> 6%
where the time goes in v5:
time: 94.2 us; the launch traced here: 93.9 us
  blocking collectives  26 us (28%)
  waiting for transfers between devices  24.9 us (26%)
  Pallas kernels  24.7 us (26%)
  starting transfers between devices  13.7 us (15%)
  local copies, waits for them, and re-layouts  3.16 us (3%)
    all_to_all x1, blocking collectives, exchange(): lax.all_to_all(values, 'ctx', split_axis=0, concat_axis=0, tiled=True)  26 us
    all_to_all x1, waiting for transfers between devices, exchange(): lax.all_to_all(values, 'ctx', split_axis=0, concat_axis=0, tiled=True)  24.9 us
    pallas_call x1, Pallas kernels, convolve(): pl.pallas_call(conv_kernel, grid=(1,), in_specs=[anywhere, pl.BlockSpec((...  13.6 us
    all_to_all x1, starting transfers between devices, exchange(): lax.all_to_all(values, 'ctx', split_axis=0, concat_axis=0, tiled=True)  11 us
    pallas_call x1, Pallas kernels, finish(): pl.pallas_call(finish_kernel, in_specs=[vmem] * 5, out_specs=[anywhere, a...  4.58 us
    pallas_call x1, Pallas kernels, pack(): pl.pallas_call(pack_kernel, in_specs=[anywhere] * 3, out_specs=anywhere,...  4.46 us
    unnamed x22, local copies, waits for them, and re-layouts  3.11 us
    ppermute x1, starting transfers between devices, shards(): arrived = lax.ppermute(other, 'ch', [(0, 1), (1, 0)])  2.7 us
  transfers between devices with their start and end apart: 2, of which 1 were waited for; matrix products, arithmetic and copies ran while one was open for 0% of the time, Pallas kernels for 6%

profile of v5, /device:TPU:1, one launch (start us, length us, event | category | flops | bytes accessed | tf_op | source)
XLA Modules:
  0.0 93.9 jit_solution(14397379104471663052)
XLA Ops:
  0.6 4.5 %pack.1 = bf16[64,136,128]{2,1,0:T(8,128)(2,1)} custom-call(bf16[3,128,2048]{2,1,0:T(8,128)(2,1)} %feat_ref.3, bf16[128,2048]{1,0:T(8,128)(2,1)} %cot_ref.3, f32[128,256]{1,0:T(8,128)} %filt_ref.1), custom_call_target="tpu_custom_call" | custom-call | tf_op jit(solution)/shard_map/pack/pallas_call | solution.py:531
  5.1 0.0 copy-start.4
  5.1 11.0 %all-to-all-start = ((bf16[64,136,128]{2,1,0:T(8,128)(2,1)}), bf16[64,136,128]{2,1,0:T(8,128)(2,1)S(1)}, u32[]{:S(2)}, u32[]{:S(2)}) async-start(bf16[64,136,128]{2,1,0:T(8,128)(2,1)} %pack.1), calls=%async_computation | async-start | bytes 4456448 | tf_op jit(solution)/shard_map/all_to_all | solution.py:526
  16.1 0.0 copy-done.4
  16.1 0.1 concatenate.8
  16.2 0.0 copy-start.2
  16.2 1.4 %copy-done.2 = bf16[3,128,2048]{2,1,0:T(8,128)(2,1)S(1)} copy-done((bf16[3,128,2048]{2,1,0:T(8,128)(2,1)S(1)}, bf16[3,128,2048]{2,1,0:T(8,128)(2,1)}, u32[]{:S(2)}) %copy-start.2) | copy-done | bytes 1572888
  17.6 0.0 copy-start.10
  17.6 0.0 copy-start.5
  17.6 0.0 copy-start.9
  17.6 1.4 %prepare.1.shaped_ref = f32[3,128,2048]{2,1,0:T(8,128)S(1)} custom-call(bf16[3,128,2048]{2,1,0:T(8,128)(2,1)S(1)} %copy-done.2, f32[3,3,2048]{2,1,0:T(4,128)S(1)} %copy-done.4), custom_call_target="tpu_custom_call" | custom-call | tf_op jit(solution)/shard_map/prepare/pallas_call | solution.py:626
  19.1 0.0 copy-start
  19.1 1.7 %copy-done = f32[3,128,2048]{2,1,0:T(8,128)} copy-done((f32[3,128,2048]{2,1,0:T(8,128)}, f32[3,128,2048]{2,1,0:T(8,128)S(1)}, u32[]{:S(2)}) %copy-start) | copy-done | bytes 3145752
  20.7 0.0 copy-done.10
  20.8 24.9 %all-to-all-done.in_ref.taps_ref = bf16[64,136,128]{2,1,0:T(8,128)(2,1)S(1)} async-done(((bf16[64,136,128]{2,1,0:T(8,128)(2,1)}), bf16[64,136,128]{2,1,0:T(8,128)(2,1)S(1)}, u32[]{:S(2)}, u32[]{:S(2)}) %all-to-all-start) | async-done | bytes 2228256 | tf_op jit(solution)/shard_map/all_to_all | solution.py:526
  45.7 0.0 copy-done.5
  45.7 0.0 copy-done.7
  45.7 0.0 copy-done.8
  45.7 0.0 copy-done.9
  45.7 0.0 copy-start.6
  45.7 13.6 %conv.1 = bf16[64,80,128]{2,1,0:T(8,128)(2,1)S(1)} custom-call(bf16[64,136,128]{2,1,0:T(8,128)(2,1)S(1)} %all-to-all-done.in_ref.taps_ref, bf16[64,136,128]{2,1,0:T(8,128)(2,1)S(1)} %all-to-all-done.in_ref.taps_ref, f32[10,8,256]{2,1,0:T(8,128)S(1)} %pad_maximum_fusion.weight_ref, bf16[144,192]{1,0:T(8,128)(2,1)S(1)} %copy-done.8, ...), custom_call_target="tpu_custom_call" | custom-call | tf_op jit(solution)/shard_map/conv/pallas_call | solution.py:557
  59.3 0.0 copy-start.1
  59.3 0.0 copy-start.3
  59.3 26.0 %all_to_all.10.in_ref = bf16[64,80,128]{2,1,0:T(8,128)(2,1)S(1)} all-to-all(bf16[64,80,128]{2,1,0:T(8,128)(2,1)S(1)} %conv.1), channel_id=1, replica_groups=mesh['ctx'=64,'ch'=2] {'ctx'}, dimensions={0} | all-to-all | bytes 2621440 | tf_op jit(solution)/shard_map/all_to_all | solution.py:526
  85.3 0.0 copy-done.6
  85.3 0.6 extras.1
  85.9 2.7 %collective-permute-start = (f32[128,128]{1,0:T(8,128)S(1)}, f32[128,128]{1,0:T(8,128)S(1)}, u32[]{:S(2)}, u32[]{:S(2)}) collective-permute-start(f32[128,128]{1,0:T(8,128)S(1)} %get-tuple-element.24), channel_id=1, source_target_pairs={{0,1},{1,0},{2,3},{3,2},{4,5},{5,4},{6,7},{7,6},{8,9},{9,8},{10,11... | collective-permute-start | bytes 196616 | tf_op jit(solution)/shard_map/ppermute | solution.py:678
  88.6 0.0 copy-done.1
  88.6 0.0 copy-done.3
  88.7 4.6 %finish.1 = (bf16[128,2048]{1,0:T(8,128)(2,1)}, f32[3,128,2048]{2,1,0:T(8,128)}, f32[3,3,2048]{2,1,0:T(4,128)}, f32[1,2048]{1,0:T(1,128)}) custom-call(bf16[64,80,128]{2,1,0:T(8,128)(2,1)S(1)} %all_to_all.10.in_ref, f32[3,128,2048]{2,1,0:T(8,128)S(1)} %copy-done.1, bf16[128,2048]{1,0:T(8,128)(2,1)S(1)} %copy-done.3, f32[3,3,2048]{2,1,0:T(4,128)S(1)} %copy-done.4, ...), custom_call_target="tpu_custom_call" | custom-call | tf_op jit(solution)/shard_map/finish/pallas_call | solution.py:641
  93.2 0.0 collective-permute-done
  93.2 0.6 add.3
  (4 shorter events, 0.0 us)
Async XLA Ops:
  5.1 11.0 %copy-start.4 = (f32[3,3,2048]{2,1,0:T(4,128)S(1)}, f32[3,3,2048]{2,1,0:T(4,128)}, u32[]{:S(2)}) copy-start(f32[3,3,2048]{2,1,0:T(4,128)} %weight_ref.3) | copy-start | bytes 221188
  5.1 40.5 %all-to-all-start = ((bf16[64,136,128]{2,1,0:T(8,128)(2,1)}), bf16[64,136,128]{2,1,0:T(8,128)(2,1)S(1)}, u32[]{:S(2)}, u32[]{:S(2)}) async-start(bf16[64,136,128]{2,1,0:T(8,128)(2,1)} %pack.1), calls=%async_computation | async-start | bytes 4456448 | tf_op jit(solution)/shard_map/all_to_all | solution.py:526
  16.2 1.4 %copy-start.2 = (bf16[3,128,2048]{2,1,0:T(8,128)(2,1)S(1)}, bf16[3,128,2048]{2,1,0:T(8,128)(2,1)}, u32[]{:S(2)}) copy-start(bf16[3,128,2048]{2,1,0:T(8,128)(2,1)} %feat_ref.3) | copy-start | bytes 4718596
  17.6 3.1 %copy-start.10 = (f32[2048]{0:T(1024)S(1)}, f32[2048]{0:T(1024)}, u32[]{:S(2)}) copy-start(f32[2048]{0:T(1024)} %param.12) | copy-start | bytes 24580
  17.6 28.1 %copy-start.5 = (bf16[768,256]{1,0:T(8,128)(2,1)S(1)}, bf16[768,256]{1,0:T(8,128)(2,1)}, u32[]{:S(2)}) copy-start(bf16[768,256]{1,0:T(8,128)(2,1)} %constant.13.clone.forward_ref) | copy-start | bytes 1179652
  17.6 28.1 %copy-start.7 = (f32[2,72,128]{2,1,0:T(8,128)S(1)}, f32[2,72,128]{2,1,0:T(8,128)}, u32[]{:S(2)}) copy-start(f32[2,72,128]{2,1,0:T(8,128)} %constant.12.clone.twiddle_ref) | copy-start | bytes 221188
  17.6 28.1 %copy-start.8 = (bf16[144,192]{1,0:T(8,128)(2,1)S(1)}, bf16[144,192]{1,0:T(8,128)(2,1)}, u32[]{:S(2)}) copy-start(bf16[144,192]{1,0:T(8,128)(2,1)} %constant.10.clone.first_ref) | copy-start | bytes 165892
  17.6 28.1 %copy-start.9 = (bf16[64,432]{1,0:T(8,128)(2,1)S(1)}, bf16[64,432]{1,0:T(8,128)(2,1)}, u32[]{:S(2)}) copy-start(bf16[64,432]{1,0:T(8,128)(2,1)} %constant.11.clone.last_ref) | copy-start | bytes 165892
  19.1 1.7 %copy-start = (f32[3,128,2048]{2,1,0:T(8,128)}, f32[3,128,2048]{2,1,0:T(8,128)S(1)}, u32[]{:S(2)}) copy-start(f32[3,128,2048]{2,1,0:T(8,128)S(1)} %prepare.1.shaped_ref) | copy-start | bytes 9437188
  45.7 39.6 %copy-start.6 = (bf16[4,64,256]{2,1,0:T(8,128)(2,1)S(1)}, bf16[4,64,256]{2,1,0:T(8,128)(2,1)}, u32[]{:S(2)}) copy-start(bf16[4,64,256]{2,1,0:T(8,128)(2,1)} %constant.14.clone.spread_ref) | copy-start | bytes 393220
  59.3 29.4 %copy-start.1 = (f32[3,128,2048]{2,1,0:T(8,128)S(1)}, f32[3,128,2048]{2,1,0:T(8,128)}, u32[]{:S(2)}) copy-start(f32[3,128,2048]{2,1,0:T(8,128)} %copy-done) | copy-start | bytes 9437188
  59.3 29.4 %copy-start.3 = (bf16[128,2048]{1,0:T(8,128)(2,1)S(1)}, bf16[128,2048]{1,0:T(8,128)(2,1)}, u32[]{:S(2)}) copy-start(bf16[128,2048]{1,0:T(8,128)(2,1)} %cot_ref.3) | copy-start | bytes 1572868
  85.9 7.3 %collective-permute-start = (f32[128,128]{1,0:T(8,128)S(1)}, f32[128,128]{1,0:T(8,128)S(1)}, u32[]{:S(2)}, u32[]{:S(2)}) collective-permute-start(f32[128,128]{1,0:T(8,128)S(1)} %get-tuple-element.24), channel_id=1, source_target_pairs={{0,1},{1,0},{2,3},{3,2},{4,5},{5,4},{6,7},{7,6},{8,9},{9,8},{10,11... | collective-permute-start | bytes 196616 | tf_op jit(solution)/shard_map/ppermute | solution.py:678

commit v6 on v5

--- a/solution.py
+++ b/solution.py
@@ -121,7 +121,7 @@
             copy.wait()
         for part in range(4):
             source = cot[k] if part == 3 else feat[k, part]
-            turned[part, SPACING * k : SPACING * k + GROUPS, :] = source.astype(f32).T
+            turned[part, SPACING * k : SPACING * k + GROUPS, :] = source.T.astype(f32)
 
     def one(d, _):
         for gi in range(OWN):

time: 94.2 us -> 94.1 us (level)
  no operation moved by 1% of the time
where the time goes in v6:
time: 94.1 us; the launch traced here: 93.8 us
  blocking collectives  26 us (28%)
  waiting for transfers between devices  24.9 us (26%)
  Pallas kernels  24.6 us (26%)
  starting transfers between devices  13.7 us (15%)
  local copies, waits for them, and re-layouts  3.16 us (3%)
    all_to_all x1, blocking collectives, exchange(): lax.all_to_all(values, 'ctx', split_axis=0, concat_axis=0, tiled=True)  26 us
    all_to_all x1, waiting for transfers between devices, exchange(): lax.all_to_all(values, 'ctx', split_axis=0, concat_axis=0, tiled=True)  24.9 us
    pallas_call x1, Pallas kernels, convolve(): pl.pallas_call(conv_kernel, grid=(1,), in_specs=[anywhere, pl.BlockSpec((...  13.6 us
    all_to_all x1, starting transfers between devices, exchange(): lax.all_to_all(values, 'ctx', split_axis=0, concat_axis=0, tiled=True)  11 us
    pallas_call x1, Pallas kernels, finish(): pl.pallas_call(finish_kernel, in_specs=[vmem] * 5, out_specs=[anywhere, a...  4.58 us
    pallas_call x1, Pallas kernels, pack(): pl.pallas_call(pack_kernel, in_specs=[anywhere] * 3, out_specs=anywhere,...  4.34 us
    unnamed x22, local copies, waits for them, and re-layouts  3.11 us
    ppermute x1, starting transfers between devices, shards(): arrived = lax.ppermute(other, 'ch', [(0, 1), (1, 0)])  2.7 us
  transfers between devices with their start and end apart: 2, of which 1 were waited for; matrix products, arithmetic and copies ran while one was open for 0% of the time, Pallas kernels for 6%

profile of v6, /device:TPU:1, one launch (start us, length us, event | category | flops | bytes accessed | tf_op | source)
XLA Modules:
  0.0 93.8 jit_solution(14812718191724931650)
XLA Ops:
  0.6 4.3 %pack.1 = bf16[64,136,128]{2,1,0:T(8,128)(2,1)} custom-call(bf16[3,128,2048]{2,1,0:T(8,128)(2,1)} %feat_ref.3, bf16[128,2048]{1,0:T(8,128)(2,1)} %cot_ref.3, f32[128,256]{1,0:T(8,128)} %filt_ref.1), custom_call_target="tpu_custom_call" | custom-call | tf_op jit(solution)/shard_map/pack/pallas_call | solution.py:531
  5.0 0.0 copy-start.4
  5.0 11.0 %all-to-all-start = ((bf16[64,136,128]{2,1,0:T(8,128)(2,1)}), bf16[64,136,128]{2,1,0:T(8,128)(2,1)S(1)}, u32[]{:S(2)}, u32[]{:S(2)}) async-start(bf16[64,136,128]{2,1,0:T(8,128)(2,1)} %pack.1), calls=%async_computation | async-start | bytes 4456448 | tf_op jit(solution)/shard_map/all_to_all | solution.py:526
  16.0 0.0 copy-done.4
  16.0 0.1 concatenate.8
  16.1 0.0 copy-start.2
  16.1 1.4 %copy-done.2 = bf16[3,128,2048]{2,1,0:T(8,128)(2,1)S(1)} copy-done((bf16[3,128,2048]{2,1,0:T(8,128)(2,1)S(1)}, bf16[3,128,2048]{2,1,0:T(8,128)(2,1)}, u32[]{:S(2)}) %copy-start.2) | copy-done | bytes 1572888
  17.5 0.0 copy-start.10
  17.5 0.0 copy-start.5
  17.5 0.0 copy-start.9
  17.5 1.4 %prepare.1.shaped_ref = f32[3,128,2048]{2,1,0:T(8,128)S(1)} custom-call(bf16[3,128,2048]{2,1,0:T(8,128)(2,1)S(1)} %copy-done.2, f32[3,3,2048]{2,1,0:T(4,128)S(1)} %copy-done.4), custom_call_target="tpu_custom_call" | custom-call | tf_op jit(solution)/shard_map/prepare/pallas_call | solution.py:626
  18.9 0.0 copy-start
  19.0 1.7 %copy-done = f32[3,128,2048]{2,1,0:T(8,128)} copy-done((f32[3,128,2048]{2,1,0:T(8,128)}, f32[3,128,2048]{2,1,0:T(8,128)S(1)}, u32[]{:S(2)}) %copy-start) | copy-done | bytes 3145752
  20.6 0.0 copy-done.10
  20.6 24.9 %all-to-all-done.in_ref.taps_ref = bf16[64,136,128]{2,1,0:T(8,128)(2,1)S(1)} async-done(((bf16[64,136,128]{2,1,0:T(8,128)(2,1)}), bf16[64,136,128]{2,1,0:T(8,128)(2,1)S(1)}, u32[]{:S(2)}, u32[]{:S(2)}) %all-to-all-start) | async-done | bytes 2228256 | tf_op jit(solution)/shard_map/all_to_all | solution.py:526
  45.5 0.0 copy-done.5
  45.5 0.0 copy-done.7
  45.5 0.0 copy-done.8
  45.6 0.0 copy-done.9
  45.6 0.0 copy-start.6
  45.6 13.6 %conv.1 = bf16[64,80,128]{2,1,0:T(8,128)(2,1)S(1)} custom-call(bf16[64,136,128]{2,1,0:T(8,128)(2,1)S(1)} %all-to-all-done.in_ref.taps_ref, bf16[64,136,128]{2,1,0:T(8,128)(2,1)S(1)} %all-to-all-done.in_ref.taps_ref, f32[10,8,256]{2,1,0:T(8,128)S(1)} %pad_maximum_fusion.weight_ref, bf16[144,192]{1,0:T(8,128)(2,1)S(1)} %copy-done.8, ...), custom_call_target="tpu_custom_call" | custom-call | tf_op jit(solution)/shard_map/conv/pallas_call | solution.py:557
  59.2 0.0 copy-start.1
  59.2 0.0 copy-start.3
  59.2 26.0 %all_to_all.10.in_ref = bf16[64,80,128]{2,1,0:T(8,128)(2,1)S(1)} all-to-all(bf16[64,80,128]{2,1,0:T(8,128)(2,1)S(1)} %conv.1), channel_id=1, replica_groups=mesh['ctx'=64,'ch'=2] {'ctx'}, dimensions={0} | all-to-all | bytes 2621440 | tf_op jit(solution)/shard_map/all_to_all | solution.py:526
  85.2 0.0 copy-done.6
  85.2 0.6 extras.1
  85.8 2.7 %collective-permute-start = (f32[128,128]{1,0:T(8,128)S(1)}, f32[128,128]{1,0:T(8,128)S(1)}, u32[]{:S(2)}, u32[]{:S(2)}) collective-permute-start(f32[128,128]{1,0:T(8,128)S(1)} %get-tuple-element.24), channel_id=1, source_target_pairs={{0,1},{1,0},{2,3},{3,2},{4,5},{5,4},{6,7},{7,6},{8,9},{9,8},{10,11... | collective-permute-start | bytes 196616 | tf_op jit(solution)/shard_map/ppermute | solution.py:678
  88.5 0.0 copy-done.1
  88.5 0.0 copy-done.3
  88.5 4.6 %finish.1 = (bf16[128,2048]{1,0:T(8,128)(2,1)}, f32[3,128,2048]{2,1,0:T(8,128)}, f32[3,3,2048]{2,1,0:T(4,128)}, f32[1,2048]{1,0:T(1,128)}) custom-call(bf16[64,80,128]{2,1,0:T(8,128)(2,1)S(1)} %all_to_all.10.in_ref, f32[3,128,2048]{2,1,0:T(8,128)S(1)} %copy-done.1, bf16[128,2048]{1,0:T(8,128)(2,1)S(1)} %copy-done.3, f32[3,3,2048]{2,1,0:T(4,128)S(1)} %copy-done.4, ...), custom_call_target="tpu_custom_call" | custom-call | tf_op jit(solution)/shard_map/finish/pallas_call | solution.py:641
  93.1 0.0 collective-permute-done
  93.1 0.6 add.3
  (4 shorter events, 0.0 us)
Async XLA Ops:
  5.0 11.0 %copy-start.4 = (f32[3,3,2048]{2,1,0:T(4,128)S(1)}, f32[3,3,2048]{2,1,0:T(4,128)}, u32[]{:S(2)}) copy-start(f32[3,3,2048]{2,1,0:T(4,128)} %weight_ref.3) | copy-start | bytes 221188
  5.0 40.5 %all-to-all-start = ((bf16[64,136,128]{2,1,0:T(8,128)(2,1)}), bf16[64,136,128]{2,1,0:T(8,128)(2,1)S(1)}, u32[]{:S(2)}, u32[]{:S(2)}) async-start(bf16[64,136,128]{2,1,0:T(8,128)(2,1)} %pack.1), calls=%async_computation | async-start | bytes 4456448 | tf_op jit(solution)/shard_map/all_to_all | solution.py:526
  16.1 1.4 %copy-start.2 = (bf16[3,128,2048]{2,1,0:T(8,128)(2,1)S(1)}, bf16[3,128,2048]{2,1,0:T(8,128)(2,1)}, u32[]{:S(2)}) copy-start(bf16[3,128,2048]{2,1,0:T(8,128)(2,1)} %feat_ref.3) | copy-start | bytes 4718596
  17.5 3.1 %copy-start.10 = (f32[2048]{0:T(1024)S(1)}, f32[2048]{0:T(1024)}, u32[]{:S(2)}) copy-start(f32[2048]{0:T(1024)} %param.12) | copy-start | bytes 24580
  17.5 28.1 %copy-start.5 = (bf16[768,256]{1,0:T(8,128)(2,1)S(1)}, bf16[768,256]{1,0:T(8,128)(2,1)}, u32[]{:S(2)}) copy-start(bf16[768,256]{1,0:T(8,128)(2,1)} %constant.13.clone.forward_ref) | copy-start | bytes 1179652
  17.5 28.1 %copy-start.7 = (f32[2,72,128]{2,1,0:T(8,128)S(1)}, f32[2,72,128]{2,1,0:T(8,128)}, u32[]{:S(2)}) copy-start(f32[2,72,128]{2,1,0:T(8,128)} %constant.12.clone.twiddle_ref) | copy-start | bytes 221188
  17.5 28.1 %copy-start.8 = (bf16[144,192]{1,0:T(8,128)(2,1)S(1)}, bf16[144,192]{1,0:T(8,128)(2,1)}, u32[]{:S(2)}) copy-start(bf16[144,192]{1,0:T(8,128)(2,1)} %constant.10.clone.first_ref) | copy-start | bytes 165892
  17.5 28.1 %copy-start.9 = (bf16[64,432]{1,0:T(8,128)(2,1)S(1)}, bf16[64,432]{1,0:T(8,128)(2,1)}, u32[]{:S(2)}) copy-start(bf16[64,432]{1,0:T(8,128)(2,1)} %constant.11.clone.last_ref) | copy-start | bytes 165892
  18.9 1.7 %copy-start = (f32[3,128,2048]{2,1,0:T(8,128)}, f32[3,128,2048]{2,1,0:T(8,128)S(1)}, u32[]{:S(2)}) copy-start(f32[3,128,2048]{2,1,0:T(8,128)S(1)} %prepare.1.shaped_ref) | copy-start | bytes 9437188
  45.6 39.6 %copy-start.6 = (bf16[4,64,256]{2,1,0:T(8,128)(2,1)S(1)}, bf16[4,64,256]{2,1,0:T(8,128)(2,1)}, u32[]{:S(2)}) copy-start(bf16[4,64,256]{2,1,0:T(8,128)(2,1)} %constant.14.clone.spread_ref) | copy-start | bytes 393220
  59.2 29.4 %copy-start.1 = (f32[3,128,2048]{2,1,0:T(8,128)S(1)}, f32[3,128,2048]{2,1,0:T(8,128)}, u32[]{:S(2)}) copy-start(f32[3,128,2048]{2,1,0:T(8,128)} %copy-done) | copy-start | bytes 9437188
  59.2 29.4 %copy-start.3 = (bf16[128,2048]{1,0:T(8,128)(2,1)S(1)}, bf16[128,2048]{1,0:T(8,128)(2,1)}, u32[]{:S(2)}) copy-start(bf16[128,2048]{1,0:T(8,128)(2,1)} %cot_ref.3) | copy-start | bytes 1572868
  85.8 7.3 %collective-permute-start = (f32[128,128]{1,0:T(8,128)S(1)}, f32[128,128]{1,0:T(8,128)S(1)}, u32[]{:S(2)}, u32[]{:S(2)}) collective-permute-start(f32[128,128]{1,0:T(8,128)S(1)} %get-tuple-element.24), channel_id=1, source_target_pairs={{0,1},{1,0},{2,3},{3,2},{4,5},{5,4},{6,7},{7,6},{8,9},{9,8},{10,11... | collective-permute-start | bytes 196616 | tf_op jit(solution)/shard_map/ppermute | solution.py:678
